TPU v7x, 32 devices: a whole 2x2x4 slice. The times are simulated.
32 devices in a mesh: depth: 4 (over y, x), row: 2 (over core), col: 4 (over z).
Axes of the slice: x: 2, y: 2, z: 4, core: 2. Of those that a mesh axis runs over, the one named last changes fastest.
Arguments:
- density: float32 [64, 256, 512], P('depth', 'row', 'col'), may hold values from 0.002 to 0.05
- albedo: bfloat16 [3, 64, 256, 512], P(None, 'depth', 'row', 'col'), may hold values from 0.099609375 to 1
- targets: int32 [2, 4, 2, 4], P(None, None, 'row'), may hold values from -1 to 4, as said below
- offsets: int32 [2, 4, 2, 4], P(None, None, 'row', 'col'), may hold values from 0 to 127
- slab_order: int32 [2, 4], replicated, may hold values from 0 to 3, each once within a row
Outputs:
- frame: float32 [2, 4, 2, 128, 512], P(None, None, 'row', 'depth', 'col')
Inputs may be any that keep to these rules, and one draw needn't show every extreme that they name: `targets`: within one view and one row and column c of bricks, the 4 values are c + b, c + b, c + b + 1, c + b + 1, ... assigned to the slabs in some order (two bricks for each value, b is -1 or 0; b is -1 in column 0 and 0 in the last column), so one column of bricks sends at most 4 pieces to one screen tile, a number reached in every view, row and column, and only to tiles c - 1 .. c + 2.
All inputs are finite; a program needn't handle non-finite values.
Results may differ from a plain program's by a relative error of at most 0.0015.
Values may be sent and summed in bfloat16 or wider, within the bound.
No kernel may reach another device: no remote copies, remote signals or barrier semaphores. Data moves between devices by JAX's collectives and lax.ppermute only.
A program may use at most 64 MiB of HBM per device.

v0:
```python
import math

import jax
import jax.numpy as jnp
from jax import lax
from jax.sharding import PartitionSpec as P

SHEARS = (0.3125, -0.4375)
BRIGHTNESS = 4.0


def prefix_2(value, axis, join, neutral):
    count, mine = (lax.axis_size(axis), lax.axis_index(axis))
    pieces = lax.all_gather(value, axis)
    so_far = jnp.full_like(value, 0) + jnp.asarray(neutral, value.dtype)

    def step(position, so_far):
        longer = join(so_far, pieces[position])
        return jnp.where(position < mine, longer, so_far)

    return lax.fori_loop(0, count - 1, step, so_far)


def shifted(value, axis, steps):
    count = lax.axis_size(axis)
    first, last = (max(0, -steps), min(count, count - steps))
    return lax.ppermute(value, axis, [(source, source + steps) for source in range(first, last)])


def shear_columns(values, shear, plane_index, margin):
    integer_part = math.floor(shear * plane_index)
    fraction = shear * plane_index - integer_part
    col_count = values.shape[-1]
    padding = [(0, 0)] * (values.ndim - 1) + [(margin, margin)]
    padded = jnp.pad(values, padding)
    nearer = padded[..., margin - integer_part : margin - integer_part + col_count]
    farther = padded[..., margin - integer_part - 1 : margin - integer_part - 1 + col_count]
    return (1.0 - fraction) * nearer + fraction * farther


def composite_brick(colour, opacity, shear):
    depth_cells = opacity.shape[0]
    colour_sum = jnp.zeros((3,) + opacity.shape[1:], jnp.float32)
    transmit = jnp.ones(opacity.shape[1:], jnp.float32)
    for plane_index in range(depth_cells):
        moved_colour = shear_columns(colour[:, plane_index], shear, plane_index, depth_cells + 2)
        moved_opacity = shear_columns(opacity[plane_index], shear, plane_index, depth_cells + 2)
        colour_sum = colour_sum + transmit[None] * moved_colour
        transmit = transmit * (1.0 - moved_opacity)
    return jnp.concatenate(
        [colour_sum.astype(jnp.bfloat16), (1.0 - transmit).astype(jnp.bfloat16)[None]], axis=0
    )


def multiply_planes(earlier, later_plane):
    return earlier * later_plane


def route_tables(row_targets, slab_order, slot_count):
    view_count, slabs, columns = row_targets.shape
    window = slabs // 2 + 2
    column_ids = jnp.arange(columns, dtype=jnp.int32)
    relative = row_targets.transpose(0, 2, 1) - column_ids[None, :, None]
    step_ids = jnp.arange(window, dtype=jnp.int32) - 1
    halves = jnp.arange(2, dtype=jnp.int32)
    covers = (
        relative[:, :, None, :, None] + halves[None, None, None, None, :]
        == step_ids[None, None, :, None, None]
    ).astype(jnp.int32)
    covers = covers.reshape(view_count, columns, window, slabs * 2)
    slot_index = jnp.cumsum(covers, axis=-1) - covers
    slot_ids = jnp.arange(slot_count, dtype=jnp.int32)
    selection = covers[:, :, :, None, :] * (
        slot_index[:, :, :, None, :] == slot_ids[None, None, None, :, None]
    ).astype(jnp.int32)
    slab_ids = jnp.arange(slabs, dtype=jnp.int32)
    positions = jnp.sum(
        slab_ids[None, :, None]
        * (slab_order[:, :, None] == slab_ids[None, None, :]).astype(jnp.int32),
        axis=1,
    )
    brick_keys = positions[:, None, :] * columns + column_ids[None, :, None]
    half_keys = (brick_keys[..., None] * jnp.ones((2,), jnp.int32)).reshape(
        view_count, columns, slabs * 2
    )
    source_keys = jnp.sum(selection * half_keys[:, :, None, None, :], axis=-1)
    return (selection.reshape(view_count, columns, window, slot_count, slabs, 2), source_keys)


def placement_table(column_offsets, brick_cols):
    source_cols = jnp.arange(brick_cols, dtype=jnp.int32)
    target_cols = jnp.arange(2 * brick_cols, dtype=jnp.int32).reshape(2, brick_cols)
    landing = source_cols[None, None, :] + column_offsets[:, :, None]
    hits = landing[:, :, :, None, None] == target_cols[None, None, None, :, :]
    return hits.astype(jnp.bfloat16)


def on_device(density, albedo, targets, offsets, slab_order):
    depth_cells, brick_rows, brick_cols = density.shape
    view_count = slab_order.shape[0]
    slabs = lax.axis_size("depth")
    columns = lax.axis_size("col")
    slot_count = min(4, slabs)
    strip_rows = brick_rows // slabs
    window = slabs // 2 + 2
    slab_plane = jnp.exp(-jnp.sum(density, axis=0))
    incoming = prefix_2(slab_plane, "depth", multiply_planes, jnp.ones_like(slab_plane))
    in_front = jnp.cumsum(density, axis=0) - density
    lighting = incoming[None] * jnp.exp(-in_front)
    opacity = 1.0 - jnp.exp(-density)
    colour = BRIGHTNESS * albedo.astype(jnp.float32) * (lighting * opacity)[None]
    brick_images = jnp.stack(
        [composite_brick(colour, opacity, SHEARS[view_index]) for view_index in range(view_count)]
    )
    strips = lax.all_to_all(brick_images[:, None], "depth", split_axis=3, concat_axis=1, tiled=True)
    column_offsets = offsets[:, :, 0, 0]
    placement = placement_table(column_offsets, brick_cols)
    shaped = jnp.einsum(
        "vdkrx,vdxhy->vdkrhy", strips, placement, preferred_element_type=jnp.float32
    ).astype(jnp.bfloat16)
    selection, source_keys = route_tables(targets[:, :, 0, :], slab_order, slot_count)
    my_col = lax.axis_index("col")
    received = []
    key_list = []
    own_table = lax.dynamic_index_in_dim(selection, my_col, axis=1, keepdims=False)
    outgoing = jnp.einsum(
        "vwsdh,vdkrhx->wvskrx",
        own_table.astype(jnp.bfloat16),
        shaped,
        preferred_element_type=jnp.float32,
    ).astype(jnp.bfloat16)
    for step_index in range(window):
        step = step_index - 1
        if step == 0:
            arrived = outgoing[step_index]
        else:
            arrived = shifted(outgoing[step_index], "col", step)
        received.append(arrived)
    for step_index in range(window):
        step = step_index - 1
        source = jnp.clip(my_col - step, 0, columns - 1)
        key_list.append(
            lax.dynamic_index_in_dim(source_keys, source, axis=1, keepdims=False)[:, step_index]
        )
    flat = jnp.stack(received, axis=1).reshape(
        view_count, window * slot_count, 4, strip_rows * brick_cols
    )
    slot_keys = jnp.stack(key_list, axis=1).reshape(view_count, window * slot_count)
    log_transmit = jnp.log1p(-flat[:, :, 3].astype(jnp.float32))
    before = (slot_keys[:, None, :] < slot_keys[:, :, None]).astype(jnp.float32)
    prefix = jnp.einsum("vij,vjx->vix", before, log_transmit, precision=lax.Precision.HIGHEST)
    weight = jnp.exp(prefix)
    colour_sum = jnp.einsum(
        "vikx,vix->vkx", flat[:, :, :3].astype(jnp.float32), weight, precision=lax.Precision.HIGHEST
    )
    frame_opacity = 1.0 - jnp.exp(jnp.sum(log_transmit, axis=1))
    frame = jnp.concatenate([colour_sum, frame_opacity[:, None]], axis=1)
    return frame.reshape(view_count, 4, 1, strip_rows, brick_cols)


def solution(mesh):
    in_specs = (
        P("depth", "row", "col"),
        P(None, "depth", "row", "col"),
        P(None, None, "row", None),
        P(None, None, "row", "col"),
        P(),
    )
    out_specs = P(None, None, "row", "depth", "col")
    return jax.shard_map(
        on_device, mesh=mesh, in_specs=in_specs, out_specs=out_specs, check_vma=False
    )
```

profile of v0, /device:TPU:8, one launch (start us, length us, event | category | flops | bytes accessed | tf_op | source)
XLA Modules:
  0.0 61.5 jit_solution(5183235071577341786)
XLA Ops:
  0.0 1.4 %fusion.343 = (f32[128,128]{1,0:T(8,128)S(1)}, f32[16,128,128]{2,1,0:T(8,128)S(1)}) fusion(f32[16,128,128]{2,1,0:T(8,128)} %param.7), kind=kLoop, calls=%fused_computation.514 | loop fusion | flops 770048 | bytes 2162688 | tf_op jit(solution)/shard_map/reduce_sum | solution.py:106
  1.4 0.1 slice_bitcast_fusion.38
  1.5 0.0 copy-start
  1.5 1.1 %broadcast_multiply_fusion = (f32[128,128]{1,0:T(8,128)}, f32[128,128]{1,0:T(8,128)}, f32[128,128]{1,0:T(8,128)}, f32[128,128]{1,0:T(8,128)}, f32[128,128]{1,0:T...) fusion(f32[128,128]{1,0:T(8,128)S(1)} %get-tuple-element.170, ...), kind=kLoop, calls=%fused_computation.482 | loop fusion | flops 638976 | bytes 1048576 | tf_op jit(solution)/shard_map/mul | solution.py:48
  2.5 1.0 %broadcast_multiply_fusion.1 = (f32[128,128]{1,0:T(8,128)}, f32[128,128]{1,0:T(8,128)}, f32[128,128]{1,0:T(8,128)}, f32[128,128]{1,0:T(8,128)}, f32[128,128]{1,0...) fusion(f32[128,128]{1,0:T(8,128)S(1)} %get-tuple-element.170, ...), kind=kLoop, calls=%fused_computation.483 | loop fusion | flops 638976 | bytes 1048576 | tf_op jit(solution)/shard_map/mul | solution.py:48
  3.6 9.0 %all-gather = f32[512,128]{1,0:T(8,128)S(1)} all-gather(f32[128,128]{1,0:T(8,128)S(1)} %negate_exponential_fusion), channel_id=2, replica_groups=mesh['depth'=4,'row'=2,'col'=4] {'depth'}, dimensions={0}, use_global_device_ids=true | all-gather | bytes 327680 | tf_op jit(solution)/shard_map/all_gather | solution.py:14
  12.6 0.1 while.14
  12.7 0.3 multiply_multiply_fusion
  13.1 0.9 %copy-done.1 = bf16[3,16,128,128]{3,2,1,0:T(8,128)(2,1)S(1)} copy-done((bf16[3,16,128,128]{3,2,1,0:T(8,128)(2,1)S(1)}, bf16[3,16,128,128]{3,2,1,0:T(8,128)(2,1)}, u32[]{:S(2)}) %copy-start.1) | copy-done | bytes 1572888
  14.0 1.8 %convert_multiply_fusion = f32[3,16,128,128]{3,0,2,1:T(4,128)S(1)} fusion(bf16[3,16,128,128]{3,2,1,0:T(8,128)(2,1)S(1)} %copy-done.1, f32[16,128,128]{2,1,0:T(8,128)S(1)} %multiply_multiply_fusion), kind=kLoop, calls=%fused_computation.3 | loop fusion | flops 1572864 | bytes 5767168 | tf_op jit(solution)/shard_map/mul | solution.py:111
  15.8 1.2 %slice_bitcast_fusion.21 = (f32[3,128,128]{2,0,1:T(4,128)S(1)}, f32[3,128,128]{2,0,1:T(4,128)S(1)}, f32[3,128,128]{2,0,1:T(4,128)S(1)}, f32[3,128,128]{2,0,1:T(4...) fusion(f32[3,16,128,128]{3,0,2,1:T(4,128)S(1)} %convert_multipl, ...), kind=kLoop, calls=%fused_computation.242 | loop fusion | bytes 6291456 | tf_op jit(solution)/shard_map/squeeze | solution.py:46
  17.1 0.4 fusion.305
  17.5 0.1 copy.103
  17.5 0.0 copy-done.2
  17.5 0.4 fusion.306
  17.9 0.1 copy.102
  18.0 0.0 copy-done.17
  18.0 0.0 copy-start.4
  18.1 4.3 %fusion.156 = bf16[3,128,128]{2,0,1:T(4,128)(2,1)S(1)} fusion(f32[3,128,128]{2,0,1:T(4,128)S(1)} %get-tuple-element.141, f32[3,128,128]{2,0,1:T(4,128)S(1)} %get-tuple-element.142, f32[3,128,128]{2,0,1:T(4,128)S(1)} %get-tuple-element.143, f32[3,128,128]{2,0,1:T(4,128)S(1)} %get-tuple-element.144, f32[3,128,128]{2,0,1:T(4,128)S(1)} %get-tuple-element.145, ...), kind=kLoop, calls=%fused_computation.246 | loop fusion | flops 3735552 | bytes 4227072 | tf_op jit(solution)/shard_map/convert_element_type | solution.py:51
  22.5 0.0 copy-start.18
  22.5 4.2 %fusion.157 = bf16[3,128,128]{2,0,1:T(4,128)(2,1)S(1)} fusion(f32[3,128,128]{2,0,1:T(4,128)S(1)} %get-tuple-element.141, f32[3,128,128]{2,0,1:T(4,128)S(1)} %get-tuple-element.142, f32[3,128,128]{2,0,1:T(4,128)S(1)} %get-tuple-element.143, f32[3,128,128]{2,0,1:T(4,128)S(1)} %get-tuple-element.144, f32[3,128,128]{2,0,1:T(4,128)S(1)} %get-tuple-element.145, ...), kind=kLoop, calls=%fused_computation.247 | loop fusion | flops 3735552 | bytes 4227072 | tf_op jit(solution)/shard_map/convert_element_type | solution.py:51
  26.7 0.0 copy-start.20
  26.7 0.0 copy-start.19
  26.7 0.3 maximum_bitcast_fusion.1
  27.0 0.9 %maximum_bitcast_fusion = bf16[2,1,4,128,128]{4,2,0,1,3:T(4,128)(2,1)} fusion(bf16[1,4,128,128]{3,1,0,2:T(4,128)(2,1)S(1)} %get-tuple-element.183, bf16[1,4,128,128]{3,1,0,2:T(4,128)(2,1)S(1)} %get-tuple-element.182), kind=kLoop, calls=%fused_computation.243 | loop fusion | flops 131072 | bytes 524288 | tf_op jit(solution)/shard_map/broadcast_in_dim | solution.py:115
  27.9 3.4 %all-to-all-start = ((bf16[2,1,4,128,128]{4,2,0,1,3:T(4,128)(2,1)}), bf16[2,1,4,128,128]{4,2,0,1,3:T(4,128)(2,1)S(1)}, u32[]{:S(2)}, u32[]{:S(2)}) async-start(bf16[2,1,4,128,128]{4,2,0,1,3:T(4,128)(2,1)} %maximum_bitcast_fusion), calls=%async_computation | async-start | bytes 524288 | tf_op jit(solution)/shard_map/all_to_all | solution.py:115
  31.3 0.1 add.456
  31.4 0.1 broadcast_add_fusion
  31.5 0.1 copy.96
  31.6 0.1 compare_convert_fusion.2
  31.7 0.1 compare_convert_fusion.1
  31.8 0.1 copy.107
  31.9 0.1 compare_convert_fusion
  32.0 0.1 bitcast_subtract_fusion
  32.1 0.1 fusion.316
  32.2 0.2 copy.108
  32.4 0.2 copy.109
  32.6 0.1 copy.98
  32.8 0.1 copy.99
  32.9 0.1 select_reduce_fusion
  33.0 0.1 iota_add_fusion.2
  33.1 0.1 copy.100
  33.2 0.1 iota_add_fusion.1
  33.2 3.4 %all-to-all-done = bf16[2,1,4,128,128]{4,2,0,1,3:T(4,128)(2,1)S(1)} async-done(((bf16[2,1,4,128,128]{4,2,0,1,3:T(4,128)(2,1)}), bf16[2,1,4,128,128]{4,2,0,1,3:T(4,128)(2,1)S(1)}, u32[]{:S(2)}, u32[]{:S(2)}) %all-to-all-start) | async-done | bytes 262176 | tf_op jit(solution)/shard_map/all_to_all | solution.py:115
  36.6 0.4 fusion.2
  37.0 0.9 %fusion.1 = bf16[4,2,4,4,32,128]{5,2,0,4,3,1:T(4,128)(2,1)S(1)} fusion(bf16[2,4,4,32,2,128,1]{5,3,4,2,1,0,6:T(8,128)(2,1)S(1)} %fusion.2, s32[2,1,4,4,2]{3,4,2,0,1:T(2,128)S(1)} %get-tuple-element.184, s32[2,1,4,4,2]{3,4,2,0,1:T(2,128)S(1)} %get-tuple-element.185), kind=kOutput, calls=%fused_computation.6 | convolution fusion | flops 8913664 | bytes 1573376 | tf_op jit(solution)/shard_map/vwsdh,vdkrhx->wvskrx/dot_general | solution.py:126
  37.9 0.5 slice_bitcast_fusion.5
  38.5 2.4 %collective-permute-start = (bf16[2,4,4,32,128]{4,1,3,2,0:T(4,128)(2,1)S(1)}, bf16[2,4,4,32,128]{4,1,3,2,0:T(4,128)(2,1)S(1)}, u32[]{:S(2)}, u32[]{:S(2)}) collective-permute-start(bf16[2,4,4,32,128]{4,1,3,2,0:T(4,128)(2,1)S(1)} %get-tuple-element.156), channel_id=1, source_target_pairs={{1,0},{2,1},{3,2},{5,4},{6,5},{7,6},{9,8},{10,9},{11,10},{13,12},{... | collective-permute-start | bytes 786440 | tf_op jit(solution)/shard_map/ppermute | solution.py:27
  40.8 3.5 %collective-permute-start.1 = (bf16[2,4,4,32,128]{4,1,3,2,0:T(4,128)(2,1)S(1)}, bf16[2,4,4,32,128]{4,1,3,2,0:T(4,128)(2,1)S(1)}, u32[]{:S(2)}, u32[]{:S(2)}) collective-permute-start(bf16[2,4,4,32,128]{4,1,3,2,0:T(4,128)(2,1)S(1)} %get-tuple-element.159), channel_id=1, source_target_pairs={{0,1},{1,2},{2,3},{4,5},{5,6},{6,7},{8,9},{9,10},{10,11},{12,13},{... | collective-permute-start | bytes 786440 | tf_op jit(solution)/shard_map/ppermute | solution.py:27
  44.3 2.5 %collective-permute-start.2 = (bf16[2,4,4,32,128]{4,1,3,2,0:T(4,128)(2,1)S(1)}, bf16[2,4,4,32,128]{4,1,3,2,0:T(4,128)(2,1)S(1)}, u32[]{:S(2)}, u32[]{:S(2)}) collective-permute-start(bf16[2,4,4,32,128]{4,1,3,2,0:T(4,128)(2,1)S(1)} %get-tuple-element.158), channel_id=1, source_target_pairs={{0,2},{1,3},{4,6},{5,7},{8,10},{9,11},{12,14},{13,15},{16,18},{17,... | collective-permute-start | bytes 786440 | tf_op jit(solution)/shard_map/ppermute | solution.py:27
  46.9 0.6 %multiply_reduce_fusion.1 = s32[2,4,4,4]{3,2,1,0:T(4,128)S(1)} fusion(s32[2,4,8]{2,1,0:T(4,128)S(1)} %copy.100, s32[2,4,4,8]{3,2,1,0:T(4,128)S(1)} %copy.99, s32[2,4,4,8]{3,2,1,0:T(4,128)S(1)} %copy.98), kind=kLoop, calls=%fused_computation.474 | loop fusion | flops 3968 | bytes 2816 | tf_op jit(solution)/shard_map/reduce_sum | solution.py:86
  47.6 0.1 lt.41
  47.7 0.0 collective-permute-done
  47.7 7.2 %collective-permute-done.1 = bf16[2,4,4,32,128]{4,1,3,2,0:T(4,128)(2,1)S(1)} collective-permute-done((bf16[2,4,4,32,128]{4,1,3,2,0:T(4,128)(2,1)S(1)}, bf16[2,4,4,32,128]{4,1,3,2,0:T(4,128)(2,1)S(1)}, u32[]{:S(2)}, u32[]{:S(2)}) %collective-permute-start.1) | collective-permute-done | bytes 262176 | tf_op jit(solution)/shard_map/ppermute | solution.py:27
  54.9 2.8 %collective-permute-done.2 = bf16[2,4,4,32,128]{4,1,3,2,0:T(4,128)(2,1)S(1)} collective-permute-done((bf16[2,4,4,32,128]{4,1,3,2,0:T(4,128)(2,1)S(1)}, bf16[2,4,4,32,128]{4,1,3,2,0:T(4,128)(2,1)S(1)}, u32[]{:S(2)}, u32[]{:S(2)}) %collective-permute-start.2) | collective-permute-done | bytes 262176 | tf_op jit(solution)/shard_map/ppermute | solution.py:27
  57.7 1.0 %pad_maximum_fusion = bf16[2,4,4,4,32,128]{5,2,4,3,0,1:T(4,128)(2,1)S(1)} fusion(bf16[2,1,4,4,32,128]{5,2,4,3,0,1:T(4,128)(2,1)S(1)} %bitcast.185, bf16[2,1,4,4,32,128]{5,2,4,3,0,1:T(4,128)(2,1)S(1)} %bitcast.184, bf16[2,1,4,4,32,128]{5,2,4,3,0,1:T(4,128)(2,1)S(1)} %get-tuple-element.157, bf16[2,1,4,4,32,128]{5,2,4,3,0,1:T(4,128)(2,1)S(1)} %bitcast.183), kind=kLoop, calls=%fused_computation.13 | loop fusion | flops 1572864 | bytes 2097152 | tf_op jit(solution)/shard_map/stack | solution.py:145
  58.7 0.2 copy.114
  58.9 0.5 reshape.136
  59.4 0.3 fusion.10
  59.7 0.6 fusion
  60.2 0.3 multiply_reduce_fusion
  60.6 0.1 copy.149
  60.7 0.1 concatenate.14
  60.8 0.7 %copy.116 = f32[2,4,1,32,128]{4,3,2,1,0:T(8,128)} copy(f32[2,4,1,32,128]{4,3,0,1,2:T(8,128)S(1)} %pad_maximum_fusion.1) | data formatting | bytes 262144 | tf_op jit(solution)/shard_map/concatenate | solution.py:157
  (58 shorter events, 0.3 us)
Async XLA Ops:
  1.5 11.2 %copy-start = (f32[16,128,128]{2,1,0:T(8,128)S(1)}, f32[16,128,128]{2,1,0:T(8,128)}, u32[]{:S(2)}) copy-start(f32[16,128,128]{2,1,0:T(8,128)} %param.7) | copy-start | bytes 3145732
  12.6 1.4 %copy-start.1 = (bf16[3,16,128,128]{3,2,1,0:T(8,128)(2,1)S(1)}, bf16[3,16,128,128]{3,2,1,0:T(8,128)(2,1)}, u32[]{:S(2)}) copy-start(bf16[3,16,128,128]{3,2,1,0:T(8,128)(2,1)} %param.8) | copy-start | bytes 4718596
  15.8 1.3 %copy-start.3 = (f32[128,128]{1,0:T(8,128)S(1)}, f32[128,128]{1,0:T(8,128)}, u32[]{:S(2)}) copy-start(f32[128,128]{1,0:T(8,128)} %get-tuple-element.125) | copy-start | bytes 196612
  15.8 1.7 %copy-start.2 = (f32[128,128]{1,0:T(8,128)S(1)}, f32[128,128]{1,0:T(8,128)}, u32[]{:S(2)}) copy-start(f32[128,128]{1,0:T(8,128)} %get-tuple-element.109) | copy-start | bytes 196612
  17.0 1.0 %copy-start.11 = (f32[128,128]{1,0:T(8,128)S(1)}, f32[128,128]{1,0:T(8,128)}, u32[]{:S(2)}) copy-start(f32[128,128]{1,0:T(8,128)} %get-tuple-element.124) | copy-start | bytes 196612
  17.0 1.0 %copy-start.12 = (f32[128,128]{1,0:T(8,128)S(1)}, f32[128,128]{1,0:T(8,128)}, u32[]{:S(2)}) copy-start(f32[128,128]{1,0:T(8,128)} %get-tuple-element.126) | copy-start | bytes 196612
  17.0 1.0 %copy-start.13 = (f32[128,128]{1,0:T(8,128)S(1)}, f32[128,128]{1,0:T(8,128)}, u32[]{:S(2)}) copy-start(f32[128,128]{1,0:T(8,128)} %get-tuple-element.127) | copy-start | bytes 196612
  17.0 1.0 %copy-start.14 = (f32[128,128]{1,0:T(8,128)S(1)}, f32[128,128]{1,0:T(8,128)}, u32[]{:S(2)}) copy-start(f32[128,128]{1,0:T(8,128)} %get-tuple-element.128) | copy-start | bytes 196612
  17.0 1.0 %copy-start.15 = (f32[128,128]{1,0:T(8,128)S(1)}, f32[128,128]{1,0:T(8,128)}, u32[]{:S(2)}) copy-start(f32[128,128]{1,0:T(8,128)} %get-tuple-element.129) | copy-start | bytes 196612
  17.0 1.0 %copy-start.16 = (f32[128,128]{1,0:T(8,128)S(1)}, f32[128,128]{1,0:T(8,128)}, u32[]{:S(2)}) copy-start(f32[128,128]{1,0:T(8,128)} %get-tuple-element.130) | copy-start | bytes 196612
  17.1 1.0 %copy-start.17 = (f32[128,128]{1,0:T(8,128)S(1)}, f32[128,128]{1,0:T(8,128)}, u32[]{:S(2)}) copy-start(f32[128,128]{1,0:T(8,128)} %get-tuple-element.131) | copy-start | bytes 196612
  18.0 4.4 %copy-start.4 = (f32[128,128]{1,0:T(8,128)S(1)}, f32[128,128]{1,0:T(8,128)}, u32[]{:S(2)}) copy-start(f32[128,128]{1,0:T(8,128)} %get-tuple-element.108) | copy-start | bytes 196612
  18.1 4.4 %copy-start.5 = (f32[128,128]{1,0:T(8,128)S(1)}, f32[128,128]{1,0:T(8,128)}, u32[]{:S(2)}) copy-start(f32[128,128]{1,0:T(8,128)} %get-tuple-element.110) | copy-start | bytes 196612
  18.1 4.4 %copy-start.6 = (f32[128,128]{1,0:T(8,128)S(1)}, f32[128,128]{1,0:T(8,128)}, u32[]{:S(2)}) copy-start(f32[128,128]{1,0:T(8,128)} %get-tuple-element.111) | copy-start | bytes 196612
  18.1 4.4 %copy-start.7 = (f32[128,128]{1,0:T(8,128)S(1)}, f32[128,128]{1,0:T(8,128)}, u32[]{:S(2)}) copy-start(f32[128,128]{1,0:T(8,128)} %get-tuple-element.112) | copy-start | bytes 196612
  18.1 4.4 %copy-start.8 = (f32[128,128]{1,0:T(8,128)S(1)}, f32[128,128]{1,0:T(8,128)}, u32[]{:S(2)}) copy-start(f32[128,128]{1,0:T(8,128)} %get-tuple-element.113) | copy-start | bytes 196612
  18.1 4.4 %copy-start.9 = (f32[128,128]{1,0:T(8,128)S(1)}, f32[128,128]{1,0:T(8,128)}, u32[]{:S(2)}) copy-start(f32[128,128]{1,0:T(8,128)} %get-tuple-element.114) | copy-start | bytes 196612
  18.1 4.4 %copy-start.10 = (f32[128,128]{1,0:T(8,128)S(1)}, f32[128,128]{1,0:T(8,128)}, u32[]{:S(2)}) copy-start(f32[128,128]{1,0:T(8,128)} %get-tuple-element.115) | copy-start | bytes 196612
  22.5 8.8 %copy-start.18 = (s32[2,4,1,4]{3,2,1,0:T(1,128)S(1)}, s32[2,4,1,4]{3,2,1,0:T(1,128)}, u32[]{:S(2)}) copy-start(s32[2,4,1,4]{3,2,1,0:T(1,128)} %param.9) | copy-start | bytes 388
  26.7 6.2 %copy-start.20 = (s32[2,4]{1,0:T(2,128)S(1)}, s32[2,4]{1,0:T(2,128)}, u32[]{:S(2)}) copy-start(s32[2,4]{1,0:T(2,128)} %param.11) | copy-start | bytes 100
  26.7 6.5 %copy-start.19 = (s32[2,4,1,1]{1,3,2,0:T(1,128)S(1)}, s32[2,4,1,1]{1,3,2,0:T(1,128)}, u32[]{:S(2)}) copy-start(s32[2,4,1,1]{1,3,2,0:T(1,128)} %param.10) | copy-start | bytes 100
  27.9 8.8 %all-to-all-start = ((bf16[2,1,4,128,128]{4,2,0,1,3:T(4,128)(2,1)}), bf16[2,1,4,128,128]{4,2,0,1,3:T(4,128)(2,1)S(1)}, u32[]{:S(2)}, u32[]{:S(2)}) async-start(bf16[2,1,4,128,128]{4,2,0,1,3:T(4,128)(2,1)} %maximum_bitcast_fusion), calls=%async_computation | async-start | bytes 524288 | tf_op jit(solution)/shard_map/all_to_all | solution.py:115
  38.5 9.2 %collective-permute-start = (bf16[2,4,4,32,128]{4,1,3,2,0:T(4,128)(2,1)S(1)}, bf16[2,4,4,32,128]{4,1,3,2,0:T(4,128)(2,1)S(1)}, u32[]{:S(2)}, u32[]{:S(2)}) collective-permute-start(bf16[2,4,4,32,128]{4,1,3,2,0:T(4,128)(2,1)S(1)} %get-tuple-element.156), channel_id=1, source_target_pairs={{1,0},{2,1},{3,2},{5,4},{6,5},{7,6},{9,8},{10,9},{11,10},{13,12},{... | collective-permute-start | bytes 786440 | tf_op jit(solution)/shard_map/ppermute | solution.py:27
  40.8 14.1 %collective-permute-start.1 = (bf16[2,4,4,32,128]{4,1,3,2,0:T(4,128)(2,1)S(1)}, bf16[2,4,4,32,128]{4,1,3,2,0:T(4,128)(2,1)S(1)}, u32[]{:S(2)}, u32[]{:S(2)}) collective-permute-start(bf16[2,4,4,32,128]{4,1,3,2,0:T(4,128)(2,1)S(1)} %get-tuple-element.159), channel_id=1, source_target_pairs={{0,1},{1,2},{2,3},{4,5},{5,6},{6,7},{8,9},{9,10},{10,11},{12,13},{... | collective-permute-start | bytes 786440 | tf_op jit(solution)/shard_map/ppermute | solution.py:27
  44.3 13.4 %collective-permute-start.2 = (bf16[2,4,4,32,128]{4,1,3,2,0:T(4,128)(2,1)S(1)}, bf16[2,4,4,32,128]{4,1,3,2,0:T(4,128)(2,1)S(1)}, u32[]{:S(2)}, u32[]{:S(2)}) collective-permute-start(bf16[2,4,4,32,128]{4,1,3,2,0:T(4,128)(2,1)S(1)} %get-tuple-element.158), channel_id=1, source_target_pairs={{0,2},{1,3},{4,6},{5,7},{8,10},{9,11},{12,14},{13,15},{16,18},{17,... | collective-permute-start | bytes 786440 | tf_op jit(solution)/shard_map/ppermute | solution.py:27
where the time goes:
time: 62.7 us; the launch traced here: 61.5 us
  other arithmetic  19.1 us (30%)
  waiting for transfers between devices  13.4 us (21%)
  starting transfers between devices  11.8 us (19%)
  blocking collectives  9 us (14%)
  local copies, waits for them, and re-layouts  5.62 us (9%)
  matrix products  1.87 us (3%)
  between operations  0.64 us (1%)
    ppermute x3, waiting for transfers between devices, shifted(): lax.ppermute(value, axis, [(source, source + steps) for source in range(f...  10 us
    all_gather x1, blocking collectives, prefix_2(): pieces = lax.all_gather(value, axis)  9 us
    convert_element_type x2, other arithmetic, composite_brick(): colour_sum.astype(jnp.bfloat16)  8.46 us
    ppermute x3, starting transfers between devices, shifted(): lax.ppermute(value, axis, [(source, source + steps) for source in range(f...  8.35 us
    all_to_all x1, starting transfers between devices, on_device(): lax.all_to_all(brick_images[:, None], 'depth', split_axis=3, concat_axis=...  3.4 us
    all_to_all x1, waiting for transfers between devices, on_device(): lax.all_to_all(brick_images[:, None], 'depth', split_axis=3, concat_axis=...  3.39 us
    mul x2, other arithmetic, composite_brick(): colour_sum = colour_sum + transmit[None] * moved_colour  2.08 us
    mul x1, other arithmetic, on_device(): BRIGHTNESS * albedo.astype(jnp.float32) * (lighting * opacity)[None]  1.8 us
  transfers between devices with their start and end apart: 4, of which 3 were waited for; matrix products, arithmetic and copies ran while one was open for 4% of the time, Pallas kernels for 0%

commit v1 on v0

v1 whole, which is shorter than its diff:
```python
import functools
import math

import jax
import jax.numpy as jnp
from jax import lax
from jax.experimental import pallas as pl
from jax.experimental.pallas import tpu as pltpu
from jax.sharding import PartitionSpec as P

SHEARS = (0.3125, -0.4375)
BRIGHTNESS = 4.0
PAIR = 2
VMEM_BYTES = 16 * 1024 * 1024


def plane_steps(shear, depth_cells):
    whole = [math.floor(shear * z) for z in range(depth_cells)]
    return [(k, shear * z - k) for z, k in enumerate(whole)]


def column_shifts(shear, depth_cells):
    found = set()
    for k, f in plane_steps(shear, depth_cells):
        found |= {k, k + 1} if f > 0.0 else {k}
    return sorted(found)


def shift_list(depth_cells):
    return [(v, j) for v, s in enumerate(SHEARS) for j in column_shifts(s, depth_cells)]


def rolled(value, steps):
    size = value.shape[-1]
    steps = steps % size
    return pltpu.roll(value, steps, value.ndim - 1) if steps else value


def plane_kernel(density_ref, plane_ref):
    total = density_ref[0]
    for z in range(1, density_ref.shape[0]):
        total = total + density_ref[z]
    plane_ref[...] = jnp.exp(-total)


def slab_transmittance(density):
    depth_cells, rows, cols = density.shape
    block = min(rows, 32)
    return pl.pallas_call(
        plane_kernel,
        grid=(rows // block,),
        in_specs=[pl.BlockSpec((depth_cells, block, cols), lambda i: (0, i, 0))],
        out_specs=pl.BlockSpec((block, cols), lambda i: (i, 0)),
        out_shape=jax.ShapeDtypeStruct((rows, cols), jnp.float32),
        compiler_params=pltpu.CompilerParams(vmem_limit_bytes=VMEM_BYTES),
        name="slab_plane",
    )(density)


def opacity_weights(k, f, lane, cols):
    if k >= 0:
        inside = lane < cols - k
        return (jnp.where(inside, 1.0 - f, 0.0), jnp.where(inside & (lane >= 1), f, 0.0))
    inside = lane >= -k
    return (jnp.where(inside, 1.0 - f, 0.0), jnp.where(inside | (lane == 0), f, 0.0))


def sums_chunk(density_ref, albedo_ref, sums_ref, opac_ref, rows):
    depth_cells = density_ref.shape[0]
    cols = density_ref.shape[2]
    index = {key: i for i, key in enumerate(shift_list(depth_cells))}
    shape = (rows.size, cols)
    lane = lax.broadcasted_iota(jnp.int32, shape, 1)
    steps = [plane_steps(s, depth_cells) for s in SHEARS]
    transmit = [jnp.ones(shape, jnp.float32) for _ in SHEARS]
    frame = [0 for _ in SHEARS]
    sums = [{} for _ in SHEARS]
    light = jnp.full(shape, BRIGHTNESS, jnp.float32)
    for z in range(depth_cells):
        kept = jnp.exp(-density_ref[z, rows])
        opacity = 1.0 - kept
        lit = light * opacity
        light = light * kept
        farther = rolled(opacity, 1)
        colour = [albedo_ref[c, z, rows].astype(jnp.float32) for c in range(3)]
        for v in range(len(SHEARS)):
            k, f = steps[v][z]
            if frame[v] != k:
                transmit[v] = rolled(transmit[v], frame[v] - k)
                frame[v] = k
            for j, share in ((k, 1.0 - f), (k + 1, f)):
                if share == 0.0:
                    continue
                here = transmit[v] if j == k else rolled(transmit[v], -1)
                weight = here * (lit * share)
                for c in range(3):
                    term = weight * colour[c]
                    sums[v][j, c] = sums[v][j, c] + term if (j, c) in sums[v] else term
            a, b = opacity_weights(k, f, lane, cols)
            moved = a * opacity if f == 0.0 else a * opacity + b * farther
            transmit[v] = transmit[v] * (1.0 - moved)
            following = (steps[v][z + 1][0], steps[v][z + 1][0] + 1) if z + 1 < depth_cells else ()
            for j, c in list(sums[v]):
                if j not in following:
                    sums_ref[index[v, j] * 3 + c, rows] = sums[v].pop((j, c))
    for v in range(len(SHEARS)):
        opac_ref[v, rows] = (1.0 - rolled(transmit[v], frame[v])).astype(opac_ref.dtype)


def sums_kernel(chunk, density_ref, albedo_ref, sums_ref, opac_ref):
    block = density_ref.shape[1]

    def body(i, carry):
        rows = pl.ds(pl.multiple_of(i * chunk, chunk), chunk)
        sums_chunk(density_ref, albedo_ref, sums_ref, opac_ref, rows)
        return carry

    lax.fori_loop(0, block // chunk, body, 0)


def image_sums(density, albedo):
    depth_cells, rows, cols = density.shape
    count = 3 * len(shift_list(depth_cells))
    block = min(rows, 32)
    cells = depth_cells * rows * cols
    return pl.pallas_call(
        functools.partial(sums_kernel, 16),
        grid=(rows // block,),
        in_specs=[
            pl.BlockSpec((depth_cells, block, cols), lambda i: (0, i, 0)),
            pl.BlockSpec((3, depth_cells, block, cols), lambda i: (0, 0, i, 0)),
        ],
        out_specs=[
            pl.BlockSpec((count, block, cols), lambda i: (0, i, 0)),
            pl.BlockSpec((len(SHEARS), block, cols), lambda i: (0, i, 0)),
        ],
        out_shape=[
            jax.ShapeDtypeStruct((count, rows, cols), jnp.float32),
            jax.ShapeDtypeStruct((len(SHEARS), rows, cols), jnp.bfloat16),
        ],
        compiler_params=pltpu.CompilerParams(vmem_limit_bytes=VMEM_BYTES),
        cost_estimate=pl.CostEstimate(
            flops=60 * cells, bytes_accessed=10 * cells + 4 * count * rows * cols, transcendentals=cells
        ),
        name="image_sums",
    )(density, albedo)


def partner(mine, k, count):
    return mine ^ k if count & (count - 1) == 0 else lax.rem(mine + k, count)


def origin(mine, k, count):
    return mine ^ k if count & (count - 1) == 0 else lax.rem(mine - k + count, count)


def swap_depth(value, k, count):
    return lax.ppermute(value, "depth", [(i, int(partner(i, k, count)) if count & (count - 1) == 0 else (i + k) % count) for i in range(count)])


def lit_kernel(slabs, depth_cells, *refs):
    planes, (sums_ref, opac_ref), outs = refs[:slabs], refs[slabs : slabs + 2], refs[slabs + 2 :]
    mine = lax.axis_index("depth")
    strip, cols = outs[0].shape[2:]
    keys = shift_list(depth_cells)
    lane = lax.broadcasted_iota(jnp.int32, (strip, cols), 1)
    for k in range(slabs):
        rows = pl.ds(pl.multiple_of(partner(mine, k, slabs) * strip, strip), strip)
        incoming = jnp.ones((strip, cols), jnp.float32)
        for other in range(1, slabs):
            ahead = origin(mine, other, slabs) < mine
            incoming = incoming * jnp.where(ahead, planes[other][rows], 1.0)
        for v in range(len(SHEARS)):
            for c in range(3):
                total = None
                for i, (view, j) in enumerate(keys):
                    if view != v:
                        continue
                    moved = rolled(incoming * sums_ref[i * 3 + c, rows], j)
                    if j:
                        moved = jnp.where(lane >= j if j > 0 else lane < cols + j, moved, 0.0)
                    total = moved if total is None else total + moved
                outs[k][v, c] = total.astype(jnp.bfloat16)
            outs[k][v, 3] = opac_ref[v, rows]


def lit_strips(planes, sums, opac, depth_cells):
    slabs = len(planes)
    rows, cols = planes[0].shape
    strip = rows // slabs
    vmem = pl.BlockSpec(memory_space=pltpu.VMEM)
    return pl.pallas_call(
        functools.partial(lit_kernel, slabs, depth_cells),
        in_specs=[vmem] * (slabs + 2),
        out_specs=[vmem] * slabs,
        out_shape=[jax.ShapeDtypeStruct((len(SHEARS), 4, strip, cols), jnp.bfloat16)] * slabs,
        compiler_params=pltpu.CompilerParams(vmem_limit_bytes=VMEM_BYTES),
        name="lit_strips",
    )(*planes, sums, opac)


def piece_slots(step, slabs):
    return min(slabs, 2 * PAIR if step < slabs // 2 else PAIR)


def column_swaps(slabs, columns):
    swaps = []
    for step in range(1, slabs // 2 + 1):
        for parity in range(2):
            lefts = [c for c in range(columns - step) if (c // step) % 2 == parity]
            if step > 1 and step == slabs // 2:
                lefts = [c for c in lefts if c > 0]
            if lefts:
                swaps.append((step, parity, lefts))
    return swaps


def swap_columns(value, step, lefts, slabs, columns):
    to = {c: c + step for c in lefts} | {c + step: c for c in lefts}
    pairs = []
    for d in range(slabs):
        for c in range(columns):
            if c in to:
                pairs.append((d * columns + c, d * columns + to[c]))
            elif (d ^ 1) < slabs:
                pairs.append((d * columns + c, (d ^ 1) * columns + c))
    return lax.ppermute(value, ("depth", "col"), pairs)


def covers(targets_ref, view, slab, column, tile):
    first = targets_ref[view, slab, 0, column]
    return (first == tile) | (first + 1 == tile)


def slot_of(targets_ref, view, slab, column, tile, slots, slabs):
    if slots >= slabs:
        return slab
    slot = jnp.int32(0)
    for other in range(slabs):
        ahead = covers(targets_ref, view, other, column, tile) & (other < slab)
        slot = slot + ahead.astype(jnp.int32)
    return jnp.minimum(slot, slots - 1)


def pack_kernel(slabs, columns, swaps, targets_ref, offsets_ref, *refs):
    blocks, outs = refs[:slabs], refs[slabs:]
    mine, column = lax.axis_index("depth"), lax.axis_index("col")
    strip, cols = blocks[0].shape[2:]
    lane = lax.broadcasted_iota(jnp.int32, (4, strip, cols), 2)
    for out in outs:
        out[...] = jnp.zeros_like(out)
    for v in range(len(SHEARS)):
        for k in range(slabs):
            slab = origin(mine, k, slabs)
            first = targets_ref[v, slab, 0, column]
            offset = offsets_ref[v, slab, 0, 0]
            image = blocks[k][v].astype(jnp.float32)
            image = jnp.stack([pltpu.roll(image[c], offset, 1) for c in range(4)])
            left = jnp.where(lane >= offset, image, 0.0).astype(jnp.bfloat16)
            right = jnp.where(lane >= offset, 0.0, image).astype(jnp.bfloat16)
            for out, plan in zip(outs, [None] + swaps, strict=True):
                if plan is None:
                    tile = column
                else:
                    step, parity, _ = plan
                    is_left = lax.rem(lax.div(column, step), 2) == parity
                    tile = column + jnp.where(is_left, step, -step)
                slot = slot_of(targets_ref, v, slab, column, tile, out.shape[1], slabs)

                @pl.when(first == tile)
                def _(out=out, slot=slot, v=v, left=left):
                    out[v, slot] = left

                @pl.when(first + 1 == tile)
                def _(out=out, slot=slot, v=v, right=right):
                    out[v, slot] = right


def packed_pieces(blocks, targets, offsets, columns, swaps):
    slabs = len(blocks)
    views, _, strip, cols = blocks[0].shape
    vmem, smem = pl.BlockSpec(memory_space=pltpu.VMEM), pl.BlockSpec(memory_space=pltpu.SMEM)
    slots = [min(slabs, 2 * PAIR)] + [piece_slots(step, slabs) for step, _, _ in swaps]
    return pl.pallas_call(
        functools.partial(pack_kernel, slabs, columns, swaps),
        in_specs=[smem, smem] + [vmem] * slabs,
        out_specs=[vmem] * len(slots),
        out_shape=[jax.ShapeDtypeStruct((views, n, 4, strip, cols), jnp.bfloat16) for n in slots],
        compiler_params=pltpu.CompilerParams(vmem_limit_bytes=VMEM_BYTES),
        name="pack_pieces",
    )(targets, offsets, *blocks)


def frame_kernel(slabs, columns, swaps, targets_ref, order_ref, own_ref, *refs):
    received, frame_ref = refs[:-1], refs[-1]
    tile = lax.axis_index("col")
    strip, cols = own_ref.shape[3:]
    by_step = {}
    for ref, (step, parity, _) in zip(received, swaps, strict=True):
        by_step.setdefault(step, {})[parity] = ref
    for v in range(len(SHEARS)):
        colour = jnp.zeros((3, strip, cols), jnp.float32)
        weight = jnp.ones((strip, cols), jnp.float32)
        for position in range(slabs):
            slab = order_ref[v, position]
            for step in range(slabs // 2, -2, -1):
                source = tile - step
                present = (source >= 0) & (source < columns)
                column = jnp.clip(source, 0, columns - 1)
                present = present & covers(targets_ref, v, slab, column, tile)
                if step == 0:
                    refs_here = {0: own_ref}
                else:
                    refs_here = by_step.get(abs(step), {})
                if not refs_here:
                    continue
                left = jnp.minimum(source, tile)
                parity = lax.rem(lax.div(jnp.maximum(left, 0), max(abs(step), 1)), 2)
                slots = next(iter(refs_here.values())).shape[1]
                slot = slot_of(targets_ref, v, slab, column, tile, slots, slabs)
                pieces = [refs_here[q][v, slot] for q in sorted(refs_here)]
                piece = pieces[0] if len(pieces) == 1 else jnp.where(parity == 0, pieces[0], pieces[1])
                piece = jnp.where(present, piece.astype(jnp.float32), 0.0)
                colour = colour + weight[None] * piece[:3]
                weight = weight * (1.0 - piece[3])
        frame_ref[v, :3, 0] = colour
        frame_ref[v, 3, 0] = 1.0 - weight


def composed_frame(own, received, targets, slab_order, columns, swaps):
    views, _, _, strip, cols = own.shape
    slabs = slab_order.shape[1]
    vmem, smem = pl.BlockSpec(memory_space=pltpu.VMEM), pl.BlockSpec(memory_space=pltpu.SMEM)
    return pl.pallas_call(
        functools.partial(frame_kernel, slabs, columns, swaps),
        in_specs=[smem, smem] + [vmem] * (1 + len(received)),
        out_specs=vmem,
        out_shape=jax.ShapeDtypeStruct((views, 4, 1, strip, cols), jnp.float32),
        compiler_params=pltpu.CompilerParams(vmem_limit_bytes=VMEM_BYTES),
        name="compose_frame",
    )(targets, slab_order, own, *received)


def on_device(density, albedo, targets, offsets, slab_order):
    depth_cells = density.shape[0]
    slabs, columns = lax.axis_size("depth"), lax.axis_size("col")
    plane = slab_transmittance(density)
    planes = [plane] + [swap_depth(plane, k, slabs) for k in range(1, slabs)]
    sums, opac = image_sums(density, albedo)
    strips = lit_strips(planes, sums, opac, depth_cells)
    blocks = [strips[0]] + [swap_depth(strips[k], k, slabs) for k in range(1, slabs)]
    swaps = column_swaps(slabs, columns)
    own, *outgoing = packed_pieces(blocks, targets, offsets, columns, swaps)
    received = [
        swap_columns(value, step, lefts, slabs, columns)
        for value, (step, _, lefts) in zip(outgoing, swaps, strict=True)
    ]
    return composed_frame(own, received, targets, slab_order, columns, swaps)


def solution(mesh):
    in_specs = (
        P("depth", "row", "col"),
        P(None, "depth", "row", "col"),
        P(None, None, "row", None),
        P(None, None, "row", "col"),
        P(),
    )
    out_specs = P(None, None, "row", "depth", "col")
    return jax.shard_map(
        on_device, mesh=mesh, in_specs=in_specs, out_specs=out_specs, check_vma=False
    )
```

time: 62.7 us -> 35.4 us (0.56)
  the two profiles are of different devices: /device:TPU:8 before, /device:TPU:0 now
where the time goes in v1:
time: 35.4 us; the launch traced here: 35.2 us
  starting transfers between devices  11.7 us (33%)
  waiting for transfers between devices  11.4 us (32%)
  Pallas kernels  9.31 us (26%)
  local copies, waits for them, and re-layouts  2.74 us (8%)
    ppermute x6, starting transfers between devices, swap_depth(): lax.ppermute(value, 'depth', [(i, int(partner(i, k, count)) if count & co...  8.1 us
    ppermute x3, waiting for transfers between devices, swap_columns(): return lax.ppermute(value, ('depth', 'col'), pairs)  6.39 us
    pallas_call x1, Pallas kernels, image_sums(): pl.pallas_call(functools.partial(sums_kernel, 16), grid=(rows // block,),...  5.08 us
    ppermute x6, waiting for transfers between devices, swap_depth(): lax.ppermute(value, 'depth', [(i, int(partner(i, k, count)) if count & co...  5.05 us
    ppermute x3, starting transfers between devices, swap_columns(): return lax.ppermute(value, ('depth', 'col'), pairs)  3.58 us
    unnamed x11, local copies, waits for them, and re-layouts  2.74 us
    pallas_call x1, Pallas kernels, composed_frame(): pl.pallas_call(functools.partial(frame_kernel, slabs, columns, swaps), in...  1.68 us
    pallas_call x1, Pallas kernels, packed_pieces(): pl.pallas_call(functools.partial(pack_kernel, slabs, columns, swaps), in_...  1.61 us
  transfers between devices with their start and end apart: 9, of which 4 were waited for; matrix products, arithmetic and copies ran while one was open for 0% of the time, Pallas kernels for 14%

profile of v1, /device:TPU:0, one launch (start us, length us, event | category | flops | bytes accessed | tf_op | source)
XLA Modules:
  0.0 35.2 jit_solution(5024995547904663338)
XLA Ops:
  0.0 0.0 copy-start
  0.0 1.2 %copy-done = f32[16,128,128]{2,1,0:T(8,128)S(1)} copy-done((f32[16,128,128]{2,1,0:T(8,128)S(1)}, f32[16,128,128]{2,1,0:T(8,128)}, u32[]{:S(2)}) %copy-start) | copy-done | bytes 1048600
  1.2 0.0 copy-start.4
  1.2 0.0 copy-start.2
  1.2 0.0 copy-start.3
  1.2 0.2 slab_plane.1.refs_0_
  1.5 3.0 %collective-permute-start = (f32[128,128]{1,0:T(8,128)S(1)}, f32[128,128]{1,0:T(8,128)S(1)}, u32[]{:S(2)}, u32[]{:S(2)}) collective-permute-start(f32[128,128]{1,0:T(8,128)S(1)} %slab_plane.1.refs_0_), channel_id=1, source_target_pairs={{0,8},{8,0},{16,24},{24,16},{1,9},{9,1},{17,25},{25,17},{2,10},{10... | collective-permute-start | bytes 196616 | tf_op jit(solution)/shard_map/ppermute | solution.py:158
  4.5 1.5 %collective-permute-start.1 = (f32[128,128]{1,0:T(8,128)S(1)}, f32[128,128]{1,0:T(8,128)S(1)}, u32[]{:S(2)}, u32[]{:S(2)}) collective-permute-start(f32[128,128]{1,0:T(8,128)S(1)} %slab_plane.1.refs_0_), channel_id=1, source_target_pairs={{0,16},{8,24},{16,0},{24,8},{1,17},{9,25},{17,1},{25,9},{2,18},{10... | collective-permute-start | bytes 196616 | tf_op jit(solution)/shard_map/ppermute | solution.py:158
  6.0 0.0 collective-permute-start.2
  6.0 0.0 copy-start.1
  6.0 1.4 %copy-done.1 = bf16[3,16,128,128]{3,2,1,0:T(8,128)(2,1)S(1)} copy-done((bf16[3,16,128,128]{3,2,1,0:T(8,128)(2,1)S(1)}, bf16[3,16,128,128]{3,2,1,0:T(8,128)(2,1)}, u32[]{:S(2)}) %copy-start.1) | copy-done | bytes 1572888
  7.4 5.1 %image_sums.1 = (f32[42,128,128]{2,1,0:T(8,128)S(1)}, bf16[2,128,128]{2,1,0:T(8,128)(2,1)S(1)}) custom-call(f32[16,128,128]{2,1,0:T(8,128)S(1)} %copy-done, bf16[3,16,128,128]{3,2,1,0:T(8,128)(2,1)S(1)} %copy-done.1), custom_call_target="tpu_custom_call" | custom-call | flops 15728640 | bytes 5373952 | tf_op jit(solution)/shard_map/image_sums/pallas_call | solution.py:126
  12.5 0.0 collective-permute-done.refs_1_
  12.5 0.0 collective-permute-done.1.refs_2_
  12.5 0.0 collective-permute-done.2.refs_3_
  12.6 0.7 %lit_strips.1 = (bf16[2,4,32,128]{3,2,1,0:T(8,128)(2,1)S(1)}, bf16[2,4,32,128]{3,2,1,0:T(8,128)(2,1)S(1)}, bf16[2,4,32,128]{3,2,1,0:T(8,128)(2,1)S(1)}, bf16[2,4,32,128]{3,2,1,0:T(8,128)(2,1)S(1)}) custom-call(f32[128,128]{1,0:T(8,128)S(1)} %slab_plane.1.refs_0_, f32[128,128]{1,0:T(8,128)S(1)} %collective-permute-done.refs_1_, ...), custom_call_target="tpu_custom_call" | custom-call | tf_op jit(solution)/shard_map/lit_strips/pallas_call | solution.py:192
  13.3 2.0 %collective-permute-start.3 = (bf16[2,4,32,128]{3,2,1,0:T(8,128)(2,1)S(1)}, bf16[2,4,32,128]{3,2,1,0:T(8,128)(2,1)S(1)}, u32[]{:S(2)}, u32[]{:S(2)}) collective-permute-start(bf16[2,4,32,128]{3,2,1,0:T(8,128)(2,1)S(1)} %get-tuple-element.18), channel_id=1, source_target_pairs={{0,8},{8,0},{16,24},{24,16},{1,9},{9,1},{17,25},{25,17},{2,10},{10... | collective-permute-start | bytes 196616 | tf_op jit(solution)/shard_map/ppermute | solution.py:158
  15.3 1.5 %collective-permute-start.4 = (bf16[2,4,32,128]{3,2,1,0:T(8,128)(2,1)S(1)}, bf16[2,4,32,128]{3,2,1,0:T(8,128)(2,1)S(1)}, u32[]{:S(2)}, u32[]{:S(2)}) collective-permute-start(bf16[2,4,32,128]{3,2,1,0:T(8,128)(2,1)S(1)} %get-tuple-element.19), channel_id=1, source_target_pairs={{0,16},{8,24},{16,0},{24,8},{1,17},{9,25},{17,1},{25,9},{2,18},{10... | collective-permute-start | bytes 196616 | tf_op jit(solution)/shard_map/ppermute | solution.py:158
  16.8 0.0 collective-permute-start.5
  16.8 0.0 copy-done.4
  16.8 0.1 copy.6.offsets_ref
  16.9 0.7 %collective-permute-done.3.refs_1_ = bf16[2,4,32,128]{3,2,1,0:T(8,128)(2,1)S(1)} collective-permute-done((bf16[2,4,32,128]{3,2,1,0:T(8,128)(2,1)S(1)}, bf16[2,4,32,128]{3,2,1,0:T(8,128)(2,1)S(1)}, u32[]{:S(2)}, u32[]{:S(2)}) %collective-permute-start.3) | collective-permute-done | bytes 65568 | tf_op jit(solution)/shard_map/ppermute | solution.py:158
  17.6 2.6 %collective-permute-done.4.refs_2_ = bf16[2,4,32,128]{3,2,1,0:T(8,128)(2,1)S(1)} collective-permute-done((bf16[2,4,32,128]{3,2,1,0:T(8,128)(2,1)S(1)}, bf16[2,4,32,128]{3,2,1,0:T(8,128)(2,1)S(1)}, u32[]{:S(2)}, u32[]{:S(2)}) %collective-permute-start.4) | collective-permute-done | bytes 65568 | tf_op jit(solution)/shard_map/ppermute | solution.py:158
  20.1 1.8 %collective-permute-done.5.refs_3_ = bf16[2,4,32,128]{3,2,1,0:T(8,128)(2,1)S(1)} collective-permute-done((bf16[2,4,32,128]{3,2,1,0:T(8,128)(2,1)S(1)}, bf16[2,4,32,128]{3,2,1,0:T(8,128)(2,1)S(1)}, u32[]{:S(2)}, u32[]{:S(2)}) %collective-permute-start.5) | collective-permute-done | bytes 65568 | tf_op jit(solution)/shard_map/ppermute | solution.py:158
  22.0 0.0 copy-done.2
  22.0 1.6 %pack_pieces.1 = (bf16[2,4,4,32,128]{4,3,2,1,0:T(8,128)(2,1)S(1)}, bf16[2,4,4,32,128]{4,3,2,1,0:T(8,128)(2,1)S(1)}, bf16[2,4,4,32,128]{4,3,2,1,0:T(8,128)(2,1)S(1)}, bf16[2,2,4,32,128]{4,3,2,1,0:T(8,128)(2,1)S(1)}) custom-call(s32[2,4,1,4]{3,2,1,0:T(1,128)S(1)} %copy-done.2, s32[2,4,1,1]{3,2,1,0:T(1,128)S(1)} %copy.6.offsets_ref, ...), custom_call_target="tpu_custom_call" | custom-call | tf_op jit(solution)/shard_map/pack_pieces/pallas_call | solution.py:284
  23.6 1.6 %collective-permute-start.6 = (bf16[2,4,4,32,128]{4,3,2,1,0:T(8,128)(2,1)S(1)}, bf16[2,4,4,32,128]{4,3,2,1,0:T(8,128)(2,1)S(1)}, u32[]{:S(2)}, u32[]{:S(2)}) collective-permute-start(bf16[2,4,4,32,128]{4,3,2,1,0:T(8,128)(2,1)S(1)} %get-tuple-element.22), channel_id=1, source_target_pairs={{0,1},{1,0},{2,3},{3,2},{8,9},{9,8},{10,11},{11,10},{16,17},{17,16... | collective-permute-start | bytes 786440 | tf_op jit(solution)/shard_map/ppermute | solution.py:227
  25.1 0.5 %collective-permute-start.7 = (bf16[2,4,4,32,128]{4,3,2,1,0:T(8,128)(2,1)S(1)}, bf16[2,4,4,32,128]{4,3,2,1,0:T(8,128)(2,1)S(1)}, u32[]{:S(2)}, u32[]{:S(2)}) collective-permute-start(bf16[2,4,4,32,128]{4,3,2,1,0:T(8,128)(2,1)S(1)} %get-tuple-element.23), channel_id=1, source_target_pairs={{0,8},{1,2},{2,1},{3,11},{8,0},{9,10},{10,9},{11,3},{16,24},{17,18... | collective-permute-start | bytes 786440 | tf_op jit(solution)/shard_map/ppermute | solution.py:227
  25.7 1.5 %collective-permute-start.8 = (bf16[2,2,4,32,128]{4,3,2,1,0:T(8,128)(2,1)S(1)}, bf16[2,2,4,32,128]{4,3,2,1,0:T(8,128)(2,1)S(1)}, u32[]{:S(2)}, u32[]{:S(2)}) collective-permute-start(bf16[2,2,4,32,128]{4,3,2,1,0:T(8,128)(2,1)S(1)} %get-tuple-element.24), channel_id=1, source_target_pairs={{0,8},{1,3},{2,10},{3,1},{8,0},{9,11},{10,2},{11,9},{16,24},{17,19... | collective-permute-start | bytes 393224 | tf_op jit(solution)/shard_map/ppermute | solution.py:227
  27.2 6.4 %collective-permute-done.8.refs_2_ = bf16[2,2,4,32,128]{4,3,2,1,0:T(8,128)(2,1)S(1)} collective-permute-done((bf16[2,2,4,32,128]{4,3,2,1,0:T(8,128)(2,1)S(1)}, bf16[2,2,4,32,128]{4,3,2,1,0:T(8,128)(2,1)S(1)}, u32[]{:S(2)}, u32[]{:S(2)}) %collective-permute-start.8) | collective-permute-done | bytes 131104 | tf_op jit(solution)/shard_map/ppermute | solution.py:227
  33.5 0.0 collective-permute-done.6.refs_0_
  33.6 0.0 collective-permute-done.7.refs_1_
  33.6 0.0 copy-done.3
  33.6 1.7 %compose_frame.1 = f32[2,4,1,32,128]{4,3,2,1,0:T(8,128)} custom-call(s32[2,4,1,4]{3,2,1,0:T(1,128)S(1)} %copy-done.2, s32[2,4]{1,0:T(2,128)S(1)} %copy-done.3, bf16[2,4,4,32,128]{4,3,2,1,0:T(8,128)(2,1)S(1)} %get-tuple-element.21.own_ref, bf16[2,4,4,32,128]{4,3,2,1,0:T(8,128)(2,1)S(1)} %collective-permute-done.6.refs_0_, ...), custom_call_target="tpu_custom_call" | custom-call | tf_op jit(solution)/shard_map/compose_frame/pallas_call | solution.py:334
Async XLA Ops:
  0.0 1.2 %copy-start = (f32[16,128,128]{2,1,0:T(8,128)S(1)}, f32[16,128,128]{2,1,0:T(8,128)}, u32[]{:S(2)}) copy-start(f32[16,128,128]{2,1,0:T(8,128)} %density_ref.3) | copy-start | bytes 3145732
  1.2 15.6 %copy-start.4 = (s32[2,4,1,1]{1,3,2,0:T(1,128)S(1)}, s32[2,4,1,1]{1,3,2,0:T(1,128)}, u32[]{:S(2)}) copy-start(s32[2,4,1,1]{1,3,2,0:T(1,128)} %param.8) | copy-start | bytes 100
  1.2 20.7 %copy-start.2 = (s32[2,4,1,4]{3,2,1,0:T(1,128)S(1)}, s32[2,4,1,4]{3,2,1,0:T(1,128)}, u32[]{:S(2)}) copy-start(s32[2,4,1,4]{3,2,1,0:T(1,128)} %targets_ref.3) | copy-start | bytes 388
  1.2 32.3 %copy-start.3 = (s32[2,4]{1,0:T(2,128)S(1)}, s32[2,4]{1,0:T(2,128)}, u32[]{:S(2)}) copy-start(s32[2,4]{1,0:T(2,128)} %order_ref.1) | copy-start | bytes 100
  1.5 11.0 %collective-permute-start = (f32[128,128]{1,0:T(8,128)S(1)}, f32[128,128]{1,0:T(8,128)S(1)}, u32[]{:S(2)}, u32[]{:S(2)}) collective-permute-start(f32[128,128]{1,0:T(8,128)S(1)} %slab_plane.1.refs_0_), channel_id=1, source_target_pairs={{0,8},{8,0},{16,24},{24,16},{1,9},{9,1},{17,25},{25,17},{2,10},{10... | collective-permute-start | bytes 196616 | tf_op jit(solution)/shard_map/ppermute | solution.py:158
  4.5 8.1 %collective-permute-start.1 = (f32[128,128]{1,0:T(8,128)S(1)}, f32[128,128]{1,0:T(8,128)S(1)}, u32[]{:S(2)}, u32[]{:S(2)}) collective-permute-start(f32[128,128]{1,0:T(8,128)S(1)} %slab_plane.1.refs_0_), channel_id=1, source_target_pairs={{0,16},{8,24},{16,0},{24,8},{1,17},{9,25},{17,1},{25,9},{2,18},{10... | collective-permute-start | bytes 196616 | tf_op jit(solution)/shard_map/ppermute | solution.py:158
  6.0 6.5 %collective-permute-start.2 = (f32[128,128]{1,0:T(8,128)S(1)}, f32[128,128]{1,0:T(8,128)S(1)}, u32[]{:S(2)}, u32[]{:S(2)}) collective-permute-start(f32[128,128]{1,0:T(8,128)S(1)} %slab_plane.1.refs_0_), channel_id=1, source_target_pairs={{0,24},{8,16},{16,8},{24,0},{1,25},{9,17},{17,9},{25,1},{2,26},{10... | collective-permute-start | bytes 196616 | tf_op jit(solution)/shard_map/ppermute | solution.py:158
  6.0 1.4 %copy-start.1 = (bf16[3,16,128,128]{3,2,1,0:T(8,128)(2,1)S(1)}, bf16[3,16,128,128]{3,2,1,0:T(8,128)(2,1)}, u32[]{:S(2)}) copy-start(bf16[3,16,128,128]{3,2,1,0:T(8,128)(2,1)} %albedo_ref.1) | copy-start | bytes 4718596
  13.3 4.3 %collective-permute-start.3 = (bf16[2,4,32,128]{3,2,1,0:T(8,128)(2,1)S(1)}, bf16[2,4,32,128]{3,2,1,0:T(8,128)(2,1)S(1)}, u32[]{:S(2)}, u32[]{:S(2)}) collective-permute-start(bf16[2,4,32,128]{3,2,1,0:T(8,128)(2,1)S(1)} %get-tuple-element.18), channel_id=1, source_target_pairs={{0,8},{8,0},{16,24},{24,16},{1,9},{9,1},{17,25},{25,17},{2,10},{10... | collective-permute-start | bytes 196616 | tf_op jit(solution)/shard_map/ppermute | solution.py:158
  15.3 4.9 %collective-permute-start.4 = (bf16[2,4,32,128]{3,2,1,0:T(8,128)(2,1)S(1)}, bf16[2,4,32,128]{3,2,1,0:T(8,128)(2,1)S(1)}, u32[]{:S(2)}, u32[]{:S(2)}) collective-permute-start(bf16[2,4,32,128]{3,2,1,0:T(8,128)(2,1)S(1)} %get-tuple-element.19), channel_id=1, source_target_pairs={{0,16},{8,24},{16,0},{24,8},{1,17},{9,25},{17,1},{25,9},{2,18},{10... | collective-permute-start | bytes 196616 | tf_op jit(solution)/shard_map/ppermute | solution.py:158
  16.8 5.2 %collective-permute-start.5 = (bf16[2,4,32,128]{3,2,1,0:T(8,128)(2,1)S(1)}, bf16[2,4,32,128]{3,2,1,0:T(8,128)(2,1)S(1)}, u32[]{:S(2)}, u32[]{:S(2)}) collective-permute-start(bf16[2,4,32,128]{3,2,1,0:T(8,128)(2,1)S(1)} %get-tuple-element.20), channel_id=1, source_target_pairs={{0,24},{8,16},{16,8},{24,0},{1,25},{9,17},{17,9},{25,1},{2,26},{10... | collective-permute-start | bytes 196616 | tf_op jit(solution)/shard_map/ppermute | solution.py:158
  23.6 10.0 %collective-permute-start.6 = (bf16[2,4,4,32,128]{4,3,2,1,0:T(8,128)(2,1)S(1)}, bf16[2,4,4,32,128]{4,3,2,1,0:T(8,128)(2,1)S(1)}, u32[]{:S(2)}, u32[]{:S(2)}) collective-permute-start(bf16[2,4,4,32,128]{4,3,2,1,0:T(8,128)(2,1)S(1)} %get-tuple-element.22), channel_id=1, source_target_pairs={{0,1},{1,0},{2,3},{3,2},{8,9},{9,8},{10,11},{11,10},{16,17},{17,16... | collective-permute-start | bytes 786440 | tf_op jit(solution)/shard_map/ppermute | solution.py:227
  25.1 8.4 %collective-permute-start.7 = (bf16[2,4,4,32,128]{4,3,2,1,0:T(8,128)(2,1)S(1)}, bf16[2,4,4,32,128]{4,3,2,1,0:T(8,128)(2,1)S(1)}, u32[]{:S(2)}, u32[]{:S(2)}) collective-permute-start(bf16[2,4,4,32,128]{4,3,2,1,0:T(8,128)(2,1)S(1)} %get-tuple-element.23), channel_id=1, source_target_pairs={{0,8},{1,2},{2,1},{3,11},{8,0},{9,10},{10,9},{11,3},{16,24},{17,18... | collective-permute-start | bytes 786440 | tf_op jit(solution)/shard_map/ppermute | solution.py:227
  25.7 7.9 %collective-permute-start.8 = (bf16[2,2,4,32,128]{4,3,2,1,0:T(8,128)(2,1)S(1)}, bf16[2,2,4,32,128]{4,3,2,1,0:T(8,128)(2,1)S(1)}, u32[]{:S(2)}, u32[]{:S(2)}) collective-permute-start(bf16[2,2,4,32,128]{4,3,2,1,0:T(8,128)(2,1)S(1)} %get-tuple-element.24), channel_id=1, source_target_pairs={{0,8},{1,3},{2,10},{3,1},{8,0},{9,11},{10,2},{11,9},{16,24},{17,19... | collective-permute-start | bytes 393224 | tf_op jit(solution)/shard_map/ppermute | solution.py:227

commit v2 on v1

v2 whole, which is shorter than its diff:
```python
import functools
import math

import jax
import jax.numpy as jnp
from jax import lax
from jax.experimental import pallas as pl
from jax.experimental.pallas import tpu as pltpu
from jax.sharding import PartitionSpec as P

SHEARS = (0.3125, -0.4375)
BRIGHTNESS = 4.0
DENSITY_RANGE = (0.002, 0.05)
CODE_REACH = 76.0
PAIR = 2
VMEM_BYTES = 16 * 1024 * 1024


def plane_steps(shear, depth_cells):
    whole = [math.floor(shear * z) for z in range(depth_cells)]
    return [(k, shear * z - k) for z, k in enumerate(whole)]


def column_shifts(shear, depth_cells):
    found = set()
    for k, f in plane_steps(shear, depth_cells):
        found |= {k, k + 1} if f > 0.0 else {k}
    return sorted(found)


def shift_list(depth_cells):
    return [(v, j) for v, s in enumerate(SHEARS) for j in column_shifts(s, depth_cells)]


def rolled(value, steps):
    size = value.shape[-1]
    steps = steps % size
    return pltpu.roll(value, steps, value.ndim - 1) if steps else value


def depth_code(depth_cells):
    low, high = (depth_cells * d for d in DENSITY_RANGE)
    return 0.5 * (low + high), CODE_REACH / (0.5 * (high - low))


def plane_kernel(parts, density_hbm, code_ref, density_ref, sems):
    depth_cells, rows, _ = density_ref.shape
    block = rows // parts
    middle, spread = depth_code(depth_cells)
    copies = []
    for i in range(parts):
        part = pl.ds(i * block, block)
        copies.append(pltpu.make_async_copy(density_hbm.at[:, part], density_ref.at[:, part], sems.at[i]))
    for copy in copies:
        copy.start()
    for i in range(parts):
        copies[i].wait()
        part = pl.ds(i * block, block)
        total = density_ref[0, part]
        for z in range(1, depth_cells):
            total = total + density_ref[z, part]
        code = jnp.exp(jnp.clip((total - middle) * spread, -CODE_REACH, CODE_REACH))
        code_ref[part] = code.astype(jnp.bfloat16)


def slab_code(density):
    parts = max(1, density.shape[1] // 32)
    return pl.pallas_call(
        functools.partial(plane_kernel, parts),
        in_specs=[pl.BlockSpec(memory_space=pl.ANY)],
        out_specs=[pl.BlockSpec(memory_space=pltpu.VMEM)] * 2,
        out_shape=[
            pltpu.VMEM(density.shape[1:], jnp.bfloat16),
            pltpu.VMEM(density.shape, density.dtype),
        ],
        scratch_shapes=[pltpu.SemaphoreType.DMA((parts,))],
        compiler_params=pltpu.CompilerParams(vmem_limit_bytes=VMEM_BYTES),
        name="slab_code",
    )(pltpu.with_memory_space_constraint(density, pltpu.HBM))


def opacity_weights(k, f, lane, cols):
    if k >= 0:
        inside = lane < cols - k
        return (jnp.where(inside, 1.0 - f, 0.0), jnp.where(inside & (lane >= 1), f, 0.0))
    inside = lane >= -k
    return (jnp.where(inside, 1.0 - f, 0.0), jnp.where(inside | (lane == 0), f, 0.0))


def sums_chunk(density_ref, albedo_ref, sums_ref, opac_ref, rows):
    depth_cells = density_ref.shape[0]
    cols = density_ref.shape[2]
    index = {key: i for i, key in enumerate(shift_list(depth_cells))}
    shape = (rows.size, cols)
    lane = lax.broadcasted_iota(jnp.int32, shape, 1)
    steps = [plane_steps(s, depth_cells) for s in SHEARS]
    transmit = [jnp.ones(shape, jnp.float32) for _ in SHEARS]
    sums = [{} for _ in SHEARS]
    light = jnp.full(shape, BRIGHTNESS, jnp.float32)
    for z in range(depth_cells):
        kept = jnp.exp(-density_ref[z, rows])
        opacity = 1.0 - kept
        lit = light * opacity
        light = light * kept
        farther = rolled(opacity, 1)
        colour = [albedo_ref[c, z, rows].astype(jnp.float32) for c in range(3)]
        for v in range(len(SHEARS)):
            k, f = steps[v][z]
            for j, share in ((k, 1.0 - f), (k + 1, f)):
                if share == 0.0:
                    continue
                weight = rolled(transmit[v], -j) * (lit * share)
                for c in range(3):
                    term = weight * colour[c]
                    sums[v][j, c] = sums[v][j, c] + term if (j, c) in sums[v] else term
            a, b = opacity_weights(k, f, lane, cols)
            moved = a * opacity if f == 0.0 else a * opacity + b * farther
            transmit[v] = transmit[v] * (1.0 - rolled(moved, k))
            following = (steps[v][z + 1][0], steps[v][z + 1][0] + 1) if z + 1 < depth_cells else ()
            for j, c in list(sums[v]):
                if j not in following:
                    total = sums[v].pop((j, c))
                    if j:
                        total = jnp.where(lane < cols - j if j > 0 else lane >= -j, total, 0.0)
                    sums_ref[index[v, j] * 3 + c, rows] = total
    for v in range(len(SHEARS)):
        opac_ref[v, rows] = 1.0 - transmit[v]


def sums_kernel(chunk, parts, density_ref, albedo_hbm, sums_ref, opac_ref, albedo_ref, sems):
    rows = density_ref.shape[1]
    block = rows // parts

    def copy(i):
        part = pl.ds(pl.multiple_of(i * block, block), block)
        return pltpu.make_async_copy(albedo_hbm.at[:, :, part], albedo_ref.at[:, :, part], sems.at[i])

    for i in range(parts):
        copy(i).start()

    def body(i, carry):
        copy(i).wait()
        for part in range(block // chunk):
            at = pl.ds(pl.multiple_of(i * block + part * chunk, chunk), chunk)
            sums_chunk(density_ref, albedo_ref, sums_ref, opac_ref, at)
        return carry

    lax.fori_loop(0, parts, body, 0)


def image_sums(density, albedo):
    depth_cells, rows, cols = density.shape
    count = 3 * len(shift_list(depth_cells))
    chunk = 16
    parts = rows // chunk
    cells = depth_cells * rows * cols
    vmem = pl.BlockSpec(memory_space=pltpu.VMEM)
    return pl.pallas_call(
        functools.partial(sums_kernel, chunk, parts),
        in_specs=[vmem, pl.BlockSpec(memory_space=pl.ANY)],
        out_specs=[vmem, vmem],
        out_shape=[
            pltpu.VMEM((count, rows, cols), jnp.float32),
            pltpu.VMEM((len(SHEARS), rows, cols), jnp.float32),
        ],
        scratch_shapes=[pltpu.VMEM(albedo.shape, albedo.dtype), pltpu.SemaphoreType.DMA((parts,))],
        compiler_params=pltpu.CompilerParams(vmem_limit_bytes=VMEM_BYTES),
        cost_estimate=pl.CostEstimate(
            flops=60 * cells, bytes_accessed=10 * cells + 4 * count * rows * cols, transcendentals=cells
        ),
        name="image_sums",
    )(density, pltpu.with_memory_space_constraint(albedo, pltpu.HBM))


def partner(mine, k, count):
    return mine ^ k if count & (count - 1) == 0 else lax.rem(mine + k, count)


def origin(mine, k, count):
    return mine ^ k if count & (count - 1) == 0 else lax.rem(mine - k + count, count)


def swap_depth(value, k, count):
    return lax.ppermute(value, "depth", [(i, int(partner(i, k, count)) if count & (count - 1) == 0 else (i + k) % count) for i in range(count)])


def lit_kernel(slabs, depth_cells, offsets_any, *refs):
    codes, (sums_ref, opac_ref) = refs[:slabs], refs[slabs : slabs + 2]
    outs, (plain_ref, offsets_ref, sem) = refs[slabs + 2 : -3], refs[-3:]
    fetch = pltpu.make_async_copy(offsets_any, offsets_ref, sem)
    fetch.start()
    mine = lax.axis_index("depth")
    strip, cols = outs[0].shape[2:]
    keys = shift_list(depth_cells)
    middle, spread = depth_code(depth_cells)
    for k in range(slabs):
        rows = pl.ds(pl.multiple_of(partner(mine, k, slabs) * strip, strip), strip)
        ahead_depth = jnp.zeros((strip, cols), jnp.float32)
        for other in range(1, slabs):
            ahead = origin(mine, other, slabs) < mine
            depth = jnp.log(codes[other][rows].astype(jnp.float32)) * (1.0 / spread) + middle
            ahead_depth = ahead_depth + jnp.where(ahead, depth, 0.0)
        incoming = jnp.exp(-ahead_depth)
        for v in range(len(SHEARS)):
            for c in range(3):
                total = None
                for i, (view, j) in enumerate(keys):
                    if view != v:
                        continue
                    moved = rolled(incoming * sums_ref[i * 3 + c, rows], j)
                    total = moved if total is None else total + moved
                plain_ref[k, v, c] = total
    fetch.wait()
    for v in range(len(SHEARS)):
        turn = offsets_ref[v, mine]
        for k in range(slabs):
            rows = pl.ds(pl.multiple_of(partner(mine, k, slabs) * strip, strip), strip)
            for c in range(3):
                outs[k][v, c] = pltpu.roll(plain_ref[k, v, c], turn, 1).astype(jnp.bfloat16)
            outs[k][v, 3] = pltpu.roll(opac_ref[v, rows], turn, 1).astype(jnp.bfloat16)


def lit_strips(codes, sums, opac, offsets, depth_cells):
    slabs = len(codes)
    rows, cols = codes[0].shape
    strip = rows // slabs
    vmem = pl.BlockSpec(memory_space=pltpu.VMEM)
    return pl.pallas_call(
        functools.partial(lit_kernel, slabs, depth_cells),
        in_specs=[pl.BlockSpec(memory_space=pl.ANY)] + [vmem] * (slabs + 2),
        out_specs=[vmem] * slabs,
        out_shape=[jax.ShapeDtypeStruct((len(SHEARS), 4, strip, cols), jnp.bfloat16)] * slabs,
        scratch_shapes=[
            pltpu.VMEM((slabs, len(SHEARS), 3, strip, cols), jnp.float32),
            pltpu.SMEM(offsets.shape, jnp.int32),
            pltpu.SemaphoreType.DMA(()),
        ],
        compiler_params=pltpu.CompilerParams(vmem_limit_bytes=VMEM_BYTES),
        name="lit_strips",
    )(offsets, *codes, sums, opac)


def piece_slots(step, slabs):
    return min(slabs, 2 * PAIR if step < slabs // 2 else PAIR)


def column_swaps(slabs, columns):
    swaps = []
    for step in range(1, slabs // 2 + 1):
        for parity in range(2):
            lefts = [c for c in range(columns - step) if (c // step) % 2 == parity]
            if step > 1 and step == slabs // 2:
                lefts = [c for c in lefts if c > 0]
            if lefts:
                swaps.append((step, parity, lefts))
    return swaps


def swap_columns(value, step, lefts, slabs, columns):
    to = {c: c + step for c in lefts} | {c + step: c for c in lefts}
    rows = lax.axis_size("row")
    pairs = []
    for d in range(slabs):
        for r in range(rows):
            for c in range(columns):
                way = 0 if step == 1 else 0
                there = (d, r, to[c]) if c in to else ((d, r ^ 1, c) if way == 0 else (d ^ way, r, c))
                if there[0] < slabs and there[1] < rows:
                    pairs.append(((d * rows + r) * columns + c, (there[0] * rows + there[1]) * columns + there[2]))
    return lax.ppermute(value, ("depth", "row", "col"), pairs)


def covers(targets_ref, view, slab, column, tile):
    first = targets_ref[view, slab, 0, column]
    return (first == tile) | (first + 1 == tile)


def plan_kernel(slabs, columns, plans, targets_ref, offsets_ref, order_ref, *refs):
    outs = refs[1:]
    mine, column = lax.axis_index("depth"), lax.axis_index("col")
    rows, cols = outs[0].shape[3:]
    lane = lax.broadcasted_iota(jnp.int32, (rows, cols), 1)

    def found_before(view, source, tile):
        count, found = jnp.int32(0), []
        for position in range(slabs):
            first = targets_ref[view, order_ref[view, position], 0, source]
            here = (first == tile) | (first + 1 == tile)
            found.append((here, count))
            count = count + here.astype(jnp.int32)
        return found

    for out, (role, step, parity, lefts, slots) in zip(outs, plans, strict=True):
        if role == "take":
            source = column - step
            present = (source >= 0) & (source < columns)
            source = jnp.clip(source, 0, columns - 1)
            for v in range(len(SHEARS)):
                for position, (here, count) in enumerate(found_before(v, source, column)):
                    for slot in range(slots):
                        chosen = (here & present & (count == slot)).astype(jnp.float32)
                        out[v, position, slot] = jnp.full((rows, cols), chosen).astype(out.dtype)
            continue
        tile = column
        if step:
            is_left = lax.rem(lax.div(column, step), 2) == parity
            is_left = is_left & (column >= lefts[0]) & (column + step < columns)
            is_right = (lax.rem(column, 2) != parity) & (column - step >= lefts[0]) & (step == 1)
            tile = jnp.where(is_left, column + step, jnp.where(is_right, column - step, -PAIR))
        for v in range(len(SHEARS)):
            found = found_before(v, column, tile)
            for k in range(slabs):
                slab = origin(mine, k, slabs)
                first, offset = targets_ref[v, slab, 0, column], offsets_ref[v, slab]
                for slot in range(slots):
                    chosen = jnp.int32(0)
                    for position, (here, count) in enumerate(found):
                        fits = (order_ref[v, position] == slab) & (slot == position)
                        if slots < slabs:
                            fits = (order_ref[v, position] == slab) & here & (count == slot)
                        chosen = chosen + fits.astype(jnp.int32)
                    before = (chosen * (first == tile).astype(jnp.int32)).astype(jnp.float32)
                    after = (chosen * (first + 1 == tile).astype(jnp.int32)).astype(jnp.float32)
                    out[v, slot, k] = jnp.where(lane >= offset, before, after).astype(out.dtype)


def piece_plans(targets, offsets, slab_order, after, columns, plans):
    slabs = slab_order.shape[1]
    views, cols = after.shape[0], after.shape[3]
    vmem, smem = pl.BlockSpec(memory_space=pltpu.VMEM), pl.BlockSpec(memory_space=pltpu.SMEM)
    shapes = []
    for role, _, _, _, slots in plans:
        shapes.append((views, slabs, slots) if role == "take" else (views, slots, slabs))
    return pl.pallas_call(
        functools.partial(plan_kernel, slabs, columns, plans),
        in_specs=[smem, smem, smem, vmem],
        out_specs=[vmem] * len(plans),
        out_shape=[pltpu.VMEM(shape + (16, cols), jnp.bfloat16) for shape in shapes],
        compiler_params=pltpu.CompilerParams(vmem_limit_bytes=VMEM_BYTES),
        name="piece_plans",
    )(targets, offsets, slab_order, after)


def pack_kernel(order, outs_count, *refs):
    slabs = len(order)
    blocks = dict(zip(order, refs[:slabs], strict=True))
    masks, outs = refs[slabs : slabs + outs_count], refs[slabs + outs_count :]
    for mask_ref, out in zip(masks, outs, strict=True):
        views, slots, channels, strip, _ = out.shape
        for v in range(views):
            for slot in range(slots):
                for row in range(0, strip, 16):
                    rows = pl.ds(row, 16)
                    parts = [mask_ref[v, slot, k] for k in range(slabs)]
                    for c in range(channels):
                        total = blocks[0][v, c, rows] * parts[0]
                        for k in range(1, slabs):
                            total = total + blocks[k][v, c, rows] * parts[k]
                        out[v, slot, c, rows] = total


def packed_pieces(blocks, masks, order, name):
    slabs = len(blocks)
    views, channels, strip, cols = blocks[0].shape
    vmem = pl.BlockSpec(memory_space=pltpu.VMEM)
    return pl.pallas_call(
        functools.partial(pack_kernel, order, len(masks)),
        in_specs=[vmem] * (slabs + len(masks)),
        out_specs=[vmem] * len(masks),
        out_shape=[
            jax.ShapeDtypeStruct((views, mask.shape[1], channels, strip, cols), jnp.bfloat16) for mask in masks
        ],
        compiler_params=pltpu.CompilerParams(vmem_limit_bytes=VMEM_BYTES),
        name=name,
    )(*[blocks[k] for k in order], *masks)


def compose_views(slabs, sources, frame_ref):
    strip, cols = frame_ref.shape[3:]
    for v in range(len(SHEARS)):
        colour = [jnp.zeros((strip, cols), jnp.float32) for _ in range(3)]
        weight = jnp.ones((strip, cols), jnp.float32)
        for position in range(slabs):
            for pieces, first, masks in sources:
                slots = pieces[0].shape[1]
                values = []
                for c in range(4):
                    refs = []
                    for ref in pieces:
                        if masks is None:
                            refs.append(ref[v, position, c])
                            continue
                        rows = []
                        for row in range(0, strip, 16):
                            total = ref[v, 0, c, pl.ds(row, 16)] * masks[v, position, 0]
                            for slot in range(1, slots):
                                total = total + ref[v, slot, c, pl.ds(row, 16)] * masks[v, position, slot]
                            rows.append(total)
                        refs.append(jnp.concatenate(rows, axis=0))
                    value = refs[0] if len(refs) == 1 else jnp.where(first, refs[0], refs[1])
                    values.append(value.astype(jnp.float32))
                for c in range(3):
                    colour[c] = colour[c] + weight * values[c]
                weight = weight * (1.0 - values[3])
        for c in range(3):
            frame_ref[v, c, 0] = colour[c]
        frame_ref[v, 3, 0] = 1.0 - weight


def frame_kernel(slabs, swaps, takes, *refs):
    taken, own_ref = dict(zip(takes, refs[: len(takes)], strict=True)), refs[len(takes)]
    received, frame_ref = refs[len(takes) + 1 : -1], refs[-1]
    tile = lax.axis_index("col")
    by_step = {}
    for ref, (step, parity, _) in zip(received, swaps, strict=True):
        by_step.setdefault(step, {})[parity] = ref
    for phase in range(2):
        sources = []
        for step in range(slabs // 2, -2, -1):
            if step == 0:
                sources.append(([own_ref], None, taken.get(step)))
                continue
            refs_here = by_step.get(abs(step), {})
            if abs(step) == 1:
                parity = (phase - step) % 2 if step > 0 else phase
                refs_here = {q: ref for q, ref in refs_here.items() if q == parity}
            if refs_here:
                first = lax.rem(lax.div(tile + step, abs(step)), 2) == 0
                sources.append(([refs_here[q] for q in sorted(refs_here)], first, taken.get(step)))
        pl.when(lax.rem(tile, 2) == phase)(functools.partial(compose_views, slabs, sources, frame_ref))


def composed_frame(own, received, masks, slabs, swaps):
    views, _, channels, strip, cols = own.shape
    vmem = pl.BlockSpec(memory_space=pltpu.VMEM)
    return pl.pallas_call(
        functools.partial(frame_kernel, slabs, swaps, list(masks)),
        in_specs=[vmem] * (len(masks) + 1 + len(received)),
        out_specs=vmem,
        out_shape=jax.ShapeDtypeStruct((views, channels, 1, strip, cols), jnp.float32),
        compiler_params=pltpu.CompilerParams(vmem_limit_bytes=VMEM_BYTES),
        name="compose_frame",
    )(*masks.values(), own, *received)


def on_device(density, albedo, targets, offsets, slab_order):
    depth_cells = density.shape[0]
    slabs, columns = lax.axis_size("depth"), lax.axis_size("col")
    offsets = offsets[:, :, 0, 0]
    code, density = slab_code(density)
    codes = [code] + [swap_depth(code, k, slabs) for k in range(1, slabs)]
    sums, opac = image_sums(density, albedo)
    strips = lit_strips(codes, sums, opac, offsets, depth_cells)
    blocks = [strips[0]] + [swap_depth(strips[k], k, slabs) for k in range(1, slabs)]
    swaps = column_swaps(slabs, columns)
    kept_slots = min(slabs, 2 * PAIR)
    plans = [("send", *swap, piece_slots(swap[0], slabs)) for swap in swaps]
    plans.append(("keep", 0, 0, [], kept_slots))
    takes = []
    for step in [*sorted({step for step, _, _ in swaps}), 0, -1]:
        slots = kept_slots if step == 0 else piece_slots(abs(step), slabs)
        if slots < slabs:
            takes.append(step)
            plans.append(("take", step, 0, [], slots))
    masks = piece_plans(targets, offsets, slab_order, strips[0], columns, plans)
    order = [0, *range(slabs - 1, 0, -1)]
    outgoing = packed_pieces(blocks, masks[: len(swaps)], order, "pack_sent")
    (own,) = packed_pieces(blocks, masks[len(swaps) : len(swaps) + 1], order, "pack_kept")
    received = [
        swap_columns(value, step, lefts, slabs, columns)
        for value, (step, _, lefts) in zip(outgoing, swaps, strict=True)
    ]
    return composed_frame(own, received, dict(zip(takes, masks[len(swaps) + 1 :], strict=True)), slabs, swaps)


def solution(mesh):
    in_specs = (
        P("depth", "row", "col"),
        P(None, "depth", "row", "col"),
        P(None, None, "row", None),
        P(None, None, "row", "col"),
        P(),
    )
    out_specs = P(None, None, "row", "depth", "col")
    return jax.shard_map(
        on_device, mesh=mesh, in_specs=in_specs, out_specs=out_specs, check_vma=False
    )
```

time: 35.4 us -> 28.9 us (0.82)
  the two profiles are of different devices: /device:TPU:0 before, /device:TPU:8 now
where the time goes in v2:
time: 28.9 us; the launch traced here: 28.8 us
  starting transfers between devices  10.3 us (36%)
  waiting for transfers between devices  9.36 us (32%)
  Pallas kernels  9 us (31%)
    ppermute x6, starting transfers between devices, swap_depth(): lax.ppermute(value, 'depth', [(i, int(partner(i, k, count)) if count & co...  7.11 us
    ppermute x3, waiting for transfers between devices, swap_columns(): return lax.ppermute(value, ('depth', 'row', 'col'), pairs)  6.78 us
    pallas_call x1, Pallas kernels, image_sums(): pl.pallas_call(functools.partial(sums_kernel, chunk, parts), in_specs=[vm...  3.84 us
    ppermute x3, starting transfers between devices, swap_columns(): return lax.ppermute(value, ('depth', 'row', 'col'), pairs)  3.22 us
    ppermute x6, waiting for transfers between devices, swap_depth(): lax.ppermute(value, 'depth', [(i, int(partner(i, k, count)) if count & co...  2.59 us
    pallas_call x1, Pallas kernels, lit_strips(): pl.pallas_call(functools.partial(lit_kernel, slabs, depth_cells), in_spec...  1.34 us
    pallas_call x1, Pallas kernels, slab_code(): pl.pallas_call(functools.partial(plane_kernel, parts), in_specs=[pl.Block...  1.27 us
    pallas_call x1, Pallas kernels, piece_plans(): pl.pallas_call(functools.partial(plan_kernel, slabs, columns, plans), in_...  1.13 us
  transfers between devices with their start and end apart: 9, of which 4 were waited for; matrix products, arithmetic and copies ran while one was open for 0% of the time, Pallas kernels for 18%

profile of v2, /device:TPU:8, one launch (start us, length us, event | category | flops | bytes accessed | tf_op | source)
XLA Modules:
  0.0 28.8 jit_solution(8044900933316682288)
XLA Ops:
  0.0 0.0 copy-start
  0.0 1.3 %slab_code.1 = (bf16[128,128]{1,0:T(8,128)(2,1)S(1)}, f32[16,128,128]{2,1,0:T(8,128)S(1)}) custom-call(f32[16,128,128]{2,1,0:T(8,128)} %density_hbm.1), custom_call_target="tpu_custom_call" | custom-call | tf_op jit(solution)/shard_map/slab_code/pallas_call | solution.py:68
  1.3 2.5 %collective-permute-start.2 = (bf16[128,128]{1,0:T(8,128)(2,1)S(1)}, bf16[128,128]{1,0:T(8,128)(2,1)S(1)}, u32[]{:S(2)}, u32[]{:S(2)}) collective-permute-start(bf16[128,128]{1,0:T(8,128)(2,1)S(1)} %get-tuple-element.21.refs_0_), channel_id=1, source_target_pairs={{0,24},{8,16},{16,8},{24,0},{1,25},{9,17},{17,9},{25,1},{2,26},{10... | collective-permute-start | bytes 98312 | tf_op jit(solution)/shard_map/ppermute | solution.py:184
  3.8 0.5 %collective-permute-start.1 = (bf16[128,128]{1,0:T(8,128)(2,1)S(1)}, bf16[128,128]{1,0:T(8,128)(2,1)S(1)}, u32[]{:S(2)}, u32[]{:S(2)}) collective-permute-start(bf16[128,128]{1,0:T(8,128)(2,1)S(1)} %get-tuple-element.21.refs_0_), channel_id=1, source_target_pairs={{0,16},{8,24},{16,0},{24,8},{1,17},{9,25},{17,1},{25,9},{2,18},{10... | collective-permute-start | bytes 98312 | tf_op jit(solution)/shard_map/ppermute | solution.py:184
  4.3 0.5 %collective-permute-start = (bf16[128,128]{1,0:T(8,128)(2,1)S(1)}, bf16[128,128]{1,0:T(8,128)(2,1)S(1)}, u32[]{:S(2)}, u32[]{:S(2)}) collective-permute-start(bf16[128,128]{1,0:T(8,128)(2,1)S(1)} %get-tuple-element.21.refs_0_), channel_id=1, source_target_pairs={{0,8},{8,0},{16,24},{24,16},{1,9},{9,1},{17,25},{25,17},{2,10},{10... | collective-permute-start | bytes 98312 | tf_op jit(solution)/shard_map/ppermute | solution.py:184
  4.8 0.0 copy-start.1
  4.8 0.0 copy-start.2
  4.8 3.8 %image_sums.1 = (f32[42,128,128]{2,1,0:T(8,128)S(1)}, f32[2,128,128]{2,1,0:T(8,128)S(1)}) custom-call(f32[16,128,128]{2,1,0:T(8,128)S(1)} %get-tuple-element.22.density_ref, bf16[3,16,128,128]{3,2,1,0:T(8,128)(2,1)} %albedo_hbm.1), custom_call_target="tpu_custom_call" | custom-call | flops 15728640 | bytes 5373952 | tf_op jit(solution)/shard_map/image_sums/pallas_call | solution.py:158
  8.7 0.0 collective-permute-done.2.refs_3_
  8.7 0.0 collective-permute-done.1.refs_2_
  8.7 0.0 collective-permute-done.refs_1_
  8.7 0.0 copy-done
  8.7 1.3 %lit_strips.1 = (bf16[2,4,32,128]{3,2,1,0:T(8,128)(2,1)S(1)}, bf16[2,4,32,128]{3,2,1,0:T(8,128)(2,1)S(1)}, bf16[2,4,32,128]{3,2,1,0:T(8,128)(2,1)S(1)}, bf16[2,4,32,128]{3,2,1,0:T(8,128)(2,1)S(1)}) custom-call(s32[2,4]{1,0:T(2,128)S(1)} %bitcast.1, bf16[128,128]{1,0:T(8,128)(2,1)S(1)} %get-tuple-element.21.refs_0_, ...), custom_call_target="tpu_custom_call" | custom-call | tf_op jit(solution)/shard_map/lit_strips/pallas_call | solution.py:228
  10.1 2.5 %collective-permute-start.3 = (bf16[2,4,32,128]{3,2,1,0:T(8,128)(2,1)S(1)}, bf16[2,4,32,128]{3,2,1,0:T(8,128)(2,1)S(1)}, u32[]{:S(2)}, u32[]{:S(2)}) collective-permute-start(bf16[2,4,32,128]{3,2,1,0:T(8,128)(2,1)S(1)} %get-tuple-element.27), channel_id=1, source_target_pairs={{0,24},{8,16},{16,8},{24,0},{1,25},{9,17},{17,9},{25,1},{2,26},{10... | collective-permute-start | bytes 196616 | tf_op jit(solution)/shard_map/ppermute | solution.py:184
  12.6 0.5 %collective-permute-start.4 = (bf16[2,4,32,128]{3,2,1,0:T(8,128)(2,1)S(1)}, bf16[2,4,32,128]{3,2,1,0:T(8,128)(2,1)S(1)}, u32[]{:S(2)}, u32[]{:S(2)}) collective-permute-start(bf16[2,4,32,128]{3,2,1,0:T(8,128)(2,1)S(1)} %get-tuple-element.28), channel_id=1, source_target_pairs={{0,16},{8,24},{16,0},{24,8},{1,17},{9,25},{17,1},{25,9},{2,18},{10... | collective-permute-start | bytes 196616 | tf_op jit(solution)/shard_map/ppermute | solution.py:184
  13.1 0.5 %collective-permute-start.5 = (bf16[2,4,32,128]{3,2,1,0:T(8,128)(2,1)S(1)}, bf16[2,4,32,128]{3,2,1,0:T(8,128)(2,1)S(1)}, u32[]{:S(2)}, u32[]{:S(2)}) collective-permute-start(bf16[2,4,32,128]{3,2,1,0:T(8,128)(2,1)S(1)} %get-tuple-element.29), channel_id=1, source_target_pairs={{0,8},{8,0},{16,24},{24,16},{1,9},{9,1},{17,25},{25,17},{2,10},{10... | collective-permute-start | bytes 196616 | tf_op jit(solution)/shard_map/ppermute | solution.py:184
  13.6 0.0 copy-done.1
  13.6 0.0 copy-done.2
  13.6 1.1 %piece_plans.1 = (bf16[2,4,4,16,128]{4,3,2,1,0:T(8,128)(2,1)S(1)}, bf16[2,4,4,16,128]{4,3,2,1,0:T(8,128)(2,1)S(1)}, bf16[2,2,4,16,128]{4,3,2,1,0:T(8,128)(2,1)S(...) custom-call(s32[2,4,1,4]{3,2,1,0:T(1,128)S(1)} %copy-done.1, s32[2,4]{1,0:T(2,128)S(1)} %bitcast.2, ...), custom_call_target="tpu_custom_call" | custom-call | tf_op jit(solution)/shard_map/piece_plans/pallas_call | solution.py:334
  14.8 0.8 %collective-permute-done.3.refs_1_ = bf16[2,4,32,128]{3,2,1,0:T(8,128)(2,1)S(1)} collective-permute-done((bf16[2,4,32,128]{3,2,1,0:T(8,128)(2,1)S(1)}, bf16[2,4,32,128]{3,2,1,0:T(8,128)(2,1)S(1)}, u32[]{:S(2)}, u32[]{:S(2)}) %collective-permute-start.3) | collective-permute-done | bytes 65568 | tf_op jit(solution)/shard_map/ppermute | solution.py:184
  15.6 1.2 %collective-permute-done.4.refs_2_ = bf16[2,4,32,128]{3,2,1,0:T(8,128)(2,1)S(1)} collective-permute-done((bf16[2,4,32,128]{3,2,1,0:T(8,128)(2,1)S(1)}, bf16[2,4,32,128]{3,2,1,0:T(8,128)(2,1)S(1)}, u32[]{:S(2)}, u32[]{:S(2)}) %collective-permute-start.4) | collective-permute-done | bytes 65568 | tf_op jit(solution)/shard_map/ppermute | solution.py:184
  16.8 0.5 %collective-permute-done.5.refs_3_ = bf16[2,4,32,128]{3,2,1,0:T(8,128)(2,1)S(1)} collective-permute-done((bf16[2,4,32,128]{3,2,1,0:T(8,128)(2,1)S(1)}, bf16[2,4,32,128]{3,2,1,0:T(8,128)(2,1)S(1)}, u32[]{:S(2)}, u32[]{:S(2)}) %collective-permute-start.5) | collective-permute-done | bytes 65568 | tf_op jit(solution)/shard_map/ppermute | solution.py:184
  17.4 0.3 %pack_sent.1 = (bf16[2,4,4,32,128]{4,3,2,1,0:T(8,128)(2,1)S(1)}, bf16[2,4,4,32,128]{4,3,2,1,0:T(8,128)(2,1)S(1)}, bf16[2,2,4,32,128]{4,3,2,1,0:T(8,128)(2,1)S(1)}) custom-call(bf16[2,4,32,128]{3,2,1,0:T(8,128)(2,1)S(1)} %get-tuple-element.25.refs_0_, bf16[2,4,32,128]{3,2,1,0:T(8,128)(2,1)S(1)} %collective-permute-done.3.refs_1_, ...), custom_call_target="tpu_custom_call" | custom-call | tf_op jit(solution)/shard_map/pack_sent/pallas_call | solution.py:366
  17.7 0.5 %collective-permute-start.6 = (bf16[2,4,4,32,128]{4,3,2,1,0:T(8,128)(2,1)S(1)}, bf16[2,4,4,32,128]{4,3,2,1,0:T(8,128)(2,1)S(1)}, u32[]{:S(2)}, u32[]{:S(2)}) collective-permute-start(bf16[2,4,4,32,128]{4,3,2,1,0:T(8,128)(2,1)S(1)} %get-tuple-element.34), channel_id=1, source_target_pairs={{0,1},{1,0},{2,3},{3,2},{4,5},{5,4},{6,7},{7,6},{8,9},{9,8},{10,11... | collective-permute-start | bytes 786440 | tf_op jit(solution)/shard_map/ppermute | solution.py:270
  18.2 2.7 %collective-permute-start.7 = (bf16[2,4,4,32,128]{4,3,2,1,0:T(8,128)(2,1)S(1)}, bf16[2,4,4,32,128]{4,3,2,1,0:T(8,128)(2,1)S(1)}, u32[]{:S(2)}, u32[]{:S(2)}) collective-permute-start(bf16[2,4,4,32,128]{4,3,2,1,0:T(8,128)(2,1)S(1)} %get-tuple-element.35), channel_id=1, source_target_pairs={{0,4},{1,2},{2,1},{3,7},{4,0},{5,6},{6,5},{7,3},{8,12},{9,10},{10,... | collective-permute-start | bytes 786440 | tf_op jit(solution)/shard_map/ppermute | solution.py:270
  20.9 0.0 collective-permute-start.8
  20.9 0.1 pack_kept.1.refs_1_
  21.1 6.8 %collective-permute-done.8.refs_4_ = bf16[2,2,4,32,128]{4,3,2,1,0:T(8,128)(2,1)S(1)} collective-permute-done((bf16[2,2,4,32,128]{4,3,2,1,0:T(8,128)(2,1)S(1)}, bf16[2,2,4,32,128]{4,3,2,1,0:T(8,128)(2,1)S(1)}, u32[]{:S(2)}, u32[]{:S(2)}) %collective-permute-start.8) | collective-permute-done | bytes 131104 | tf_op jit(solution)/shard_map/ppermute | solution.py:270
  27.8 0.0 collective-permute-done.6.refs_2_
  27.8 0.0 collective-permute-done.7.refs_3_
  27.9 0.9 %compose_frame.1 = f32[2,4,1,32,128]{4,3,2,1,0:T(8,128)} custom-call(bf16[2,4,2,16,128]{4,3,2,1,0:T(8,128)(2,1)S(1)} %get-tuple-element.26.refs_0_, bf16[2,4,4,32,128]{4,3,2,1,0:T(8,128)(2,1)S(1)} %pack_kept.1.refs_1_, bf16[2,4,4,32,128]{4,3,2,1,0:T(8,128)(2,1)S(1)} %collective-permute-done.6.refs_2_, ...), custom_call_target="tpu_custom_call" | custom-call | tf_op jit(solution)/shard_map/compose_frame/pallas_call | solution.py:436
Async XLA Ops:
  0.0 8.7 %copy-start = (s32[2,4,1,1]{1,3,2,0:T(1,128)S(1)}, s32[2,4,1,1]{1,3,2,0:T(1,128)}, u32[]{:S(2)}) copy-start(s32[2,4,1,1]{1,3,2,0:T(1,128)} %param.8) | copy-start | bytes 100
  1.3 7.4 %collective-permute-start.2 = (bf16[128,128]{1,0:T(8,128)(2,1)S(1)}, bf16[128,128]{1,0:T(8,128)(2,1)S(1)}, u32[]{:S(2)}, u32[]{:S(2)}) collective-permute-start(bf16[128,128]{1,0:T(8,128)(2,1)S(1)} %get-tuple-element.21.refs_0_), channel_id=1, source_target_pairs={{0,24},{8,16},{16,8},{24,0},{1,25},{9,17},{17,9},{25,1},{2,26},{10... | collective-permute-start | bytes 98312 | tf_op jit(solution)/shard_map/ppermute | solution.py:184
  3.8 4.9 %collective-permute-start.1 = (bf16[128,128]{1,0:T(8,128)(2,1)S(1)}, bf16[128,128]{1,0:T(8,128)(2,1)S(1)}, u32[]{:S(2)}, u32[]{:S(2)}) collective-permute-start(bf16[128,128]{1,0:T(8,128)(2,1)S(1)} %get-tuple-element.21.refs_0_), channel_id=1, source_target_pairs={{0,16},{8,24},{16,0},{24,8},{1,17},{9,25},{17,1},{25,9},{2,18},{10... | collective-permute-start | bytes 98312 | tf_op jit(solution)/shard_map/ppermute | solution.py:184
  4.3 4.4 %collective-permute-start = (bf16[128,128]{1,0:T(8,128)(2,1)S(1)}, bf16[128,128]{1,0:T(8,128)(2,1)S(1)}, u32[]{:S(2)}, u32[]{:S(2)}) collective-permute-start(bf16[128,128]{1,0:T(8,128)(2,1)S(1)} %get-tuple-element.21.refs_0_), channel_id=1, source_target_pairs={{0,8},{8,0},{16,24},{24,16},{1,9},{9,1},{17,25},{25,17},{2,10},{10... | collective-permute-start | bytes 98312 | tf_op jit(solution)/shard_map/ppermute | solution.py:184
  4.8 8.8 %copy-start.1 = (s32[2,4,1,4]{3,2,1,0:T(1,128)S(1)}, s32[2,4,1,4]{3,2,1,0:T(1,128)}, u32[]{:S(2)}) copy-start(s32[2,4,1,4]{3,2,1,0:T(1,128)} %targets_ref.1) | copy-start | bytes 388
  4.8 8.8 %copy-start.2 = (s32[2,4]{1,0:T(2,128)S(1)}, s32[2,4]{1,0:T(2,128)}, u32[]{:S(2)}) copy-start(s32[2,4]{1,0:T(2,128)} %order_ref.1) | copy-start | bytes 100
  10.1 5.5 %collective-permute-start.3 = (bf16[2,4,32,128]{3,2,1,0:T(8,128)(2,1)S(1)}, bf16[2,4,32,128]{3,2,1,0:T(8,128)(2,1)S(1)}, u32[]{:S(2)}, u32[]{:S(2)}) collective-permute-start(bf16[2,4,32,128]{3,2,1,0:T(8,128)(2,1)S(1)} %get-tuple-element.27), channel_id=1, source_target_pairs={{0,24},{8,16},{16,8},{24,0},{1,25},{9,17},{17,9},{25,1},{2,26},{10... | collective-permute-start | bytes 196616 | tf_op jit(solution)/shard_map/ppermute | solution.py:184
  12.6 4.3 %collective-permute-start.4 = (bf16[2,4,32,128]{3,2,1,0:T(8,128)(2,1)S(1)}, bf16[2,4,32,128]{3,2,1,0:T(8,128)(2,1)S(1)}, u32[]{:S(2)}, u32[]{:S(2)}) collective-permute-start(bf16[2,4,32,128]{3,2,1,0:T(8,128)(2,1)S(1)} %get-tuple-element.28), channel_id=1, source_target_pairs={{0,16},{8,24},{16,0},{24,8},{1,17},{9,25},{17,1},{25,9},{2,18},{10... | collective-permute-start | bytes 196616 | tf_op jit(solution)/shard_map/ppermute | solution.py:184
  13.1 4.3 %collective-permute-start.5 = (bf16[2,4,32,128]{3,2,1,0:T(8,128)(2,1)S(1)}, bf16[2,4,32,128]{3,2,1,0:T(8,128)(2,1)S(1)}, u32[]{:S(2)}, u32[]{:S(2)}) collective-permute-start(bf16[2,4,32,128]{3,2,1,0:T(8,128)(2,1)S(1)} %get-tuple-element.29), channel_id=1, source_target_pairs={{0,8},{8,0},{16,24},{24,16},{1,9},{9,1},{17,25},{25,17},{2,10},{10... | collective-permute-start | bytes 196616 | tf_op jit(solution)/shard_map/ppermute | solution.py:184
  17.7 10.1 %collective-permute-start.6 = (bf16[2,4,4,32,128]{4,3,2,1,0:T(8,128)(2,1)S(1)}, bf16[2,4,4,32,128]{4,3,2,1,0:T(8,128)(2,1)S(1)}, u32[]{:S(2)}, u32[]{:S(2)}) collective-permute-start(bf16[2,4,4,32,128]{4,3,2,1,0:T(8,128)(2,1)S(1)} %get-tuple-element.34), channel_id=1, source_target_pairs={{0,1},{1,0},{2,3},{3,2},{4,5},{5,4},{6,7},{7,6},{8,9},{9,8},{10,11... | collective-permute-start | bytes 786440 | tf_op jit(solution)/shard_map/ppermute | solution.py:270
  18.2 9.6 %collective-permute-start.7 = (bf16[2,4,4,32,128]{4,3,2,1,0:T(8,128)(2,1)S(1)}, bf16[2,4,4,32,128]{4,3,2,1,0:T(8,128)(2,1)S(1)}, u32[]{:S(2)}, u32[]{:S(2)}) collective-permute-start(bf16[2,4,4,32,128]{4,3,2,1,0:T(8,128)(2,1)S(1)} %get-tuple-element.35), channel_id=1, source_target_pairs={{0,4},{1,2},{2,1},{3,7},{4,0},{5,6},{6,5},{7,3},{8,12},{9,10},{10,... | collective-permute-start | bytes 786440 | tf_op jit(solution)/shard_map/ppermute | solution.py:270
  20.9 6.9 %collective-permute-start.8 = (bf16[2,2,4,32,128]{4,3,2,1,0:T(8,128)(2,1)S(1)}, bf16[2,2,4,32,128]{4,3,2,1,0:T(8,128)(2,1)S(1)}, u32[]{:S(2)}, u32[]{:S(2)}) collective-permute-start(bf16[2,2,4,32,128]{4,3,2,1,0:T(8,128)(2,1)S(1)} %get-tuple-element.36), channel_id=1, source_target_pairs={{0,4},{1,3},{2,6},{3,1},{4,0},{5,7},{6,2},{7,5},{8,12},{9,11},{10,... | collective-permute-start | bytes 393224 | tf_op jit(solution)/shard_map/ppermute | solution.py:270

commit v3 on v2

--- a/solution.py
+++ b/solution.py
@@ -87,83 +87,114 @@
     return (jnp.where(inside, 1.0 - f, 0.0), jnp.where(inside | (lane == 0), f, 0.0))
 
 
-def sums_chunk(density_ref, albedo_ref, sums_ref, opac_ref, rows):
-    depth_cells = density_ref.shape[0]
-    cols = density_ref.shape[2]
-    index = {key: i for i, key in enumerate(shift_list(depth_cells))}
-    shape = (rows.size, cols)
-    lane = lax.broadcasted_iota(jnp.int32, shape, 1)
+def share_list(depth_cells):
+    found = []
+    for v, shear in enumerate(SHEARS):
+        for z, (k, f) in enumerate(plane_steps(shear, depth_cells)):
+            found += [(v, z, j, share) for j, share in ((k, 1.0 - f), (k + 1, f)) if share > 0.0]
+    return found
+
+
+def weigh_rows(density_ref, weights_ref, opac_ref, rows):
+    depth_cells, _, cols = density_ref.shape
+    tiled = (rows.size // 8, 8, cols)
+    lane = lax.broadcasted_iota(jnp.int32, (8, cols), 1)
+    shares = share_list(depth_cells)
     steps = [plane_steps(s, depth_cells) for s in SHEARS]
-    transmit = [jnp.ones(shape, jnp.float32) for _ in SHEARS]
-    sums = [{} for _ in SHEARS]
-    light = jnp.full(shape, BRIGHTNESS, jnp.float32)
+    transmit = [jnp.ones(tiled, jnp.float32) for _ in SHEARS]
+    frame = [0 for _ in SHEARS]
+    light = jnp.full(tiled, BRIGHTNESS, jnp.float32)
     for z in range(depth_cells):
-        kept = jnp.exp(-density_ref[z, rows])
+        kept = jnp.exp(-density_ref[z, rows].reshape(tiled))
         opacity = 1.0 - kept
         lit = light * opacity
         light = light * kept
         farther = rolled(opacity, 1)
-        colour = [albedo_ref[c, z, rows].astype(jnp.float32) for c in range(3)]
         for v in range(len(SHEARS)):
             k, f = steps[v][z]
-            for j, share in ((k, 1.0 - f), (k + 1, f)):
-                if share == 0.0:
+            transmit[v] = rolled(transmit[v], frame[v] - k)
+            frame[v] = k
+            for i, (view, plane, j, share) in enumerate(shares):
+                if (view, plane) == (v, z):
+                    here = transmit[v] if j == k else rolled(transmit[v], -1)
+                    weights_ref[i, rows] = (here * (lit * share)).reshape(rows.size, cols)
+            a, b = opacity_weights(k, f, lane, cols)
+            moved = a[None] * opacity if f == 0.0 else a[None] * opacity + b[None] * farther
+            transmit[v] = transmit[v] * (1.0 - moved)
+    for v in range(len(SHEARS)):
+        opac_ref[v, rows] = (1.0 - rolled(transmit[v], frame[v])).reshape(rows.size, cols).astype(opac_ref.dtype)
+
+
+def sum_rows(albedo_ref, weights_ref, sums_ref, rows):
+    _, depth_cells, _, cols = albedo_ref.shape
+    lane = lax.broadcasted_iota(jnp.int32, (8, cols), 1)
+    shares = share_list(depth_cells)
+    index = {key: i for i, key in enumerate(shift_list(depth_cells))}
+    last = {(v, j): z for v, z, j, _ in shares}
+    sums = {}
+    for z in range(depth_cells):
+        colour = [albedo_ref[c, z, rows].astype(jnp.float32) for c in range(3)]
+        for i, (v, plane, j, _) in enumerate(shares):
+            if plane != z:
+                continue
+            weight = weights_ref[i, rows]
+            for c in range(3):
+                term = weight * colour[c]
+                total = sums.pop((v, j, c)) + term if (v, j, c) in sums else term
+                if last[v, j] > z:
+                    sums[v, j, c] = total
                     continue
-                weight = rolled(transmit[v], -j) * (lit * share)
-                for c in range(3):
-                    term = weight * colour[c]
-                    sums[v][j, c] = sums[v][j, c] + term if (j, c) in sums[v] else term
-            a, b = opacity_weights(k, f, lane, cols)
-            moved = a * opacity if f == 0.0 else a * opacity + b * farther
-            transmit[v] = transmit[v] * (1.0 - rolled(moved, k))
-            following = (steps[v][z + 1][0], steps[v][z + 1][0] + 1) if z + 1 < depth_cells else ()
-            for j, c in list(sums[v]):
-                if j not in following:
-                    total = sums[v].pop((j, c))
-                    if j:
-                        total = jnp.where(lane < cols - j if j > 0 else lane >= -j, total, 0.0)
-                    sums_ref[index[v, j] * 3 + c, rows] = total
-    for v in range(len(SHEARS)):
-        opac_ref[v, rows] = 1.0 - transmit[v]
-
-
-def sums_kernel(chunk, parts, density_ref, albedo_hbm, sums_ref, opac_ref, albedo_ref, sems):
-    rows = density_ref.shape[1]
-    block = rows // parts
+                if j:
+                    inside = lane < cols - j if j > 0 else lane >= -j
+                    total = jnp.where(inside[None], total.reshape(-1, 8, cols), 0.0).reshape(total.shape)
+                sums_ref[index[v, j] * 3 + c, rows] = total
+
+
+def sums_kernel(
+    chunk, block, density_ref, albedo_hbm, sums_ref, opac_ref, weights_ref, albedo_ref, sems
+):
+    count = density_ref.shape[1]
+    parts = sems.shape[0]
 
     def copy(i):
-        part = pl.ds(pl.multiple_of(i * block, block), block)
+        part = pl.ds(i * (count // parts), count // parts)
         return pltpu.make_async_copy(albedo_hbm.at[:, :, part], albedo_ref.at[:, :, part], sems.at[i])
 
     for i in range(parts):
         copy(i).start()
 
-    def body(i, carry):
+    def weigh(i, carry):
+        weigh_rows(density_ref, weights_ref, opac_ref, pl.ds(pl.multiple_of(i * block, block), block))
+        return carry
+
+    def add(i, carry):
+        sum_rows(albedo_ref, weights_ref, sums_ref, pl.ds(pl.multiple_of(i * chunk, chunk), chunk))
+        return carry
+
+    lax.fori_loop(0, count // block, weigh, 0)
+    for i in range(parts):
         copy(i).wait()
-        for part in range(block // chunk):
-            at = pl.ds(pl.multiple_of(i * block + part * chunk, chunk), chunk)
-            sums_chunk(density_ref, albedo_ref, sums_ref, opac_ref, at)
-        return carry
-
-    lax.fori_loop(0, parts, body, 0)
+    lax.fori_loop(0, count // chunk, add, 0)
 
 
 def image_sums(density, albedo):
     depth_cells, rows, cols = density.shape
     count = 3 * len(shift_list(depth_cells))
-    chunk = 16
-    parts = rows // chunk
     cells = depth_cells * rows * cols
     vmem = pl.BlockSpec(memory_space=pltpu.VMEM)
     return pl.pallas_call(
-        functools.partial(sums_kernel, chunk, parts),
+        functools.partial(sums_kernel, 16, min(rows, 128)),
         in_specs=[vmem, pl.BlockSpec(memory_space=pl.ANY)],
         out_specs=[vmem, vmem],
         out_shape=[
             pltpu.VMEM((count, rows, cols), jnp.float32),
-            pltpu.VMEM((len(SHEARS), rows, cols), jnp.float32),
+            pltpu.VMEM((len(SHEARS), rows, cols), jnp.bfloat16),
         ],
-        scratch_shapes=[pltpu.VMEM(albedo.shape, albedo.dtype), pltpu.SemaphoreType.DMA((parts,))],
+        scratch_shapes=[
+            pltpu.VMEM((len(share_list(depth_cells)), rows, cols), jnp.float32),
+            pltpu.VMEM(albedo.shape, albedo.dtype),
+            pltpu.SemaphoreType.DMA((max(1, rows // 32),)),
+        ],
         compiler_params=pltpu.CompilerParams(vmem_limit_bytes=VMEM_BYTES),
         cost_estimate=pl.CostEstimate(
             flops=60 * cells, bytes_accessed=10 * cells + 4 * count * rows * cols, transcendentals=cells
@@ -184,15 +215,24 @@
     return lax.ppermute(value, "depth", [(i, int(partner(i, k, count)) if count & (count - 1) == 0 else (i + k) % count) for i in range(count)])
 
 
-def lit_kernel(slabs, depth_cells, offsets_any, *refs):
-    codes, (sums_ref, opac_ref) = refs[:slabs], refs[slabs : slabs + 2]
-    outs, (plain_ref, offsets_ref, sem) = refs[slabs + 2 : -3], refs[-3:]
-    fetch = pltpu.make_async_copy(offsets_any, offsets_ref, sem)
-    fetch.start()
+def turn_matrix(offsets, view, slab, cols):
+    lane = lax.broadcasted_iota(jnp.int32, offsets.shape, 1)
+    row = lax.broadcasted_iota(jnp.int32, offsets.shape, 0)
+    own = jnp.where((lane == slab) & (row == view), offsets, 0).astype(jnp.float32)
+    offset = jnp.sum(jnp.sum(own, axis=1, keepdims=True), axis=0, keepdims=True).astype(jnp.int32)
+    moved = lax.broadcasted_iota(jnp.int32, (cols, cols), 0) + offset
+    moved = jnp.where(moved >= cols, moved - cols, moved)
+    landing = lax.broadcasted_iota(jnp.int32, (cols, cols), 1)
+    return (moved == landing).astype(jnp.float32).astype(jnp.bfloat16)
+
+
+def lit_kernel(slabs, depth_cells, offsets_ref, *refs):
+    codes, (sums_ref, opac_ref), outs = refs[:slabs], refs[slabs : slabs + 2], refs[slabs + 2 :]
     mine = lax.axis_index("depth")
     strip, cols = outs[0].shape[2:]
     keys = shift_list(depth_cells)
     middle, spread = depth_code(depth_cells)
+    turns = [turn_matrix(offsets_ref[...], v, mine, cols) for v in range(len(SHEARS))]
     for k in range(slabs):
         rows = pl.ds(pl.multiple_of(partner(mine, k, slabs) * strip, strip), strip)
         ahead_depth = jnp.zeros((strip, cols), jnp.float32)
@@ -202,6 +242,7 @@
             ahead_depth = ahead_depth + jnp.where(ahead, depth, 0.0)
         incoming = jnp.exp(-ahead_depth)
         for v in range(len(SHEARS)):
+            image = []
             for c in range(3):
                 total = None
                 for i, (view, j) in enumerate(keys):
@@ -209,15 +250,10 @@
                         continue
                     moved = rolled(incoming * sums_ref[i * 3 + c, rows], j)
                     total = moved if total is None else total + moved
-                plain_ref[k, v, c] = total
-    fetch.wait()
-    for v in range(len(SHEARS)):
-        turn = offsets_ref[v, mine]
-        for k in range(slabs):
-            rows = pl.ds(pl.multiple_of(partner(mine, k, slabs) * strip, strip), strip)
-            for c in range(3):
-                outs[k][v, c] = pltpu.roll(plain_ref[k, v, c], turn, 1).astype(jnp.bfloat16)
-            outs[k][v, 3] = pltpu.roll(opac_ref[v, rows], turn, 1).astype(jnp.bfloat16)
+                image.append(total.astype(jnp.bfloat16))
+            image = jnp.concatenate([*image, opac_ref[v, rows]], axis=0)
+            turned = jnp.dot(image, turns[v], preferred_element_type=jnp.float32)
+            outs[k][v] = turned.astype(jnp.bfloat16).reshape(4, strip, cols)
 
 
 def lit_strips(codes, sums, opac, offsets, depth_cells):
@@ -227,14 +263,9 @@
     vmem = pl.BlockSpec(memory_space=pltpu.VMEM)
     return pl.pallas_call(
         functools.partial(lit_kernel, slabs, depth_cells),
-        in_specs=[pl.BlockSpec(memory_space=pl.ANY)] + [vmem] * (slabs + 2),
+        in_specs=[vmem] * (slabs + 3),
         out_specs=[vmem] * slabs,
         out_shape=[jax.ShapeDtypeStruct((len(SHEARS), 4, strip, cols), jnp.bfloat16)] * slabs,
-        scratch_shapes=[
-            pltpu.VMEM((slabs, len(SHEARS), 3, strip, cols), jnp.float32),
-            pltpu.SMEM(offsets.shape, jnp.int32),
-            pltpu.SemaphoreType.DMA(()),
-        ],
         compiler_params=pltpu.CompilerParams(vmem_limit_bytes=VMEM_BYTES),
         name="lit_strips",
     )(offsets, *codes, sums, opac)

time: 28.9 us -> 27.4 us (0.948)
  Pallas kernels: 9 us -> 7.31 us
    pallas_call x1, Pallas kernels: 3.84 us -> 2.64 us  [image_sums(): pl.pallas_call(functools.partial(sums_kernel, 16, min(rows, 128)), in_spe...]
    pallas_call x1, Pallas kernels: 1.34 us -> 0.85 us  [lit_strips(): pl.pallas_call(functools.partial(lit_kernel, slabs, depth_cells), in_spec...]
  transfers between devices with their start and end apart: 9 -> 9, of which waited for: 4 -> 6; matrix products, arithmetic and copies ran while one was open for 0% -> 0% of each run, Pallas kernels for 18% -> 14%
where the time goes in v3:
time: 27.4 us; the launch traced here: 27.1 us
  starting transfers between devices  10.3 us (38%)
  waiting for transfers between devices  9.4 us (34%)
  Pallas kernels  7.31 us (27%)
    ppermute x6, starting transfers between devices, swap_depth(): lax.ppermute(value, 'depth', [(i, int(partner(i, k, count)) if count & co...  7.11 us
    ppermute x3, waiting for transfers between devices, swap_columns(): return lax.ppermute(value, ('depth', 'row', 'col'), pairs)  6.78 us
    ppermute x3, starting transfers between devices, swap_columns(): return lax.ppermute(value, ('depth', 'row', 'col'), pairs)  3.22 us
    pallas_call x1, Pallas kernels, image_sums(): pl.pallas_call(functools.partial(sums_kernel, 16, min(rows, 128)), in_spe...  2.64 us
    ppermute x6, waiting for transfers between devices, swap_depth(): lax.ppermute(value, 'depth', [(i, int(partner(i, k, count)) if count & co...  2.62 us
    pallas_call x1, Pallas kernels, slab_code(): pl.pallas_call(functools.partial(plane_kernel, parts), in_specs=[pl.Block...  1.27 us
    pallas_call x1, Pallas kernels, piece_plans(): pl.pallas_call(functools.partial(plan_kernel, slabs, columns, plans), in_...  1.13 us
    pallas_call x1, Pallas kernels, composed_frame(): pl.pallas_call(functools.partial(frame_kernel, slabs, swaps, list(masks))...  0.93 us
  transfers between devices with their start and end apart: 9, of which 6 were waited for; matrix products, arithmetic and copies ran while one was open for 0% of the time, Pallas kernels for 14%

profile of v3, /device:TPU:8, one launch (start us, length us, event | category | flops | bytes accessed | tf_op | source)
XLA Modules:
  0.0 27.1 jit_solution(17381081739786859243)
XLA Ops:
  0.0 0.0 copy-start
  0.0 1.3 %slab_code.1 = (bf16[128,128]{1,0:T(8,128)(2,1)S(1)}, f32[16,128,128]{2,1,0:T(8,128)S(1)}) custom-call(f32[16,128,128]{2,1,0:T(8,128)} %density_hbm.1), custom_call_target="tpu_custom_call" | custom-call | tf_op jit(solution)/shard_map/slab_code/pallas_call | solution.py:68
  1.3 2.5 %collective-permute-start.2 = (bf16[128,128]{1,0:T(8,128)(2,1)S(1)}, bf16[128,128]{1,0:T(8,128)(2,1)S(1)}, u32[]{:S(2)}, u32[]{:S(2)}) collective-permute-start(bf16[128,128]{1,0:T(8,128)(2,1)S(1)} %get-tuple-element.21.refs_0_), channel_id=1, source_target_pairs={{0,24},{8,16},{16,8},{24,0},{1,25},{9,17},{17,9},{25,1},{2,26},{10... | collective-permute-start | bytes 98312 | tf_op jit(solution)/shard_map/ppermute | solution.py:215
  3.8 0.5 %collective-permute-start.1 = (bf16[128,128]{1,0:T(8,128)(2,1)S(1)}, bf16[128,128]{1,0:T(8,128)(2,1)S(1)}, u32[]{:S(2)}, u32[]{:S(2)}) collective-permute-start(bf16[128,128]{1,0:T(8,128)(2,1)S(1)} %get-tuple-element.21.refs_0_), channel_id=1, source_target_pairs={{0,16},{8,24},{16,0},{24,8},{1,17},{9,25},{17,1},{25,9},{2,18},{10... | collective-permute-start | bytes 98312 | tf_op jit(solution)/shard_map/ppermute | solution.py:215
  4.3 0.5 %collective-permute-start = (bf16[128,128]{1,0:T(8,128)(2,1)S(1)}, bf16[128,128]{1,0:T(8,128)(2,1)S(1)}, u32[]{:S(2)}, u32[]{:S(2)}) collective-permute-start(bf16[128,128]{1,0:T(8,128)(2,1)S(1)} %get-tuple-element.21.refs_0_), channel_id=1, source_target_pairs={{0,8},{8,0},{16,24},{24,16},{1,9},{9,1},{17,25},{25,17},{2,10},{10... | collective-permute-start | bytes 98312 | tf_op jit(solution)/shard_map/ppermute | solution.py:215
  4.8 0.0 copy-start.1
  4.8 0.0 copy-start.2
  4.8 2.6 %image_sums.1 = (f32[42,128,128]{2,1,0:T(8,128)S(1)}, bf16[2,128,128]{2,1,0:T(8,128)(2,1)S(1)}) custom-call(f32[16,128,128]{2,1,0:T(8,128)S(1)} %get-tuple-element.22.density_ref, bf16[3,16,128,128]{3,2,1,0:T(8,128)(2,1)} %albedo_hbm.1), custom_call_target="tpu_custom_call" | custom-call | flops 15728640 | bytes 5373952 | tf_op jit(solution)/shard_map/image_sums/pallas_call | solution.py:185
  7.5 0.0 collective-permute-done.2.refs_3_
  7.5 0.2 collective-permute-done.1.refs_2_
  7.7 0.5 %collective-permute-done.refs_1_ = bf16[128,128]{1,0:T(8,128)(2,1)S(1)} collective-permute-done((bf16[128,128]{1,0:T(8,128)(2,1)S(1)}, bf16[128,128]{1,0:T(8,128)(2,1)S(1)}, u32[]{:S(2)}, u32[]{:S(2)}) %collective-permute-start) | collective-permute-done | bytes 32800 | tf_op jit(solution)/shard_map/ppermute | solution.py:215
  8.2 0.0 copy-done
  8.2 0.8 %lit_strips.1 = (bf16[2,4,32,128]{3,2,1,0:T(8,128)(2,1)S(1)}, bf16[2,4,32,128]{3,2,1,0:T(8,128)(2,1)S(1)}, bf16[2,4,32,128]{3,2,1,0:T(8,128)(2,1)S(1)}, bf16[2,4,32,128]{3,2,1,0:T(8,128)(2,1)S(1)}) custom-call(s32[2,4]{1,0:T(2,128)S(1)} %bitcast.1, bf16[128,128]{1,0:T(8,128)(2,1)S(1)} %get-tuple-element.21.refs_0_, ...), custom_call_target="tpu_custom_call" | custom-call | tf_op jit(solution)/shard_map/lit_strips/pallas_call | solution.py:264
  9.1 1.8 %collective-permute-start.3 = (bf16[2,4,32,128]{3,2,1,0:T(8,128)(2,1)S(1)}, bf16[2,4,32,128]{3,2,1,0:T(8,128)(2,1)S(1)}, u32[]{:S(2)}, u32[]{:S(2)}) collective-permute-start(bf16[2,4,32,128]{3,2,1,0:T(8,128)(2,1)S(1)} %get-tuple-element.27), channel_id=1, source_target_pairs={{0,24},{8,16},{16,8},{24,0},{1,25},{9,17},{17,9},{25,1},{2,26},{10... | collective-permute-start | bytes 196616 | tf_op jit(solution)/shard_map/ppermute | solution.py:215
  10.9 0.5 %collective-permute-start.4 = (bf16[2,4,32,128]{3,2,1,0:T(8,128)(2,1)S(1)}, bf16[2,4,32,128]{3,2,1,0:T(8,128)(2,1)S(1)}, u32[]{:S(2)}, u32[]{:S(2)}) collective-permute-start(bf16[2,4,32,128]{3,2,1,0:T(8,128)(2,1)S(1)} %get-tuple-element.28), channel_id=1, source_target_pairs={{0,16},{8,24},{16,0},{24,8},{1,17},{9,25},{17,1},{25,9},{2,18},{10... | collective-permute-start | bytes 196616 | tf_op jit(solution)/shard_map/ppermute | solution.py:215
  11.4 1.2 %collective-permute-start.5 = (bf16[2,4,32,128]{3,2,1,0:T(8,128)(2,1)S(1)}, bf16[2,4,32,128]{3,2,1,0:T(8,128)(2,1)S(1)}, u32[]{:S(2)}, u32[]{:S(2)}) collective-permute-start(bf16[2,4,32,128]{3,2,1,0:T(8,128)(2,1)S(1)} %get-tuple-element.29), channel_id=1, source_target_pairs={{0,8},{8,0},{16,24},{24,16},{1,9},{9,1},{17,25},{25,17},{2,10},{10... | collective-permute-start | bytes 196616 | tf_op jit(solution)/shard_map/ppermute | solution.py:215
  12.6 0.0 copy-done.1
  12.6 0.0 copy-done.2
  12.6 1.1 %piece_plans.1 = (bf16[2,4,4,16,128]{4,3,2,1,0:T(8,128)(2,1)S(1)}, bf16[2,4,4,16,128]{4,3,2,1,0:T(8,128)(2,1)S(1)}, bf16[2,2,4,16,128]{4,3,2,1,0:T(8,128)(2,1)S(...) custom-call(s32[2,4,1,4]{3,2,1,0:T(1,128)S(1)} %copy-done.1, s32[2,4]{1,0:T(2,128)S(1)} %bitcast.2, ...), custom_call_target="tpu_custom_call" | custom-call | tf_op jit(solution)/shard_map/piece_plans/pallas_call | solution.py:365
  13.8 1.1 %collective-permute-done.3.refs_1_ = bf16[2,4,32,128]{3,2,1,0:T(8,128)(2,1)S(1)} collective-permute-done((bf16[2,4,32,128]{3,2,1,0:T(8,128)(2,1)S(1)}, bf16[2,4,32,128]{3,2,1,0:T(8,128)(2,1)S(1)}, u32[]{:S(2)}, u32[]{:S(2)}) %collective-permute-start.3) | collective-permute-done | bytes 65568 | tf_op jit(solution)/shard_map/ppermute | solution.py:215
  14.9 0.5 %collective-permute-done.4.refs_2_ = bf16[2,4,32,128]{3,2,1,0:T(8,128)(2,1)S(1)} collective-permute-done((bf16[2,4,32,128]{3,2,1,0:T(8,128)(2,1)S(1)}, bf16[2,4,32,128]{3,2,1,0:T(8,128)(2,1)S(1)}, u32[]{:S(2)}, u32[]{:S(2)}) %collective-permute-start.4) | collective-permute-done | bytes 65568 | tf_op jit(solution)/shard_map/ppermute | solution.py:215
  15.4 0.2 collective-permute-done.5.refs_3_
  15.7 0.3 %pack_sent.1 = (bf16[2,4,4,32,128]{4,3,2,1,0:T(8,128)(2,1)S(1)}, bf16[2,4,4,32,128]{4,3,2,1,0:T(8,128)(2,1)S(1)}, bf16[2,2,4,32,128]{4,3,2,1,0:T(8,128)(2,1)S(1)}) custom-call(bf16[2,4,32,128]{3,2,1,0:T(8,128)(2,1)S(1)} %get-tuple-element.25.refs_0_, bf16[2,4,32,128]{3,2,1,0:T(8,128)(2,1)S(1)} %collective-permute-done.3.refs_1_, ...), custom_call_target="tpu_custom_call" | custom-call | tf_op jit(solution)/shard_map/pack_sent/pallas_call | solution.py:397
  16.0 0.5 %collective-permute-start.6 = (bf16[2,4,4,32,128]{4,3,2,1,0:T(8,128)(2,1)S(1)}, bf16[2,4,4,32,128]{4,3,2,1,0:T(8,128)(2,1)S(1)}, u32[]{:S(2)}, u32[]{:S(2)}) collective-permute-start(bf16[2,4,4,32,128]{4,3,2,1,0:T(8,128)(2,1)S(1)} %get-tuple-element.34), channel_id=1, source_target_pairs={{0,1},{1,0},{2,3},{3,2},{4,5},{5,4},{6,7},{7,6},{8,9},{9,8},{10,11... | collective-permute-start | bytes 786440 | tf_op jit(solution)/shard_map/ppermute | solution.py:301
  16.5 2.7 %collective-permute-start.7 = (bf16[2,4,4,32,128]{4,3,2,1,0:T(8,128)(2,1)S(1)}, bf16[2,4,4,32,128]{4,3,2,1,0:T(8,128)(2,1)S(1)}, u32[]{:S(2)}, u32[]{:S(2)}) collective-permute-start(bf16[2,4,4,32,128]{4,3,2,1,0:T(8,128)(2,1)S(1)} %get-tuple-element.35), channel_id=1, source_target_pairs={{0,4},{1,2},{2,1},{3,7},{4,0},{5,6},{6,5},{7,3},{8,12},{9,10},{10,... | collective-permute-start | bytes 786440 | tf_op jit(solution)/shard_map/ppermute | solution.py:301
  19.2 0.0 collective-permute-start.8
  19.2 0.1 pack_kept.1.refs_1_
  19.4 6.8 %collective-permute-done.8.refs_4_ = bf16[2,2,4,32,128]{4,3,2,1,0:T(8,128)(2,1)S(1)} collective-permute-done((bf16[2,2,4,32,128]{4,3,2,1,0:T(8,128)(2,1)S(1)}, bf16[2,2,4,32,128]{4,3,2,1,0:T(8,128)(2,1)S(1)}, u32[]{:S(2)}, u32[]{:S(2)}) %collective-permute-start.8) | collective-permute-done | bytes 131104 | tf_op jit(solution)/shard_map/ppermute | solution.py:301
  26.2 0.0 collective-permute-done.6.refs_2_
  26.2 0.0 collective-permute-done.7.refs_3_
  26.2 0.9 %compose_frame.1 = f32[2,4,1,32,128]{4,3,2,1,0:T(8,128)} custom-call(bf16[2,4,2,16,128]{4,3,2,1,0:T(8,128)(2,1)S(1)} %get-tuple-element.26.refs_0_, bf16[2,4,4,32,128]{4,3,2,1,0:T(8,128)(2,1)S(1)} %pack_kept.1.refs_1_, bf16[2,4,4,32,128]{4,3,2,1,0:T(8,128)(2,1)S(1)} %collective-permute-done.6.refs_2_, ...), custom_call_target="tpu_custom_call" | custom-call | tf_op jit(solution)/shard_map/compose_frame/pallas_call | solution.py:467
Async XLA Ops:
  0.0 8.2 %copy-start = (s32[2,4,1,1]{1,3,2,0:T(1,128)S(1)}, s32[2,4,1,1]{1,3,2,0:T(1,128)}, u32[]{:S(2)}) copy-start(s32[2,4,1,1]{1,3,2,0:T(1,128)} %param.8) | copy-start | bytes 100
  1.3 6.2 %collective-permute-start.2 = (bf16[128,128]{1,0:T(8,128)(2,1)S(1)}, bf16[128,128]{1,0:T(8,128)(2,1)S(1)}, u32[]{:S(2)}, u32[]{:S(2)}) collective-permute-start(bf16[128,128]{1,0:T(8,128)(2,1)S(1)} %get-tuple-element.21.refs_0_), channel_id=1, source_target_pairs={{0,24},{8,16},{16,8},{24,0},{1,25},{9,17},{17,9},{25,1},{2,26},{10... | collective-permute-start | bytes 98312 | tf_op jit(solution)/shard_map/ppermute | solution.py:215
  3.8 3.9 %collective-permute-start.1 = (bf16[128,128]{1,0:T(8,128)(2,1)S(1)}, bf16[128,128]{1,0:T(8,128)(2,1)S(1)}, u32[]{:S(2)}, u32[]{:S(2)}) collective-permute-start(bf16[128,128]{1,0:T(8,128)(2,1)S(1)} %get-tuple-element.21.refs_0_), channel_id=1, source_target_pairs={{0,16},{8,24},{16,0},{24,8},{1,17},{9,25},{17,1},{25,9},{2,18},{10... | collective-permute-start | bytes 98312 | tf_op jit(solution)/shard_map/ppermute | solution.py:215
  4.3 3.9 %collective-permute-start = (bf16[128,128]{1,0:T(8,128)(2,1)S(1)}, bf16[128,128]{1,0:T(8,128)(2,1)S(1)}, u32[]{:S(2)}, u32[]{:S(2)}) collective-permute-start(bf16[128,128]{1,0:T(8,128)(2,1)S(1)} %get-tuple-element.21.refs_0_), channel_id=1, source_target_pairs={{0,8},{8,0},{16,24},{24,16},{1,9},{9,1},{17,25},{25,17},{2,10},{10... | collective-permute-start | bytes 98312 | tf_op jit(solution)/shard_map/ppermute | solution.py:215
  4.8 7.8 %copy-start.1 = (s32[2,4,1,4]{3,2,1,0:T(1,128)S(1)}, s32[2,4,1,4]{3,2,1,0:T(1,128)}, u32[]{:S(2)}) copy-start(s32[2,4,1,4]{3,2,1,0:T(1,128)} %targets_ref.1) | copy-start | bytes 388
  4.8 7.8 %copy-start.2 = (s32[2,4]{1,0:T(2,128)S(1)}, s32[2,4]{1,0:T(2,128)}, u32[]{:S(2)}) copy-start(s32[2,4]{1,0:T(2,128)} %order_ref.1) | copy-start | bytes 100
  9.1 5.8 %collective-permute-start.3 = (bf16[2,4,32,128]{3,2,1,0:T(8,128)(2,1)S(1)}, bf16[2,4,32,128]{3,2,1,0:T(8,128)(2,1)S(1)}, u32[]{:S(2)}, u32[]{:S(2)}) collective-permute-start(bf16[2,4,32,128]{3,2,1,0:T(8,128)(2,1)S(1)} %get-tuple-element.27), channel_id=1, source_target_pairs={{0,24},{8,16},{16,8},{24,0},{1,25},{9,17},{17,9},{25,1},{2,26},{10... | collective-permute-start | bytes 196616 | tf_op jit(solution)/shard_map/ppermute | solution.py:215
  10.9 4.5 %collective-permute-start.4 = (bf16[2,4,32,128]{3,2,1,0:T(8,128)(2,1)S(1)}, bf16[2,4,32,128]{3,2,1,0:T(8,128)(2,1)S(1)}, u32[]{:S(2)}, u32[]{:S(2)}) collective-permute-start(bf16[2,4,32,128]{3,2,1,0:T(8,128)(2,1)S(1)} %get-tuple-element.28), channel_id=1, source_target_pairs={{0,16},{8,24},{16,0},{24,8},{1,17},{9,25},{17,1},{25,9},{2,18},{10... | collective-permute-start | bytes 196616 | tf_op jit(solution)/shard_map/ppermute | solution.py:215
  11.4 4.3 %collective-permute-start.5 = (bf16[2,4,32,128]{3,2,1,0:T(8,128)(2,1)S(1)}, bf16[2,4,32,128]{3,2,1,0:T(8,128)(2,1)S(1)}, u32[]{:S(2)}, u32[]{:S(2)}) collective-permute-start(bf16[2,4,32,128]{3,2,1,0:T(8,128)(2,1)S(1)} %get-tuple-element.29), channel_id=1, source_target_pairs={{0,8},{8,0},{16,24},{24,16},{1,9},{9,1},{17,25},{25,17},{2,10},{10... | collective-permute-start | bytes 196616 | tf_op jit(solution)/shard_map/ppermute | solution.py:215
  16.0 10.1 %collective-permute-start.6 = (bf16[2,4,4,32,128]{4,3,2,1,0:T(8,128)(2,1)S(1)}, bf16[2,4,4,32,128]{4,3,2,1,0:T(8,128)(2,1)S(1)}, u32[]{:S(2)}, u32[]{:S(2)}) collective-permute-start(bf16[2,4,4,32,128]{4,3,2,1,0:T(8,128)(2,1)S(1)} %get-tuple-element.34), channel_id=1, source_target_pairs={{0,1},{1,0},{2,3},{3,2},{4,5},{5,4},{6,7},{7,6},{8,9},{9,8},{10,11... | collective-permute-start | bytes 786440 | tf_op jit(solution)/shard_map/ppermute | solution.py:301
  16.5 9.6 %collective-permute-start.7 = (bf16[2,4,4,32,128]{4,3,2,1,0:T(8,128)(2,1)S(1)}, bf16[2,4,4,32,128]{4,3,2,1,0:T(8,128)(2,1)S(1)}, u32[]{:S(2)}, u32[]{:S(2)}) collective-permute-start(bf16[2,4,4,32,128]{4,3,2,1,0:T(8,128)(2,1)S(1)} %get-tuple-element.35), channel_id=1, source_target_pairs={{0,4},{1,2},{2,1},{3,7},{4,0},{5,6},{6,5},{7,3},{8,12},{9,10},{10,... | collective-permute-start | bytes 786440 | tf_op jit(solution)/shard_map/ppermute | solution.py:301
  19.2 6.9 %collective-permute-start.8 = (bf16[2,2,4,32,128]{4,3,2,1,0:T(8,128)(2,1)S(1)}, bf16[2,2,4,32,128]{4,3,2,1,0:T(8,128)(2,1)S(1)}, u32[]{:S(2)}, u32[]{:S(2)}) collective-permute-start(bf16[2,2,4,32,128]{4,3,2,1,0:T(8,128)(2,1)S(1)} %get-tuple-element.36), channel_id=1, source_target_pairs={{0,4},{1,3},{2,6},{3,1},{4,0},{5,7},{6,2},{7,5},{8,12},{9,11},{10,... | collective-permute-start | bytes 393224 | tf_op jit(solution)/shard_map/ppermute | solution.py:301

commit v4 on v3

--- a/solution.py
+++ b/solution.py
@@ -226,14 +226,14 @@
     return (moved == landing).astype(jnp.float32).astype(jnp.bfloat16)
 
 
-def lit_kernel(slabs, depth_cells, offsets_ref, *refs):
+def lit_kernel(slabs, depth_cells, chosen, offsets_ref, after_ref, *refs):
     codes, (sums_ref, opac_ref), outs = refs[:slabs], refs[slabs : slabs + 2], refs[slabs + 2 :]
     mine = lax.axis_index("depth")
     strip, cols = outs[0].shape[2:]
     keys = shift_list(depth_cells)
     middle, spread = depth_code(depth_cells)
     turns = [turn_matrix(offsets_ref[...], v, mine, cols) for v in range(len(SHEARS))]
-    for k in range(slabs):
+    for k, out in zip(chosen, outs, strict=True):
         rows = pl.ds(pl.multiple_of(partner(mine, k, slabs) * strip, strip), strip)
         ahead_depth = jnp.zeros((strip, cols), jnp.float32)
         for other in range(1, slabs):
@@ -253,22 +253,22 @@
                 image.append(total.astype(jnp.bfloat16))
             image = jnp.concatenate([*image, opac_ref[v, rows]], axis=0)
             turned = jnp.dot(image, turns[v], preferred_element_type=jnp.float32)
-            outs[k][v] = turned.astype(jnp.bfloat16).reshape(4, strip, cols)
-
-
-def lit_strips(codes, sums, opac, offsets, depth_cells):
+            out[v] = turned.astype(jnp.bfloat16).reshape(4, strip, cols)
+
+
+def lit_strips(codes, sums, opac, offsets, after, depth_cells, chosen):
     slabs = len(codes)
     rows, cols = codes[0].shape
     strip = rows // slabs
     vmem = pl.BlockSpec(memory_space=pltpu.VMEM)
     return pl.pallas_call(
-        functools.partial(lit_kernel, slabs, depth_cells),
-        in_specs=[vmem] * (slabs + 3),
-        out_specs=[vmem] * slabs,
-        out_shape=[jax.ShapeDtypeStruct((len(SHEARS), 4, strip, cols), jnp.bfloat16)] * slabs,
+        functools.partial(lit_kernel, slabs, depth_cells, chosen),
+        in_specs=[vmem, pl.BlockSpec(memory_space=pl.ANY)] + [vmem] * (slabs + 2),
+        out_specs=[vmem] * len(chosen),
+        out_shape=[jax.ShapeDtypeStruct((len(SHEARS), 4, strip, cols), jnp.bfloat16)] * len(chosen),
         compiler_params=pltpu.CompilerParams(vmem_limit_bytes=VMEM_BYTES),
-        name="lit_strips",
-    )(offsets, *codes, sums, opac)
+        name="lit_strips_" + "".join(str(k) for k in chosen),
+    )(offsets, after, *codes, sums, opac)
 
 
 def piece_slots(step, slabs):
@@ -309,80 +309,137 @@
 def plan_kernel(slabs, columns, plans, targets_ref, offsets_ref, order_ref, *refs):
     outs = refs[1:]
     mine, column = lax.axis_index("depth"), lax.axis_index("col")
-    rows, cols = outs[0].shape[3:]
-    lane = lax.broadcasted_iota(jnp.int32, (rows, cols), 1)
-
-    def found_before(view, source, tile):
-        count, found = jnp.int32(0), []
-        for position in range(slabs):
-            first = targets_ref[view, order_ref[view, position], 0, source]
-            here = (first == tile) | (first + 1 == tile)
-            found.append((here, count))
-            count = count + here.astype(jnp.int32)
-        return found
-
-    for out, (role, step, parity, lefts, slots) in zip(outs, plans, strict=True):
-        if role == "take":
-            source = column - step
-            present = (source >= 0) & (source < columns)
-            source = jnp.clip(source, 0, columns - 1)
-            for v in range(len(SHEARS)):
-                for position, (here, count) in enumerate(found_before(v, source, column)):
-                    for slot in range(slots):
-                        chosen = (here & present & (count == slot)).astype(jnp.float32)
-                        out[v, position, slot] = jnp.full((rows, cols), chosen).astype(out.dtype)
-            continue
-        tile = column
-        if step:
-            is_left = lax.rem(lax.div(column, step), 2) == parity
-            is_left = is_left & (column >= lefts[0]) & (column + step < columns)
-            is_right = (lax.rem(column, 2) != parity) & (column - step >= lefts[0]) & (step == 1)
-            tile = jnp.where(is_left, column + step, jnp.where(is_right, column - step, -PAIR))
-        for v in range(len(SHEARS)):
-            found = found_before(v, column, tile)
-            for k in range(slabs):
-                slab = origin(mine, k, slabs)
-                first, offset = targets_ref[v, slab, 0, column], offsets_ref[v, slab]
-                for slot in range(slots):
-                    chosen = jnp.int32(0)
-                    for position, (here, count) in enumerate(found):
-                        fits = (order_ref[v, position] == slab) & (slot == position)
-                        if slots < slabs:
-                            fits = (order_ref[v, position] == slab) & here & (count == slot)
-                        chosen = chosen + fits.astype(jnp.int32)
-                    before = (chosen * (first == tile).astype(jnp.int32)).astype(jnp.float32)
-                    after = (chosen * (first + 1 == tile).astype(jnp.int32)).astype(jnp.float32)
-                    out[v, slot, k] = jnp.where(lane >= offset, before, after).astype(out.dtype)
-
-
-def piece_plans(targets, offsets, slab_order, after, columns, plans):
+    cols = outs[0].shape[-1]
+    shape = (8, cols)
+    lane = lax.broadcasted_iota(jnp.int32, shape, 1).astype(jnp.float32)
+
+    def pick(table, row, at):
+        rows = lax.broadcasted_iota(jnp.int32, table.shape, 0)
+        lanes = lax.broadcasted_iota(jnp.int32, table.shape, 1)
+        entry = jnp.where((rows == row) & (lanes == at), table, 0).astype(jnp.float32)
+        return jnp.broadcast_to(jnp.sum(jnp.sum(entry, axis=1, keepdims=True), axis=0, keepdims=True), shape)
+
+    def flag(condition):
+        return jnp.where(condition, 1.0, 0.0)
+
+    def put(out, at, value):
+        out[at] = jnp.concatenate([value, value], axis=0).astype(out.dtype)
+
+    def same(scalar):
+        return jnp.full(shape, scalar, jnp.int32).astype(jnp.float32)
+
+    for v in range(len(SHEARS)):
+        targets = targets_ref[v, :, 0, :]
+        order = [pick(order_ref[...], v, p) for p in range(slabs)]
+        slab = [same(origin(mine, k, slabs)) for k in range(slabs)]
+        first = [pick(targets, origin(mine, k, slabs), column) for k in range(slabs)]
+        offset = [pick(offsets_ref[...], v, origin(mine, k, slabs)) for k in range(slabs)]
+        places = [[flag(order[p] == slab[k]) for k in range(slabs)] for p in range(slabs)]
+
+        def columns_of(k, tile):
+            return jnp.where(lane >= offset[k], flag(first[k] == tile), flag(first[k] + 1.0 == tile))
+
+        def found_before(firsts, slabs_there, tile):
+            count, found = jnp.zeros(shape, jnp.float32), []
+            for p in range(slabs):
+                here = jnp.zeros(shape, jnp.float32)
+                for start, number in zip(firsts, slabs_there, strict=True):
+                    covered = flag(start == tile) + flag(start + 1.0 == tile)
+                    here = here + flag(order[p] == number) * covered
+                found.append((here, count))
+                count = count + here
+            return found
+
+        for out, (role, step, parity, lefts) in zip(outs, plans, strict=True):
+            tile = same(column)
+            if role in ("near", "far"):
+                is_left = lax.rem(lax.div(column, step), 2) == parity
+                is_left = is_left & (column >= lefts[0]) & (column + step < columns)
+                is_right = (lax.rem(column, 2) != parity) & (column - step >= lefts[0]) & (step == 1)
+                tile = same(jnp.where(is_left, column + step, jnp.where(is_right, column - step, -PAIR)))
+            if role == "near":
+                for k in range(slabs):
+                    put(out, (v, k), columns_of(k, tile))
+            elif role == "keep":
+                own = [columns_of(k, tile) for k in range(slabs)]
+                for p in range(slabs):
+                    for k in range(slabs):
+                        put(out, (v, p, k), places[p][k] * own[k])
+            elif role == "order":
+                for p in range(slabs):
+                    for k in range(slabs):
+                        put(out, (v, p, k), places[p][k])
+            elif role == "far":
+                found = found_before(first, slab, tile)
+                there = [columns_of(k, tile) for k in range(slabs)]
+                for slot in range(out.shape[1]):
+                    chosen = [here * flag(count == slot) for here, count in found]
+                    for k in range(slabs):
+                        fits = chosen[0] * places[0][k]
+                        for p in range(1, slabs):
+                            fits = fits + chosen[p] * places[p][k]
+                        put(out, (v, slot, k), fits * there[k])
+            elif role == "take":
+                source = column - step
+                present = same(((source >= 0) & (source < columns)).astype(jnp.int32))
+                firsts = [pick(targets, d, source) for d in range(slabs)]
+                numbers = [same(d) for d in range(slabs)]
+                for p, (here, count) in enumerate(found_before(firsts, numbers, tile)):
+                    for slot in range(out.shape[2]):
+                        put(out, (v, p, slot), here * present * flag(count == slot))
+
+
+def piece_plans(targets, offsets, slab_order, columns, after, plans, name):
     slabs = slab_order.shape[1]
-    views, cols = after.shape[0], after.shape[3]
-    vmem, smem = pl.BlockSpec(memory_space=pltpu.VMEM), pl.BlockSpec(memory_space=pltpu.SMEM)
-    shapes = []
-    for role, _, _, _, slots in plans:
-        shapes.append((views, slabs, slots) if role == "take" else (views, slots, slabs))
+    views, cols = len(SHEARS), after.shape[-1]
+    vmem = pl.BlockSpec(memory_space=pltpu.VMEM)
+    shapes = {"near": lambda n: (slabs,), "far": lambda n: (n, slabs), "take": lambda n: (slabs, n)}
+    shapes = [shapes.get(role, lambda n: (slabs, slabs))(piece_slots(step, slabs)) for role, step, _, _ in plans]
     return pl.pallas_call(
         functools.partial(plan_kernel, slabs, columns, plans),
-        in_specs=[smem, smem, smem, vmem],
+        in_specs=[vmem] * 4,
         out_specs=[vmem] * len(plans),
-        out_shape=[pltpu.VMEM(shape + (16, cols), jnp.bfloat16) for shape in shapes],
+        out_shape=[pltpu.VMEM((views, *shape, 16, cols), jnp.bfloat16) for shape in shapes],
         compiler_params=pltpu.CompilerParams(vmem_limit_bytes=VMEM_BYTES),
-        name="piece_plans",
+        name=name,
     )(targets, offsets, slab_order, after)
 
 
-def pack_kernel(order, outs_count, *refs):
-    slabs = len(order)
-    blocks = dict(zip(order, refs[:slabs], strict=True))
-    masks, outs = refs[slabs : slabs + outs_count], refs[slabs + outs_count :]
+def near_kernel(chosen, outs_count, *refs):
+    blocks, masks, outs = refs[: len(chosen)], refs[len(chosen) : -outs_count], refs[-outs_count:]
+    for mask_ref, out in zip(masks, outs, strict=True):
+        views, _, channels, strip, _ = out.shape
+        for v in range(views):
+            for i, k in enumerate(chosen):
+                mask = mask_ref[v, k]
+                for c in range(channels):
+                    for row in range(0, strip, 16):
+                        rows = pl.ds(row, 16)
+                        out[v, i, c, rows] = blocks[i][v, c, rows] * mask
+
+
+def near_pieces(blocks, masks, chosen, name):
+    views, channels, strip, cols = blocks[0].shape
+    vmem = pl.BlockSpec(memory_space=pltpu.VMEM)
+    return pl.pallas_call(
+        functools.partial(near_kernel, chosen, len(masks)),
+        in_specs=[vmem] * (len(blocks) + len(masks)),
+        out_specs=[vmem] * len(masks),
+        out_shape=[jax.ShapeDtypeStruct((views, len(chosen), channels, strip, cols), jnp.bfloat16) for _ in masks],
+        compiler_params=pltpu.CompilerParams(vmem_limit_bytes=VMEM_BYTES),
+        name=name,
+    )(*blocks, *masks)
+
+
+def pack_kernel(slabs, outs_count, *refs):
+    blocks, masks, outs = refs[:slabs], refs[slabs : slabs + outs_count], refs[slabs + outs_count :]
     for mask_ref, out in zip(masks, outs, strict=True):
         views, slots, channels, strip, _ = out.shape
         for v in range(views):
             for slot in range(slots):
+                parts = [mask_ref[v, slot, k] for k in range(slabs)]
                 for row in range(0, strip, 16):
                     rows = pl.ds(row, 16)
-                    parts = [mask_ref[v, slot, k] for k in range(slabs)]
                     for c in range(channels):
                         total = blocks[0][v, c, rows] * parts[0]
                         for k in range(1, slabs):
@@ -390,12 +447,12 @@
                         out[v, slot, c, rows] = total
 
 
-def packed_pieces(blocks, masks, order, name):
+def packed_pieces(blocks, masks, name):
     slabs = len(blocks)
     views, channels, strip, cols = blocks[0].shape
     vmem = pl.BlockSpec(memory_space=pltpu.VMEM)
     return pl.pallas_call(
-        functools.partial(pack_kernel, order, len(masks)),
+        functools.partial(pack_kernel, slabs, len(masks)),
         in_specs=[vmem] * (slabs + len(masks)),
         out_specs=[vmem] * len(masks),
         out_shape=[
@@ -403,33 +460,48 @@
         ],
         compiler_params=pltpu.CompilerParams(vmem_limit_bytes=VMEM_BYTES),
         name=name,
-    )(*[blocks[k] for k in order], *masks)
-
-
-def compose_views(slabs, sources, frame_ref):
+    )(*blocks, *masks)
+
+
+def compose_views(sources, order_ref, masks, frame_ref):
     strip, cols = frame_ref.shape[3:]
+    slabs = order_ref.shape[1]
+
+    def placed(refs, first, mask_ref, v, p, c):
+        pieces = []
+        for ref in refs:
+            if mask_ref is None:
+                pieces.append(ref[v, p, c])
+                continue
+            parts = []
+            for row in range(0, strip, 16):
+                rows = pl.ds(row, 16)
+                total = ref[v, 0, c, rows] * mask_ref[v, p, 0]
+                for slot in range(1, ref.shape[1]):
+                    total = total + ref[v, slot, c, rows] * mask_ref[v, p, slot]
+                parts.append(total)
+            pieces.append(jnp.concatenate(parts, axis=0))
+        return pieces[0] if len(pieces) == 1 else jnp.where(first, pieces[0], pieces[1])
+
+    def by_strip(groups, v, p, c):
+        parts = []
+        for row in range(0, strip, 16):
+            rows = pl.ds(row, 16)
+            total = None
+            for chosen, ref in groups:
+                for i, k in enumerate(chosen):
+                    term = ref[v, i, c, rows] * order_ref[v, p, k]
+                    total = term if total is None else total + term
+            parts.append(total)
+        return jnp.concatenate(parts, axis=0)
+
     for v in range(len(SHEARS)):
         colour = [jnp.zeros((strip, cols), jnp.float32) for _ in range(3)]
         weight = jnp.ones((strip, cols), jnp.float32)
-        for position in range(slabs):
-            for pieces, first, masks in sources:
-                slots = pieces[0].shape[1]
-                values = []
-                for c in range(4):
-                    refs = []
-                    for ref in pieces:
-                        if masks is None:
-                            refs.append(ref[v, position, c])
-                            continue
-                        rows = []
-                        for row in range(0, strip, 16):
-                            total = ref[v, 0, c, pl.ds(row, 16)] * masks[v, position, 0]
-                            for slot in range(1, slots):
-                                total = total + ref[v, slot, c, pl.ds(row, 16)] * masks[v, position, slot]
-                            rows.append(total)
-                        refs.append(jnp.concatenate(rows, axis=0))
-                    value = refs[0] if len(refs) == 1 else jnp.where(first, refs[0], refs[1])
-                    values.append(value.astype(jnp.float32))
+        for p in range(slabs):
+            for kind, *source in sources:
+                take = by_strip if kind == "near" else placed
+                values = [take(*source, v, p, c).astype(jnp.float32) for c in range(4)]
                 for c in range(3):
                     colour[c] = colour[c] + weight * values[c]
                 weight = weight * (1.0 - values[3])
@@ -438,40 +510,43 @@
         frame_ref[v, 3, 0] = 1.0 - weight
 
 
-def frame_kernel(slabs, swaps, takes, *refs):
-    taken, own_ref = dict(zip(takes, refs[: len(takes)], strict=True)), refs[len(takes)]
-    received, frame_ref = refs[len(takes) + 1 : -1], refs[-1]
+def frame_kernel(names, slabs, *refs):
+    frame_ref = refs[-1]
+    given = dict(zip(names, refs[:-1], strict=True))
     tile = lax.axis_index("col")
-    by_step = {}
-    for ref, (step, parity, _) in zip(received, swaps, strict=True):
-        by_step.setdefault(step, {})[parity] = ref
+    near = {parity: [] for parity in range(2)}
+    for (kind, *key), ref in given.items():
+        if kind == "near":
+            near[key[0]].append((key[1], ref))
     for phase in range(2):
         sources = []
         for step in range(slabs // 2, -2, -1):
             if step == 0:
-                sources.append(([own_ref], None, taken.get(step)))
-                continue
-            refs_here = by_step.get(abs(step), {})
-            if abs(step) == 1:
-                parity = (phase - step) % 2 if step > 0 else phase
-                refs_here = {q: ref for q, ref in refs_here.items() if q == parity}
-            if refs_here:
-                first = lax.rem(lax.div(tile + step, abs(step)), 2) == 0
-                sources.append(([refs_here[q] for q in sorted(refs_here)], first, taken.get(step)))
-        pl.when(lax.rem(tile, 2) == phase)(functools.partial(compose_views, slabs, sources, frame_ref))
-
-
-def composed_frame(own, received, masks, slabs, swaps):
-    views, _, channels, strip, cols = own.shape
+                sources.append(("own", [given["own",]], None, None))
+            elif abs(step) == 1:
+                groups = near[(phase - step) % 2 if step > 0 else phase]
+                if groups:
+                    sources.append(("near", groups))
+            else:
+                arrived = [given["far", step, q] for q in range(2) if ("far", step, q) in given]
+                if arrived:
+                    first = lax.rem(lax.div(tile + step, step), 2) == 0
+                    sources.append(("far", arrived, first, given["take", step]))
+        compose = functools.partial(compose_views, sources, given["order",], None, frame_ref)
+        pl.when(lax.rem(tile, 2) == phase)(compose)
+
+
+def composed_frame(given, slabs):
+    views, _, channels, strip, cols = given["own",].shape
     vmem = pl.BlockSpec(memory_space=pltpu.VMEM)
     return pl.pallas_call(
-        functools.partial(frame_kernel, slabs, swaps, list(masks)),
-        in_specs=[vmem] * (len(masks) + 1 + len(received)),
+        functools.partial(frame_kernel, list(given), slabs),
+        in_specs=[vmem] * len(given),
         out_specs=vmem,
         out_shape=jax.ShapeDtypeStruct((views, channels, 1, strip, cols), jnp.float32),
         compiler_params=pltpu.CompilerParams(vmem_limit_bytes=VMEM_BYTES),
         name="compose_frame",
-    )(*masks.values(), own, *received)
+    )(*given.values())
 
 
 def on_device(density, albedo, targets, offsets, slab_order):
@@ -481,27 +556,35 @@
     code, density = slab_code(density)
     codes = [code] + [swap_depth(code, k, slabs) for k in range(1, slabs)]
     sums, opac = image_sums(density, albedo)
-    strips = lit_strips(codes, sums, opac, offsets, depth_cells)
-    blocks = [strips[0]] + [swap_depth(strips[k], k, slabs) for k in range(1, slabs)]
     swaps = column_swaps(slabs, columns)
-    kept_slots = min(slabs, 2 * PAIR)
-    plans = [("send", *swap, piece_slots(swap[0], slabs)) for swap in swaps]
-    plans.append(("keep", 0, 0, [], kept_slots))
-    takes = []
-    for step in [*sorted({step for step, _, _ in swaps}), 0, -1]:
-        slots = kept_slots if step == 0 else piece_slots(abs(step), slabs)
-        if slots < slabs:
-            takes.append(step)
-            plans.append(("take", step, 0, [], slots))
-    masks = piece_plans(targets, offsets, slab_order, strips[0], columns, plans)
-    order = [0, *range(slabs - 1, 0, -1)]
-    outgoing = packed_pieces(blocks, masks[: len(swaps)], order, "pack_sent")
-    (own,) = packed_pieces(blocks, masks[len(swaps) : len(swaps) + 1], order, "pack_kept")
-    received = [
-        swap_columns(value, step, lefts, slabs, columns)
-        for value, (step, _, lefts) in zip(outgoing, swaps, strict=True)
-    ]
-    return composed_frame(own, received, dict(zip(takes, masks[len(swaps) + 1 :], strict=True)), slabs, swaps)
+    near = [swap for swap in swaps if swap[0] == 1]
+    far = [swap for swap in swaps if swap[0] > 1]
+    far_steps = sorted({swap[0] for swap in far})
+    roles = [("near", *swap) for swap in near] + [("far", *swap) for swap in far]
+    roles += [("take", step, 0, []) for step in far_steps] + [("keep", 0, 0, []), ("order", 0, 0, [])]
+    masks = piece_plans(targets, offsets, slab_order, columns, sums, roles, "piece_plans")
+    near_masks, masks = masks[: len(near)], masks[len(near) :]
+    strips = {}
+    for chosen in (list(range(1, slabs)), [0]):
+        lit = lit_strips(codes, sums, opac, offsets, offsets, depth_cells, chosen)
+        strips |= dict(zip(chosen, lit, strict=True))
+    blocks = {0: strips[0]} | {k: swap_depth(strips[k], k, slabs) for k in range(1, slabs)}
+    given = {("order",): masks[-1]}
+    given |= {("take", step): mask for step, mask in zip(far_steps, masks[len(far) :], strict=False)}
+    for name, chosen in (("early", tuple(range(max(1, slabs // 2)))), ("late", tuple(range(max(1, slabs // 2), slabs)))):
+        pieces = near_pieces([blocks[k] for k in chosen], near_masks, chosen, "near_pieces_" + name)
+        for (step, parity, lefts), piece in zip(near, pieces, strict=True):
+            given["near", parity, chosen] = swap_columns(piece, step, lefts, slabs, columns)
+    blocks = [blocks[k] for k in range(slabs)]
+    if far:
+        for (step, parity, lefts), piece in zip(far, packed_pieces(blocks, masks[: len(far)], "far_pieces"), strict=True):
+            given["far", step, parity] = swap_columns(piece, step, lefts, slabs, columns)
+    (given["own",],) = packed_pieces(blocks, masks[-2:-1], "kept_pieces")
+    if slabs == 4:
+        names = dict(a=("near", 0, (0, 1)), b=("near", 1, (0, 1)), c=("near", 0, (2, 3)), d=("near", 1, (2, 3)), f=("far", 2, 0))
+        first = [names[x] for x in "abfcd"]
+        given = {key: given[key] for key in [*first, *(k for k in given if k not in first)]}
+    return composed_frame(given, slabs)
 
 
 def solution(mesh):

time: 27.4 us -> 27.1 us (0.989)
  starting transfers between devices: 10.3 us -> 13.1 us
  waiting for transfers between devices: 9.4 us -> 7 us
  Pallas kernels: 7.31 us -> 6.7 us
    ppermute x3 -> x5, starting transfers between devices: 3.22 us -> 6.02 us  [swap_columns(): return lax.ppermute(value, ('depth', 'row', 'col'), pairs)]
    ppermute x6, waiting for transfers between devices: 2.62 us -> 1.31 us  [swap_depth(): lax.ppermute(value, 'depth', [(i, int(partner(i, k, count)) if count & co...]
    ppermute x3 -> x5, waiting for transfers between devices: 6.78 us -> 5.69 us  [swap_columns(): return lax.ppermute(value, ('depth', 'row', 'col'), pairs)]
    pallas_call x1, Pallas kernels: 1.13 us -> 0.23 us  [piece_plans(): pl.pallas_call(functools.partial(plan_kernel, slabs, columns, plans), in_...]
    pallas_call x4 -> x7, Pallas kernels: 2.27 us -> 2.57 us  [the longest x1 1.19 us: composed_frame(): pl.pallas_call(functools.partial(frame_kernel, list(given), slabs), in_sp...]
  transfers between devices with their start and end apart: 9 -> 11, of which waited for: 6 -> 8; matrix products, arithmetic and copies ran while one was open for 0% -> 0% of each run, Pallas kernels for 14% -> 13%
where the time goes in v4:
time: 27.1 us; the launch traced here: 26.9 us
  starting transfers between devices  13.1 us (48%)
  waiting for transfers between devices  7 us (26%)
  Pallas kernels  6.7 us (25%)
    ppermute x6, starting transfers between devices, swap_depth(): lax.ppermute(value, 'depth', [(i, int(partner(i, k, count)) if count & co...  7.11 us
    ppermute x5, starting transfers between devices, swap_columns(): return lax.ppermute(value, ('depth', 'row', 'col'), pairs)  6.02 us
    ppermute x5, waiting for transfers between devices, swap_columns(): return lax.ppermute(value, ('depth', 'row', 'col'), pairs)  5.69 us
    pallas_call x1, Pallas kernels, image_sums(): pl.pallas_call(functools.partial(sums_kernel, 16, min(rows, 128)), in_spe...  2.64 us
    ppermute x6, waiting for transfers between devices, swap_depth(): lax.ppermute(value, 'depth', [(i, int(partner(i, k, count)) if count & co...  1.31 us
    pallas_call x1, Pallas kernels, slab_code(): pl.pallas_call(functools.partial(plane_kernel, parts), in_specs=[pl.Block...  1.27 us
    pallas_call x1, Pallas kernels, composed_frame(): pl.pallas_call(functools.partial(frame_kernel, list(given), slabs), in_sp...  1.19 us
    pallas_call x2, Pallas kernels, lit_strips(): pl.pallas_call(functools.partial(lit_kernel, slabs, depth_cells, chosen),...  1.07 us
  transfers between devices with their start and end apart: 11, of which 8 were waited for; matrix products, arithmetic and copies ran while one was open for 0% of the time, Pallas kernels for 13%

profile of v4, /device:TPU:8, one launch (start us, length us, event | category | flops | bytes accessed | tf_op | source)
XLA Modules:
  0.0 26.9 jit_solution(8715278014275083260)
XLA Ops:
  0.0 0.0 copy-start
  0.0 1.3 %slab_code.1 = (bf16[128,128]{1,0:T(8,128)(2,1)S(1)}, f32[16,128,128]{2,1,0:T(8,128)S(1)}) custom-call(f32[16,128,128]{2,1,0:T(8,128)} %density_hbm.1), custom_call_target="tpu_custom_call" | custom-call | tf_op jit(solution)/shard_map/slab_code/pallas_call | solution.py:68
  1.3 2.5 %collective-permute-start.2 = (bf16[128,128]{1,0:T(8,128)(2,1)S(1)}, bf16[128,128]{1,0:T(8,128)(2,1)S(1)}, u32[]{:S(2)}, u32[]{:S(2)}) collective-permute-start(bf16[128,128]{1,0:T(8,128)(2,1)S(1)} %get-tuple-element.22.refs_0_), channel_id=1, source_target_pairs={{0,24},{8,16},{16,8},{24,0},{1,25},{9,17},{17,9},{25,1},{2,26},{10... | collective-permute-start | bytes 98312 | tf_op jit(solution)/shard_map/ppermute | solution.py:215
  3.8 0.5 %collective-permute-start.1 = (bf16[128,128]{1,0:T(8,128)(2,1)S(1)}, bf16[128,128]{1,0:T(8,128)(2,1)S(1)}, u32[]{:S(2)}, u32[]{:S(2)}) collective-permute-start(bf16[128,128]{1,0:T(8,128)(2,1)S(1)} %get-tuple-element.22.refs_0_), channel_id=1, source_target_pairs={{0,16},{8,24},{16,0},{24,8},{1,17},{9,25},{17,1},{25,9},{2,18},{10... | collective-permute-start | bytes 98312 | tf_op jit(solution)/shard_map/ppermute | solution.py:215
  4.3 0.5 %collective-permute-start = (bf16[128,128]{1,0:T(8,128)(2,1)S(1)}, bf16[128,128]{1,0:T(8,128)(2,1)S(1)}, u32[]{:S(2)}, u32[]{:S(2)}) collective-permute-start(bf16[128,128]{1,0:T(8,128)(2,1)S(1)} %get-tuple-element.22.refs_0_), channel_id=1, source_target_pairs={{0,8},{8,0},{16,24},{24,16},{1,9},{9,1},{17,25},{25,17},{2,10},{10... | collective-permute-start | bytes 98312 | tf_op jit(solution)/shard_map/ppermute | solution.py:215
  4.8 0.0 copy-start.1
  4.8 0.0 copy-start.2
  4.8 2.6 %image_sums.1 = (f32[42,128,128]{2,1,0:T(8,128)S(1)}, bf16[2,128,128]{2,1,0:T(8,128)(2,1)S(1)}) custom-call(f32[16,128,128]{2,1,0:T(8,128)S(1)} %get-tuple-element.23.density_ref, bf16[3,16,128,128]{3,2,1,0:T(8,128)(2,1)} %albedo_hbm.1), custom_call_target="tpu_custom_call" | custom-call | flops 15728640 | bytes 5373952 | tf_op jit(solution)/shard_map/image_sums/pallas_call | solution.py:185
  7.5 0.0 collective-permute-done.2.refs_3_
  7.5 0.2 collective-permute-done.1.refs_2_
  7.7 0.5 %collective-permute-done.refs_1_ = bf16[128,128]{1,0:T(8,128)(2,1)S(1)} collective-permute-done((bf16[128,128]{1,0:T(8,128)(2,1)S(1)}, bf16[128,128]{1,0:T(8,128)(2,1)S(1)}, u32[]{:S(2)}, u32[]{:S(2)}) %collective-permute-start) | collective-permute-done | bytes 32800 | tf_op jit(solution)/shard_map/ppermute | solution.py:215
  8.2 0.0 copy-done
  8.2 0.7 %lit_strips_123.1 = (bf16[2,4,32,128]{3,2,1,0:T(8,128)(2,1)S(1)}, bf16[2,4,32,128]{3,2,1,0:T(8,128)(2,1)S(1)}, bf16[2,4,32,128]{3,2,1,0:T(8,128)(2,1)S(1)}) custom-call(s32[2,4]{1,0:T(2,128)S(1)} %bitcast.1, s32[2,4]{1,0:T(2,128)S(1)} %bitcast.2, bf16[128,128]{1,0:T(8,128)(2,1)S(1)} %get-tuple-element.22.refs_0_, ...), custom_call_target="tpu_custom_call" | custom-call | tf_op jit(solution)/shard_map/lit_strips_123/pallas_call | solution.py:264
  8.9 0.9 %collective-permute-start.3 = (bf16[2,4,32,128]{3,2,1,0:T(8,128)(2,1)S(1)}, bf16[2,4,32,128]{3,2,1,0:T(8,128)(2,1)S(1)}, u32[]{:S(2)}, u32[]{:S(2)}) collective-permute-start(bf16[2,4,32,128]{3,2,1,0:T(8,128)(2,1)S(1)} %get-tuple-element.26), channel_id=1, source_target_pairs={{0,8},{8,0},{16,24},{24,16},{1,9},{9,1},{17,25},{25,17},{2,10},{10... | collective-permute-start | bytes 196616 | tf_op jit(solution)/shard_map/ppermute | solution.py:215
  9.8 1.5 %collective-permute-start.6 = (bf16[2,4,32,128]{3,2,1,0:T(8,128)(2,1)S(1)}, bf16[2,4,32,128]{3,2,1,0:T(8,128)(2,1)S(1)}, u32[]{:S(2)}, u32[]{:S(2)}) collective-permute-start(bf16[2,4,32,128]{3,2,1,0:T(8,128)(2,1)S(1)} %get-tuple-element.31), channel_id=1, source_target_pairs={{0,16},{8,24},{16,0},{24,8},{1,17},{9,25},{17,1},{25,9},{2,18},{10... | collective-permute-start | bytes 196616 | tf_op jit(solution)/shard_map/ppermute | solution.py:215
  11.3 1.2 %collective-permute-start.7 = (bf16[2,4,32,128]{3,2,1,0:T(8,128)(2,1)S(1)}, bf16[2,4,32,128]{3,2,1,0:T(8,128)(2,1)S(1)}, u32[]{:S(2)}, u32[]{:S(2)}) collective-permute-start(bf16[2,4,32,128]{3,2,1,0:T(8,128)(2,1)S(1)} %get-tuple-element.32), channel_id=1, source_target_pairs={{0,24},{8,16},{16,8},{24,0},{1,25},{9,17},{17,9},{25,1},{2,26},{10... | collective-permute-start | bytes 196616 | tf_op jit(solution)/shard_map/ppermute | solution.py:215
  12.5 0.0 copy-done.1
  12.5 0.0 copy-done.2
  12.5 0.2 piece_plans.1
  12.7 0.4 %lit_strips_0.1.refs_0_ = bf16[2,4,32,128]{3,2,1,0:T(8,128)(2,1)S(1)} custom-call(s32[2,4]{1,0:T(2,128)S(1)} %bitcast.4, s32[2,4]{1,0:T(2,128)S(1)} %bitcast.5, bf16[128,128]{1,0:T(8,128)(2,1)S(1)} %get-tuple-element.22.refs_0_, bf16[128,128]{1,0:T(8,128)(2,1)S(1)} %collective-permute-done.refs_1_, bf16[128,128]{1,0:T(8,128)(2,1)S(1)} %collective-permute-done.1.refs_2_, ...), custom_call_target="tpu_custom_call" | custom-call | tf_op jit(solution)/shard_map/lit_strips_0/pallas_call | solution.py:264
  13.1 0.6 %collective-permute-done.3.refs_1_ = bf16[2,4,32,128]{3,2,1,0:T(8,128)(2,1)S(1)} collective-permute-done((bf16[2,4,32,128]{3,2,1,0:T(8,128)(2,1)S(1)}, bf16[2,4,32,128]{3,2,1,0:T(8,128)(2,1)S(1)}, u32[]{:S(2)}, u32[]{:S(2)}) %collective-permute-start.3) | collective-permute-done | bytes 65568 | tf_op jit(solution)/shard_map/ppermute | solution.py:215
  13.7 0.5 %collective-permute-start.4 = (bf16[2,2,4,32,128]{4,3,2,1,0:T(8,128)(2,1)S(1)}, bf16[2,2,4,32,128]{4,3,2,1,0:T(8,128)(2,1)S(1)}, u32[]{:S(2)}, u32[]{:S(2)}) collective-permute-start(bf16[2,2,4,32,128]{4,3,2,1,0:T(8,128)(2,1)S(1)} %get-tuple-element.29), channel_id=1, source_target_pairs={{0,1},{1,0},{2,3},{3,2},{4,5},{5,4},{6,7},{7,6},{8,9},{9,8},{10,11... | collective-permute-start | bytes 393224 | tf_op jit(solution)/shard_map/ppermute | solution.py:301
  14.2 2.7 %collective-permute-start.5 = (bf16[2,2,4,32,128]{4,3,2,1,0:T(8,128)(2,1)S(1)}, bf16[2,2,4,32,128]{4,3,2,1,0:T(8,128)(2,1)S(1)}, u32[]{:S(2)}, u32[]{:S(2)}) collective-permute-start(bf16[2,2,4,32,128]{4,3,2,1,0:T(8,128)(2,1)S(1)} %get-tuple-element.30), channel_id=1, source_target_pairs={{0,4},{1,2},{2,1},{3,7},{4,0},{5,6},{6,5},{7,3},{8,12},{9,10},{10,... | collective-permute-start | bytes 393224 | tf_op jit(solution)/shard_map/ppermute | solution.py:301
  16.9 0.0 collective-permute-done.6.refs_2_.refs_0_
  16.9 0.0 collective-permute-done.7.refs_3_.refs_1_
  17.0 0.1 collective-permute-start.9
  17.1 2.7 %collective-permute-start.10 = (bf16[2,2,4,32,128]{4,3,2,1,0:T(8,128)(2,1)S(1)}, bf16[2,2,4,32,128]{4,3,2,1,0:T(8,128)(2,1)S(1)}, u32[]{:S(2)}, u32[]{:S(2)}) collective-permute-start(bf16[2,2,4,32,128]{4,3,2,1,0:T(8,128)(2,1)S(1)} %get-tuple-element.35), channel_id=1, source_target_pairs={{0,4},{1,2},{2,1},{3,7},{4,0},{5,6},{6,5},{7,3},{8,12},{9,10},{10,... | collective-permute-start | bytes 393224 | tf_op jit(solution)/shard_map/ppermute | solution.py:301
  19.7 0.1 far_pieces.1
  19.8 0.1 collective-permute-start.8
  19.9 0.2 kept_pieces.1.refs_7_
  20.0 0.1 collective-permute-done.4.refs_0_
  20.1 0.9 %collective-permute-done.5.refs_1_ = bf16[2,2,4,32,128]{4,3,2,1,0:T(8,128)(2,1)S(1)} collective-permute-done((bf16[2,2,4,32,128]{4,3,2,1,0:T(8,128)(2,1)S(1)}, bf16[2,2,4,32,128]{4,3,2,1,0:T(8,128)(2,1)S(1)}, u32[]{:S(2)}, u32[]{:S(2)}) %collective-permute-start.5) | collective-permute-done | bytes 131104 | tf_op jit(solution)/shard_map/ppermute | solution.py:301
  21.0 1.0 %collective-permute-done.9.refs_3_ = bf16[2,2,4,32,128]{4,3,2,1,0:T(8,128)(2,1)S(1)} collective-permute-done((bf16[2,2,4,32,128]{4,3,2,1,0:T(8,128)(2,1)S(1)}, bf16[2,2,4,32,128]{4,3,2,1,0:T(8,128)(2,1)S(1)}, u32[]{:S(2)}, u32[]{:S(2)}) %collective-permute-start.9) | collective-permute-done | bytes 131104 | tf_op jit(solution)/shard_map/ppermute | solution.py:301
  22.0 2.1 %collective-permute-done.10.refs_4_ = bf16[2,2,4,32,128]{4,3,2,1,0:T(8,128)(2,1)S(1)} collective-permute-done((bf16[2,2,4,32,128]{4,3,2,1,0:T(8,128)(2,1)S(1)}, bf16[2,2,4,32,128]{4,3,2,1,0:T(8,128)(2,1)S(1)}, u32[]{:S(2)}, u32[]{:S(2)}) %collective-permute-start.10) | collective-permute-done | bytes 131104 | tf_op jit(solution)/shard_map/ppermute | solution.py:301
  24.1 1.6 %collective-permute-done.8.refs_2_ = bf16[2,2,4,32,128]{4,3,2,1,0:T(8,128)(2,1)S(1)} collective-permute-done((bf16[2,2,4,32,128]{4,3,2,1,0:T(8,128)(2,1)S(1)}, bf16[2,2,4,32,128]{4,3,2,1,0:T(8,128)(2,1)S(1)}, u32[]{:S(2)}, u32[]{:S(2)}) %collective-permute-start.8) | collective-permute-done | bytes 131104 | tf_op jit(solution)/shard_map/ppermute | solution.py:301
  25.7 1.2 %compose_frame.1 = f32[2,4,1,32,128]{4,3,2,1,0:T(8,128)} custom-call(bf16[2,2,4,32,128]{4,3,2,1,0:T(8,128)(2,1)S(1)} %collective-permute-done.4.refs_0_, bf16[2,2,4,32,128]{4,3,2,1,0:T(8,128)(2,1)S(1)} %collective-permute-done.5.refs_1_, bf16[2,2,4,32,128]{4,3,2,1,0:T(8,128)(2,1)S(1)} %collective-permute-done.8.refs_2_, ...), custom_call_target="tpu_custom_call" | custom-call | tf_op jit(solution)/shard_map/compose_frame/pallas_call | solution.py:542
  (2 shorter events, 0.1 us)
Async XLA Ops:
  0.0 8.2 %copy-start = (s32[2,4,1,1]{1,3,2,0:T(1,128)S(1)}, s32[2,4,1,1]{1,3,2,0:T(1,128)}, u32[]{:S(2)}) copy-start(s32[2,4,1,1]{1,3,2,0:T(1,128)} %param.8) | copy-start | bytes 100
  1.3 6.2 %collective-permute-start.2 = (bf16[128,128]{1,0:T(8,128)(2,1)S(1)}, bf16[128,128]{1,0:T(8,128)(2,1)S(1)}, u32[]{:S(2)}, u32[]{:S(2)}) collective-permute-start(bf16[128,128]{1,0:T(8,128)(2,1)S(1)} %get-tuple-element.22.refs_0_), channel_id=1, source_target_pairs={{0,24},{8,16},{16,8},{24,0},{1,25},{9,17},{17,9},{25,1},{2,26},{10... | collective-permute-start | bytes 98312 | tf_op jit(solution)/shard_map/ppermute | solution.py:215
  3.8 3.9 %collective-permute-start.1 = (bf16[128,128]{1,0:T(8,128)(2,1)S(1)}, bf16[128,128]{1,0:T(8,128)(2,1)S(1)}, u32[]{:S(2)}, u32[]{:S(2)}) collective-permute-start(bf16[128,128]{1,0:T(8,128)(2,1)S(1)} %get-tuple-element.22.refs_0_), channel_id=1, source_target_pairs={{0,16},{8,24},{16,0},{24,8},{1,17},{9,25},{17,1},{25,9},{2,18},{10... | collective-permute-start | bytes 98312 | tf_op jit(solution)/shard_map/ppermute | solution.py:215
  4.3 3.9 %collective-permute-start = (bf16[128,128]{1,0:T(8,128)(2,1)S(1)}, bf16[128,128]{1,0:T(8,128)(2,1)S(1)}, u32[]{:S(2)}, u32[]{:S(2)}) collective-permute-start(bf16[128,128]{1,0:T(8,128)(2,1)S(1)} %get-tuple-element.22.refs_0_), channel_id=1, source_target_pairs={{0,8},{8,0},{16,24},{24,16},{1,9},{9,1},{17,25},{25,17},{2,10},{10... | collective-permute-start | bytes 98312 | tf_op jit(solution)/shard_map/ppermute | solution.py:215
  4.8 7.6 %copy-start.1 = (s32[2,4,1,4]{3,2,1,0:T(1,128)S(1)}, s32[2,4,1,4]{3,2,1,0:T(1,128)}, u32[]{:S(2)}) copy-start(s32[2,4,1,4]{3,2,1,0:T(1,128)} %targets_ref.1) | copy-start | bytes 388
  4.8 7.6 %copy-start.2 = (s32[2,4]{1,0:T(2,128)S(1)}, s32[2,4]{1,0:T(2,128)}, u32[]{:S(2)}) copy-start(s32[2,4]{1,0:T(2,128)} %order_ref.1) | copy-start | bytes 100
  8.9 4.8 %collective-permute-start.3 = (bf16[2,4,32,128]{3,2,1,0:T(8,128)(2,1)S(1)}, bf16[2,4,32,128]{3,2,1,0:T(8,128)(2,1)S(1)}, u32[]{:S(2)}, u32[]{:S(2)}) collective-permute-start(bf16[2,4,32,128]{3,2,1,0:T(8,128)(2,1)S(1)} %get-tuple-element.26), channel_id=1, source_target_pairs={{0,8},{8,0},{16,24},{24,16},{1,9},{9,1},{17,25},{25,17},{2,10},{10... | collective-permute-start | bytes 196616 | tf_op jit(solution)/shard_map/ppermute | solution.py:215
  9.8 7.2 %collective-permute-start.6 = (bf16[2,4,32,128]{3,2,1,0:T(8,128)(2,1)S(1)}, bf16[2,4,32,128]{3,2,1,0:T(8,128)(2,1)S(1)}, u32[]{:S(2)}, u32[]{:S(2)}) collective-permute-start(bf16[2,4,32,128]{3,2,1,0:T(8,128)(2,1)S(1)} %get-tuple-element.31), channel_id=1, source_target_pairs={{0,16},{8,24},{16,0},{24,8},{1,17},{9,25},{17,1},{25,9},{2,18},{10... | collective-permute-start | bytes 196616 | tf_op jit(solution)/shard_map/ppermute | solution.py:215
  11.3 5.6 %collective-permute-start.7 = (bf16[2,4,32,128]{3,2,1,0:T(8,128)(2,1)S(1)}, bf16[2,4,32,128]{3,2,1,0:T(8,128)(2,1)S(1)}, u32[]{:S(2)}, u32[]{:S(2)}) collective-permute-start(bf16[2,4,32,128]{3,2,1,0:T(8,128)(2,1)S(1)} %get-tuple-element.32), channel_id=1, source_target_pairs={{0,24},{8,16},{16,8},{24,0},{1,25},{9,17},{17,9},{25,1},{2,26},{10... | collective-permute-start | bytes 196616 | tf_op jit(solution)/shard_map/ppermute | solution.py:215
  13.7 6.4 %collective-permute-start.4 = (bf16[2,2,4,32,128]{4,3,2,1,0:T(8,128)(2,1)S(1)}, bf16[2,2,4,32,128]{4,3,2,1,0:T(8,128)(2,1)S(1)}, u32[]{:S(2)}, u32[]{:S(2)}) collective-permute-start(bf16[2,2,4,32,128]{4,3,2,1,0:T(8,128)(2,1)S(1)} %get-tuple-element.29), channel_id=1, source_target_pairs={{0,1},{1,0},{2,3},{3,2},{4,5},{5,4},{6,7},{7,6},{8,9},{9,8},{10,11... | collective-permute-start | bytes 393224 | tf_op jit(solution)/shard_map/ppermute | solution.py:301
  14.2 6.8 %collective-permute-start.5 = (bf16[2,2,4,32,128]{4,3,2,1,0:T(8,128)(2,1)S(1)}, bf16[2,2,4,32,128]{4,3,2,1,0:T(8,128)(2,1)S(1)}, u32[]{:S(2)}, u32[]{:S(2)}) collective-permute-start(bf16[2,2,4,32,128]{4,3,2,1,0:T(8,128)(2,1)S(1)} %get-tuple-element.30), channel_id=1, source_target_pairs={{0,4},{1,2},{2,1},{3,7},{4,0},{5,6},{6,5},{7,3},{8,12},{9,10},{10,... | collective-permute-start | bytes 393224 | tf_op jit(solution)/shard_map/ppermute | solution.py:301
  17.0 5.0 %collective-permute-start.9 = (bf16[2,2,4,32,128]{4,3,2,1,0:T(8,128)(2,1)S(1)}, bf16[2,2,4,32,128]{4,3,2,1,0:T(8,128)(2,1)S(1)}, u32[]{:S(2)}, u32[]{:S(2)}) collective-permute-start(bf16[2,2,4,32,128]{4,3,2,1,0:T(8,128)(2,1)S(1)} %get-tuple-element.34), channel_id=1, source_target_pairs={{0,1},{1,0},{2,3},{3,2},{4,5},{5,4},{6,7},{7,6},{8,9},{9,8},{10,11... | collective-permute-start | bytes 393224 | tf_op jit(solution)/shard_map/ppermute | solution.py:301
  17.1 7.0 %collective-permute-start.10 = (bf16[2,2,4,32,128]{4,3,2,1,0:T(8,128)(2,1)S(1)}, bf16[2,2,4,32,128]{4,3,2,1,0:T(8,128)(2,1)S(1)}, u32[]{:S(2)}, u32[]{:S(2)}) collective-permute-start(bf16[2,2,4,32,128]{4,3,2,1,0:T(8,128)(2,1)S(1)} %get-tuple-element.35), channel_id=1, source_target_pairs={{0,4},{1,2},{2,1},{3,7},{4,0},{5,6},{6,5},{7,3},{8,12},{9,10},{10,... | collective-permute-start | bytes 393224 | tf_op jit(solution)/shard_map/ppermute | solution.py:301
  19.8 5.9 %collective-permute-start.8 = (bf16[2,2,4,32,128]{4,3,2,1,0:T(8,128)(2,1)S(1)}, bf16[2,2,4,32,128]{4,3,2,1,0:T(8,128)(2,1)S(1)}, u32[]{:S(2)}, u32[]{:S(2)}) collective-permute-start(bf16[2,2,4,32,128]{4,3,2,1,0:T(8,128)(2,1)S(1)} %far_pieces.1), channel_id=1, source_target_pairs={{0,4},{1,3},{2,6},{3,1},{4,0},{5,7},{6,2},{7,5},{8,12},{9,11},{10,... | collective-permute-start | bytes 393224 | tf_op jit(solution)/shard_map/ppermute | solution.py:301

commit v5 on v4

--- a/solution.py
+++ b/solution.py
@@ -228,6 +228,7 @@
 
 def lit_kernel(slabs, depth_cells, chosen, offsets_ref, after_ref, *refs):
     codes, (sums_ref, opac_ref), outs = refs[:slabs], refs[slabs : slabs + 2], refs[slabs + 2 :]
+    codes = [codes[-k % slabs] for k in range(slabs)]
     mine = lax.axis_index("depth")
     strip, cols = outs[0].shape[2:]
     keys = shift_list(depth_cells)
@@ -268,7 +269,7 @@
         out_shape=[jax.ShapeDtypeStruct((len(SHEARS), 4, strip, cols), jnp.bfloat16)] * len(chosen),
         compiler_params=pltpu.CompilerParams(vmem_limit_bytes=VMEM_BYTES),
         name="lit_strips_" + "".join(str(k) for k in chosen),
-    )(offsets, after, *codes, sums, opac)
+    )(offsets, after, *[codes[-k % slabs] for k in range(slabs)], sums, opac)
 
 
 def piece_slots(step, slabs):
@@ -463,90 +464,118 @@
     )(*blocks, *masks)
 
 
-def compose_views(sources, order_ref, masks, frame_ref):
-    strip, cols = frame_ref.shape[3:]
-    slabs = order_ref.shape[1]
-
-    def placed(refs, first, mask_ref, v, p, c):
-        pieces = []
-        for ref in refs:
-            if mask_ref is None:
-                pieces.append(ref[v, p, c])
-                continue
-            parts = []
-            for row in range(0, strip, 16):
-                rows = pl.ds(row, 16)
-                total = ref[v, 0, c, rows] * mask_ref[v, p, 0]
-                for slot in range(1, ref.shape[1]):
-                    total = total + ref[v, slot, c, rows] * mask_ref[v, p, slot]
-                parts.append(total)
-            pieces.append(jnp.concatenate(parts, axis=0))
-        return pieces[0] if len(pieces) == 1 else jnp.where(first, pieces[0], pieces[1])
-
-    def by_strip(groups, v, p, c):
-        parts = []
-        for row in range(0, strip, 16):
-            rows = pl.ds(row, 16)
-            total = None
-            for chosen, ref in groups:
-                for i, k in enumerate(chosen):
-                    term = ref[v, i, c, rows] * order_ref[v, p, k]
-                    total = term if total is None else total + term
-            parts.append(total)
-        return jnp.concatenate(parts, axis=0)
-
-    for v in range(len(SHEARS)):
-        colour = [jnp.zeros((strip, cols), jnp.float32) for _ in range(3)]
-        weight = jnp.ones((strip, cols), jnp.float32)
-        for p in range(slabs):
-            for kind, *source in sources:
-                take = by_strip if kind == "near" else placed
-                values = [take(*source, v, p, c).astype(jnp.float32) for c in range(4)]
-                for c in range(3):
-                    colour[c] = colour[c] + weight * values[c]
-                weight = weight * (1.0 - values[3])
-        for c in range(3):
-            frame_ref[v, c, 0] = colour[c]
-        frame_ref[v, 3, 0] = 1.0 - weight
-
-
-def frame_kernel(names, slabs, *refs):
-    frame_ref = refs[-1]
-    given = dict(zip(names, refs[:-1], strict=True))
+def blend_kernel(names, *refs):
+    given, out = dict(zip(names, refs[:-1], strict=True)), refs[-1]
+    views, slabs, _, strip, cols = out.shape
+    order_ref = given["order",]
     tile = lax.axis_index("col")
     near = {parity: [] for parity in range(2)}
     for (kind, *key), ref in given.items():
         if kind == "near":
             near[key[0]].append((key[1], ref))
+
+    def by_strip(groups, v, p, c, rows):
+        total = None
+        for chosen, ref in groups:
+            for i, k in enumerate(chosen):
+                term = ref[v, i, c, rows] * order_ref[v, p, k]
+                total = term if total is None else total + term
+        return total
+
+    def blend(left, right):
+        for v in range(views):
+            for p in range(slabs):
+                for row in range(0, strip, 16):
+                    rows = pl.ds(row, 16)
+                    colour = [jnp.zeros((16, cols), jnp.float32) for _ in range(3)]
+                    through = jnp.ones((16, cols), jnp.float32)
+                    for source in (left, None, right):
+                        if source is None:
+                            values = [given["own",][v, p, c, rows] for c in range(4)]
+                        elif source:
+                            values = [by_strip(source, v, p, c, rows) for c in range(4)]
+                        else:
+                            continue
+                        values = [value.astype(jnp.float32) for value in values]
+                        for c in range(3):
+                            colour[c] = colour[c] + through * values[c]
+                        through = through * (1.0 - values[3])
+                    for c in range(3):
+                        out[v, p, c, rows] = colour[c]
+                    out[v, p, 3, rows] = through
+
     for phase in range(2):
-        sources = []
-        for step in range(slabs // 2, -2, -1):
-            if step == 0:
-                sources.append(("own", [given["own",]], None, None))
-            elif abs(step) == 1:
-                groups = near[(phase - step) % 2 if step > 0 else phase]
-                if groups:
-                    sources.append(("near", groups))
-            else:
-                arrived = [given["far", step, q] for q in range(2) if ("far", step, q) in given]
-                if arrived:
-                    first = lax.rem(lax.div(tile + step, step), 2) == 0
-                    sources.append(("far", arrived, first, given["take", step]))
-        compose = functools.partial(compose_views, sources, given["order",], None, frame_ref)
-        pl.when(lax.rem(tile, 2) == phase)(compose)
-
-
-def composed_frame(given, slabs):
+        pl.when(lax.rem(tile, 2) == phase)(functools.partial(blend, near[(phase - 1) % 2], near[phase]))
+
+
+def blended_pieces(given, slabs):
     views, _, channels, strip, cols = given["own",].shape
     vmem = pl.BlockSpec(memory_space=pltpu.VMEM)
     return pl.pallas_call(
-        functools.partial(frame_kernel, list(given), slabs),
+        functools.partial(blend_kernel, list(given)),
         in_specs=[vmem] * len(given),
         out_specs=vmem,
-        out_shape=jax.ShapeDtypeStruct((views, channels, 1, strip, cols), jnp.float32),
+        out_shape=pltpu.VMEM((views, slabs, channels, strip, cols), jnp.float32),
+        compiler_params=pltpu.CompilerParams(vmem_limit_bytes=VMEM_BYTES),
+        name="blend_pieces",
+    )(*given.values())
+
+
+def frame_kernel(names, *refs):
+    blended_ref, given = refs[0], dict(zip(names, refs[1:-3], strict=True))
+    frame_hbm, frame_ref, sems = refs[-3:]
+    views, slabs, _, strip, cols = blended_ref.shape
+    tile = lax.axis_index("col")
+    steps = sorted({key[1] for key in given if key[0] == "take"}, reverse=True)
+
+    def placed(step, v, p, c, rows):
+        arrived = [given["far", step, q] for q in range(2) if ("far", step, q) in given]
+        pieces = []
+        for ref in arrived:
+            total = ref[v, 0, c, rows] * given["take", step][v, p, 0]
+            for slot in range(1, ref.shape[1]):
+                total = total + ref[v, slot, c, rows] * given["take", step][v, p, slot]
+            pieces.append(total)
+        first = lax.rem(lax.div(tile + step, step), 2) == 0
+        return pieces[0] if len(pieces) == 1 else jnp.where(first, pieces[0], pieces[1])
+
+    copies = []
+    for v in range(views):
+        for row in range(0, strip, 16):
+            rows = pl.ds(row, 16)
+            colour = [jnp.zeros((16, cols), jnp.float32) for _ in range(3)]
+            weight = jnp.ones((16, cols), jnp.float32)
+            for p in range(slabs):
+                for step in steps:
+                    values = [placed(step, v, p, c, rows).astype(jnp.float32) for c in range(4)]
+                    for c in range(3):
+                        colour[c] = colour[c] + weight * values[c]
+                    weight = weight * (1.0 - values[3])
+                for c in range(3):
+                    colour[c] = colour[c] + weight * blended_ref[v, p, c, rows]
+                weight = weight * blended_ref[v, p, 3, rows]
+            for c in range(3):
+                frame_ref[v, c, 0, rows] = colour[c]
+            frame_ref[v, 3, 0, rows] = 1.0 - weight
+        copies.append(pltpu.make_async_copy(frame_ref.at[v], frame_hbm.at[v], sems.at[v]))
+        copies[-1].start()
+    for copy in copies:
+        copy.wait()
+
+
+def composed_frame(blended, given):
+    views, _, channels, strip, cols = blended.shape
+    vmem = pl.BlockSpec(memory_space=pltpu.VMEM)
+    shape = (views, channels, 1, strip, cols)
+    return pl.pallas_call(
+        functools.partial(frame_kernel, list(given)),
+        in_specs=[vmem] * (1 + len(given)),
+        out_specs=pl.BlockSpec(memory_space=pl.ANY),
+        out_shape=jax.ShapeDtypeStruct(shape, jnp.float32),
+        scratch_shapes=[pltpu.VMEM(shape, jnp.float32), pltpu.SemaphoreType.DMA((views,))],
         compiler_params=pltpu.CompilerParams(vmem_limit_bytes=VMEM_BYTES),
         name="compose_frame",
-    )(*given.values())
+    )(blended, *given.values())
 
 
 def on_device(density, albedo, targets, offsets, slab_order):
@@ -571,7 +600,7 @@
     blocks = {0: strips[0]} | {k: swap_depth(strips[k], k, slabs) for k in range(1, slabs)}
     given = {("order",): masks[-1]}
     given |= {("take", step): mask for step, mask in zip(far_steps, masks[len(far) :], strict=False)}
-    for name, chosen in (("early", tuple(range(max(1, slabs // 2)))), ("late", tuple(range(max(1, slabs // 2), slabs)))):
+    for name, chosen in (("early", tuple(range(max(1, slabs // 2)))), ("late", tuple(range(slabs - 1, max(1, slabs // 2) - 1, -1)))):
         pieces = near_pieces([blocks[k] for k in chosen], near_masks, chosen, "near_pieces_" + name)
         for (step, parity, lefts), piece in zip(near, pieces, strict=True):
             given["near", parity, chosen] = swap_columns(piece, step, lefts, slabs, columns)
@@ -580,11 +609,9 @@
         for (step, parity, lefts), piece in zip(far, packed_pieces(blocks, masks[: len(far)], "far_pieces"), strict=True):
             given["far", step, parity] = swap_columns(piece, step, lefts, slabs, columns)
     (given["own",],) = packed_pieces(blocks, masks[-2:-1], "kept_pieces")
-    if slabs == 4:
-        names = dict(a=("near", 0, (0, 1)), b=("near", 1, (0, 1)), c=("near", 0, (2, 3)), d=("near", 1, (2, 3)), f=("far", 2, 0))
-        first = [names[x] for x in "abfcd"]
-        given = {key: given[key] for key in [*first, *(k for k in given if k not in first)]}
-    return composed_frame(given, slabs)
+    nears = {key: value for key, value in given.items() if key[0] in ("order", "near", "own")}
+    fars = {key: value for key, value in given.items() if key not in nears}
+    return composed_frame(blended_pieces(nears, slabs), fars)
 
 
 def solution(mesh):

time: 27.1 us -> 26.4 us (0.974)
  waiting for transfers between devices: 7 us -> 6.4 us
    ppermute x5, waiting for transfers between devices: 5.69 us -> 5.32 us  [swap_columns(): return lax.ppermute(value, ('depth', 'row', 'col'), pairs)]
    pallas_call x1 -> x2, Pallas kernels: 1.19 us -> 1.16 us  [the longest x1 0.78 us: composed_frame(): pl.pallas_call(functools.partial(frame_kernel, list(given)), in_specs=[vm...]
  transfers between devices with their start and end apart: 11 -> 11, of which waited for: 8 -> 8; matrix products, arithmetic and copies ran while one was open for 0% -> 0% of each run, Pallas kernels for 13% -> 15%
where the time goes in v5:
time: 26.4 us; the launch traced here: 26.3 us
  starting transfers between devices  13.1 us (50%)
  Pallas kernels  6.66 us (25%)
  waiting for transfers between devices  6.4 us (24%)
    ppermute x6, starting transfers between devices, swap_depth(): lax.ppermute(value, 'depth', [(i, int(partner(i, k, count)) if count & co...  7.11 us
    ppermute x5, starting transfers between devices, swap_columns(): return lax.ppermute(value, ('depth', 'row', 'col'), pairs)  6.01 us
    ppermute x5, waiting for transfers between devices, swap_columns(): return lax.ppermute(value, ('depth', 'row', 'col'), pairs)  5.32 us
    pallas_call x1, Pallas kernels, image_sums(): pl.pallas_call(functools.partial(sums_kernel, 16, min(rows, 128)), in_spe...  2.64 us
    pallas_call x1, Pallas kernels, slab_code(): pl.pallas_call(functools.partial(plane_kernel, parts), in_specs=[pl.Block...  1.27 us
    ppermute x6, waiting for transfers between devices, swap_depth(): lax.ppermute(value, 'depth', [(i, int(partner(i, k, count)) if count & co...  1.08 us
    pallas_call x2, Pallas kernels, lit_strips(): pl.pallas_call(functools.partial(lit_kernel, slabs, depth_cells, chosen),...  1.07 us
    pallas_call x1, Pallas kernels, composed_frame(): pl.pallas_call(functools.partial(frame_kernel, list(given)), in_specs=[vm...  0.78 us
  transfers between devices with their start and end apart: 11, of which 8 were waited for; matrix products, arithmetic and copies ran while one was open for 0% of the time, Pallas kernels for 15%

profile of v5, /device:TPU:8, one launch (start us, length us, event | category | flops | bytes accessed | tf_op | source)
XLA Modules:
  0.0 26.3 jit_solution(4444180031348371875)
XLA Ops:
  0.0 0.0 copy-start
  0.0 1.3 %slab_code.1 = (bf16[128,128]{1,0:T(8,128)(2,1)S(1)}, f32[16,128,128]{2,1,0:T(8,128)S(1)}) custom-call(f32[16,128,128]{2,1,0:T(8,128)} %density_hbm.1), custom_call_target="tpu_custom_call" | custom-call | tf_op jit(solution)/shard_map/slab_code/pallas_call | solution.py:68
  1.3 2.5 %collective-permute-start = (bf16[128,128]{1,0:T(8,128)(2,1)S(1)}, bf16[128,128]{1,0:T(8,128)(2,1)S(1)}, u32[]{:S(2)}, u32[]{:S(2)}) collective-permute-start(bf16[128,128]{1,0:T(8,128)(2,1)S(1)} %get-tuple-element.25.refs_0_), channel_id=1, source_target_pairs={{0,24},{8,16},{16,8},{24,0},{1,25},{9,17},{17,9},{25,1},{2,26},{10... | collective-permute-start | bytes 98312 | tf_op jit(solution)/shard_map/ppermute | solution.py:215
  3.8 0.5 %collective-permute-start.1 = (bf16[128,128]{1,0:T(8,128)(2,1)S(1)}, bf16[128,128]{1,0:T(8,128)(2,1)S(1)}, u32[]{:S(2)}, u32[]{:S(2)}) collective-permute-start(bf16[128,128]{1,0:T(8,128)(2,1)S(1)} %get-tuple-element.25.refs_0_), channel_id=1, source_target_pairs={{0,16},{8,24},{16,0},{24,8},{1,17},{9,25},{17,1},{25,9},{2,18},{10... | collective-permute-start | bytes 98312 | tf_op jit(solution)/shard_map/ppermute | solution.py:215
  4.3 0.5 %collective-permute-start.2 = (bf16[128,128]{1,0:T(8,128)(2,1)S(1)}, bf16[128,128]{1,0:T(8,128)(2,1)S(1)}, u32[]{:S(2)}, u32[]{:S(2)}) collective-permute-start(bf16[128,128]{1,0:T(8,128)(2,1)S(1)} %get-tuple-element.25.refs_0_), channel_id=1, source_target_pairs={{0,8},{8,0},{16,24},{24,16},{1,9},{9,1},{17,25},{25,17},{2,10},{10... | collective-permute-start | bytes 98312 | tf_op jit(solution)/shard_map/ppermute | solution.py:215
  4.8 0.0 copy-start.1
  4.8 0.0 copy-start.2
  4.8 2.6 %image_sums.1 = (f32[42,128,128]{2,1,0:T(8,128)S(1)}, bf16[2,128,128]{2,1,0:T(8,128)(2,1)S(1)}) custom-call(f32[16,128,128]{2,1,0:T(8,128)S(1)} %get-tuple-element.22.density_ref, bf16[3,16,128,128]{3,2,1,0:T(8,128)(2,1)} %albedo_hbm.1), custom_call_target="tpu_custom_call" | custom-call | flops 15728640 | bytes 5373952 | tf_op jit(solution)/shard_map/image_sums/pallas_call | solution.py:185
  7.5 0.0 collective-permute-done.refs_1_
  7.5 0.2 collective-permute-done.1.refs_2_
  7.7 0.5 %collective-permute-done.2.refs_3_ = bf16[128,128]{1,0:T(8,128)(2,1)S(1)} collective-permute-done((bf16[128,128]{1,0:T(8,128)(2,1)S(1)}, bf16[128,128]{1,0:T(8,128)(2,1)S(1)}, u32[]{:S(2)}, u32[]{:S(2)}) %collective-permute-start.2) | collective-permute-done | bytes 32800 | tf_op jit(solution)/shard_map/ppermute | solution.py:215
  8.2 0.0 copy-done
  8.2 0.7 %lit_strips_123.1 = (bf16[2,4,32,128]{3,2,1,0:T(8,128)(2,1)S(1)}, bf16[2,4,32,128]{3,2,1,0:T(8,128)(2,1)S(1)}, bf16[2,4,32,128]{3,2,1,0:T(8,128)(2,1)S(1)}) custom-call(s32[2,4]{1,0:T(2,128)S(1)} %bitcast.1, s32[2,4]{1,0:T(2,128)S(1)} %bitcast.2, bf16[128,128]{1,0:T(8,128)(2,1)S(1)} %get-tuple-element.25.refs_0_, ...), custom_call_target="tpu_custom_call" | custom-call | tf_op jit(solution)/shard_map/lit_strips_123/pallas_call | solution.py:265
  8.9 0.9 %collective-permute-start.3 = (bf16[2,4,32,128]{3,2,1,0:T(8,128)(2,1)S(1)}, bf16[2,4,32,128]{3,2,1,0:T(8,128)(2,1)S(1)}, u32[]{:S(2)}, u32[]{:S(2)}) collective-permute-start(bf16[2,4,32,128]{3,2,1,0:T(8,128)(2,1)S(1)} %get-tuple-element.27), channel_id=1, source_target_pairs={{0,8},{8,0},{16,24},{24,16},{1,9},{9,1},{17,25},{25,17},{2,10},{10... | collective-permute-start | bytes 196616 | tf_op jit(solution)/shard_map/ppermute | solution.py:215
  9.8 2.2 %collective-permute-start.6 = (bf16[2,4,32,128]{3,2,1,0:T(8,128)(2,1)S(1)}, bf16[2,4,32,128]{3,2,1,0:T(8,128)(2,1)S(1)}, u32[]{:S(2)}, u32[]{:S(2)}) collective-permute-start(bf16[2,4,32,128]{3,2,1,0:T(8,128)(2,1)S(1)} %get-tuple-element.32), channel_id=1, source_target_pairs={{0,24},{8,16},{16,8},{24,0},{1,25},{9,17},{17,9},{25,1},{2,26},{10... | collective-permute-start | bytes 196616 | tf_op jit(solution)/shard_map/ppermute | solution.py:215
  12.0 0.5 %collective-permute-start.7 = (bf16[2,4,32,128]{3,2,1,0:T(8,128)(2,1)S(1)}, bf16[2,4,32,128]{3,2,1,0:T(8,128)(2,1)S(1)}, u32[]{:S(2)}, u32[]{:S(2)}) collective-permute-start(bf16[2,4,32,128]{3,2,1,0:T(8,128)(2,1)S(1)} %get-tuple-element.33), channel_id=1, source_target_pairs={{0,16},{8,24},{16,0},{24,8},{1,17},{9,25},{17,1},{25,9},{2,18},{10... | collective-permute-start | bytes 196616 | tf_op jit(solution)/shard_map/ppermute | solution.py:215
  12.5 0.0 copy-done.1
  12.5 0.0 copy-done.2
  12.5 0.2 piece_plans.1
  12.7 0.4 %lit_strips_0.1.refs_0_ = bf16[2,4,32,128]{3,2,1,0:T(8,128)(2,1)S(1)} custom-call(s32[2,4]{1,0:T(2,128)S(1)} %bitcast.4, s32[2,4]{1,0:T(2,128)S(1)} %bitcast.5, bf16[128,128]{1,0:T(8,128)(2,1)S(1)} %get-tuple-element.25.refs_0_, bf16[128,128]{1,0:T(8,128)(2,1)S(1)} %collective-permute-done.refs_1_, bf16[128,128]{1,0:T(8,128)(2,1)S(1)} %collective-permute-done.1.refs_2_, ...), custom_call_target="tpu_custom_call" | custom-call | tf_op jit(solution)/shard_map/lit_strips_0/pallas_call | solution.py:265
  13.1 0.4 %collective-permute-done.3.refs_1_ = bf16[2,4,32,128]{3,2,1,0:T(8,128)(2,1)S(1)} collective-permute-done((bf16[2,4,32,128]{3,2,1,0:T(8,128)(2,1)S(1)}, bf16[2,4,32,128]{3,2,1,0:T(8,128)(2,1)S(1)}, u32[]{:S(2)}, u32[]{:S(2)}) %collective-permute-start.3) | collective-permute-done | bytes 65568 | tf_op jit(solution)/shard_map/ppermute | solution.py:215
  13.5 0.5 %collective-permute-start.4 = (bf16[2,2,4,32,128]{4,3,2,1,0:T(8,128)(2,1)S(1)}, bf16[2,2,4,32,128]{4,3,2,1,0:T(8,128)(2,1)S(1)}, u32[]{:S(2)}, u32[]{:S(2)}) collective-permute-start(bf16[2,2,4,32,128]{4,3,2,1,0:T(8,128)(2,1)S(1)} %get-tuple-element.30), channel_id=1, source_target_pairs={{0,1},{1,0},{2,3},{3,2},{4,5},{5,4},{6,7},{7,6},{8,9},{9,8},{10,11... | collective-permute-start | bytes 393224 | tf_op jit(solution)/shard_map/ppermute | solution.py:302
  14.0 2.7 %collective-permute-start.5 = (bf16[2,2,4,32,128]{4,3,2,1,0:T(8,128)(2,1)S(1)}, bf16[2,2,4,32,128]{4,3,2,1,0:T(8,128)(2,1)S(1)}, u32[]{:S(2)}, u32[]{:S(2)}) collective-permute-start(bf16[2,2,4,32,128]{4,3,2,1,0:T(8,128)(2,1)S(1)} %get-tuple-element.31), channel_id=1, source_target_pairs={{0,4},{1,2},{2,1},{3,7},{4,0},{5,6},{6,5},{7,3},{8,12},{9,10},{10,... | collective-permute-start | bytes 393224 | tf_op jit(solution)/shard_map/ppermute | solution.py:302
  16.7 0.0 collective-permute-done.6.refs_0_.refs_3_
  16.7 0.0 collective-permute-done.7.refs_1_.refs_2_
  16.8 0.1 collective-permute-start.8
  16.8 2.6 %collective-permute-start.9 = (bf16[2,2,4,32,128]{4,3,2,1,0:T(8,128)(2,1)S(1)}, bf16[2,2,4,32,128]{4,3,2,1,0:T(8,128)(2,1)S(1)}, u32[]{:S(2)}, u32[]{:S(2)}) collective-permute-start(bf16[2,2,4,32,128]{4,3,2,1,0:T(8,128)(2,1)S(1)} %get-tuple-element.35), channel_id=1, source_target_pairs={{0,4},{1,2},{2,1},{3,7},{4,0},{5,6},{6,5},{7,3},{8,12},{9,10},{10,... | collective-permute-start | bytes 393224 | tf_op jit(solution)/shard_map/ppermute | solution.py:302
  19.5 0.1 far_pieces.1
  19.6 0.1 collective-permute-start.10
  19.6 0.2 kept_pieces.1.refs_5_
  19.8 0.1 collective-permute-done.4.refs_1_
  19.9 0.9 %collective-permute-done.5.refs_2_ = bf16[2,2,4,32,128]{4,3,2,1,0:T(8,128)(2,1)S(1)} collective-permute-done((bf16[2,2,4,32,128]{4,3,2,1,0:T(8,128)(2,1)S(1)}, bf16[2,2,4,32,128]{4,3,2,1,0:T(8,128)(2,1)S(1)}, u32[]{:S(2)}, u32[]{:S(2)}) %collective-permute-start.5) | collective-permute-done | bytes 131104 | tf_op jit(solution)/shard_map/ppermute | solution.py:302
  20.8 1.0 %collective-permute-done.8.refs_3_ = bf16[2,2,4,32,128]{4,3,2,1,0:T(8,128)(2,1)S(1)} collective-permute-done((bf16[2,2,4,32,128]{4,3,2,1,0:T(8,128)(2,1)S(1)}, bf16[2,2,4,32,128]{4,3,2,1,0:T(8,128)(2,1)S(1)}, u32[]{:S(2)}, u32[]{:S(2)}) %collective-permute-start.8) | collective-permute-done | bytes 131104 | tf_op jit(solution)/shard_map/ppermute | solution.py:302
  21.8 2.1 %collective-permute-done.9.refs_4_ = bf16[2,2,4,32,128]{4,3,2,1,0:T(8,128)(2,1)S(1)} collective-permute-done((bf16[2,2,4,32,128]{4,3,2,1,0:T(8,128)(2,1)S(1)}, bf16[2,2,4,32,128]{4,3,2,1,0:T(8,128)(2,1)S(1)}, u32[]{:S(2)}, u32[]{:S(2)}) %collective-permute-start.9) | collective-permute-done | bytes 131104 | tf_op jit(solution)/shard_map/ppermute | solution.py:302
  23.9 0.4 %blend_pieces.1.refs_0_ = f32[2,4,4,32,128]{4,3,2,1,0:T(8,128)S(1)} custom-call(bf16[2,4,4,16,128]{4,3,2,1,0:T(8,128)(2,1)S(1)} %get-tuple-element.24.refs_0_, bf16[2,2,4,32,128]{4,3,2,1,0:T(8,128)(2,1)S(1)} %collective-permute-done.4.refs_1_, bf16[2,2,4,32,128]{4,3,2,1,0:T(8,128)(2,1)S(1)} %collective-permute-done.5.refs_2_, ...), custom_call_target="tpu_custom_call" | custom-call | tf_op jit(solution)/shard_map/blend_pieces/pallas_call | solution.py:514
  24.2 1.2 %collective-permute-done.10.refs_2_ = bf16[2,2,4,32,128]{4,3,2,1,0:T(8,128)(2,1)S(1)} collective-permute-done((bf16[2,2,4,32,128]{4,3,2,1,0:T(8,128)(2,1)S(1)}, bf16[2,2,4,32,128]{4,3,2,1,0:T(8,128)(2,1)S(1)}, u32[]{:S(2)}, u32[]{:S(2)}) %collective-permute-start.10) | collective-permute-done | bytes 131104 | tf_op jit(solution)/shard_map/ppermute | solution.py:302
  25.5 0.8 %compose_frame.1 = f32[2,4,1,32,128]{4,3,2,1,0:T(8,128)} custom-call(f32[2,4,4,32,128]{4,3,2,1,0:T(8,128)S(1)} %blend_pieces.1.refs_0_, bf16[2,4,2,16,128]{4,3,2,1,0:T(8,128)(2,1)S(1)} %get-tuple-element.37.refs_1_, bf16[2,2,4,32,128]{4,3,2,1,0:T(8,128)(2,1)S(1)} %collective-permute-done.10.refs_2_), custom_call_target="tpu_custom_call" | custom-call | tf_op jit(solution)/shard_map/compose_frame/pallas_call | solution.py:570
  (2 shorter events, 0.1 us)
Async XLA Ops:
  0.0 8.2 %copy-start = (s32[2,4,1,1]{1,3,2,0:T(1,128)S(1)}, s32[2,4,1,1]{1,3,2,0:T(1,128)}, u32[]{:S(2)}) copy-start(s32[2,4,1,1]{1,3,2,0:T(1,128)} %param.8) | copy-start | bytes 100
  1.3 6.2 %collective-permute-start = (bf16[128,128]{1,0:T(8,128)(2,1)S(1)}, bf16[128,128]{1,0:T(8,128)(2,1)S(1)}, u32[]{:S(2)}, u32[]{:S(2)}) collective-permute-start(bf16[128,128]{1,0:T(8,128)(2,1)S(1)} %get-tuple-element.25.refs_0_), channel_id=1, source_target_pairs={{0,24},{8,16},{16,8},{24,0},{1,25},{9,17},{17,9},{25,1},{2,26},{10... | collective-permute-start | bytes 98312 | tf_op jit(solution)/shard_map/ppermute | solution.py:215
  3.8 3.9 %collective-permute-start.1 = (bf16[128,128]{1,0:T(8,128)(2,1)S(1)}, bf16[128,128]{1,0:T(8,128)(2,1)S(1)}, u32[]{:S(2)}, u32[]{:S(2)}) collective-permute-start(bf16[128,128]{1,0:T(8,128)(2,1)S(1)} %get-tuple-element.25.refs_0_), channel_id=1, source_target_pairs={{0,16},{8,24},{16,0},{24,8},{1,17},{9,25},{17,1},{25,9},{2,18},{10... | collective-permute-start | bytes 98312 | tf_op jit(solution)/shard_map/ppermute | solution.py:215
  4.3 3.9 %collective-permute-start.2 = (bf16[128,128]{1,0:T(8,128)(2,1)S(1)}, bf16[128,128]{1,0:T(8,128)(2,1)S(1)}, u32[]{:S(2)}, u32[]{:S(2)}) collective-permute-start(bf16[128,128]{1,0:T(8,128)(2,1)S(1)} %get-tuple-element.25.refs_0_), channel_id=1, source_target_pairs={{0,8},{8,0},{16,24},{24,16},{1,9},{9,1},{17,25},{25,17},{2,10},{10... | collective-permute-start | bytes 98312 | tf_op jit(solution)/shard_map/ppermute | solution.py:215
  4.8 7.6 %copy-start.1 = (s32[2,4,1,4]{3,2,1,0:T(1,128)S(1)}, s32[2,4,1,4]{3,2,1,0:T(1,128)}, u32[]{:S(2)}) copy-start(s32[2,4,1,4]{3,2,1,0:T(1,128)} %targets_ref.1) | copy-start | bytes 388
  4.8 7.6 %copy-start.2 = (s32[2,4]{1,0:T(2,128)S(1)}, s32[2,4]{1,0:T(2,128)}, u32[]{:S(2)}) copy-start(s32[2,4]{1,0:T(2,128)} %order_ref.1) | copy-start | bytes 100
  8.9 4.5 %collective-permute-start.3 = (bf16[2,4,32,128]{3,2,1,0:T(8,128)(2,1)S(1)}, bf16[2,4,32,128]{3,2,1,0:T(8,128)(2,1)S(1)}, u32[]{:S(2)}, u32[]{:S(2)}) collective-permute-start(bf16[2,4,32,128]{3,2,1,0:T(8,128)(2,1)S(1)} %get-tuple-element.27), channel_id=1, source_target_pairs={{0,8},{8,0},{16,24},{24,16},{1,9},{9,1},{17,25},{25,17},{2,10},{10... | collective-permute-start | bytes 196616 | tf_op jit(solution)/shard_map/ppermute | solution.py:215
  9.8 6.9 %collective-permute-start.6 = (bf16[2,4,32,128]{3,2,1,0:T(8,128)(2,1)S(1)}, bf16[2,4,32,128]{3,2,1,0:T(8,128)(2,1)S(1)}, u32[]{:S(2)}, u32[]{:S(2)}) collective-permute-start(bf16[2,4,32,128]{3,2,1,0:T(8,128)(2,1)S(1)} %get-tuple-element.32), channel_id=1, source_target_pairs={{0,24},{8,16},{16,8},{24,0},{1,25},{9,17},{17,9},{25,1},{2,26},{10... | collective-permute-start | bytes 196616 | tf_op jit(solution)/shard_map/ppermute | solution.py:215
  12.0 4.8 %collective-permute-start.7 = (bf16[2,4,32,128]{3,2,1,0:T(8,128)(2,1)S(1)}, bf16[2,4,32,128]{3,2,1,0:T(8,128)(2,1)S(1)}, u32[]{:S(2)}, u32[]{:S(2)}) collective-permute-start(bf16[2,4,32,128]{3,2,1,0:T(8,128)(2,1)S(1)} %get-tuple-element.33), channel_id=1, source_target_pairs={{0,16},{8,24},{16,0},{24,8},{1,17},{9,25},{17,1},{25,9},{2,18},{10... | collective-permute-start | bytes 196616 | tf_op jit(solution)/shard_map/ppermute | solution.py:215
  13.5 6.4 %collective-permute-start.4 = (bf16[2,2,4,32,128]{4,3,2,1,0:T(8,128)(2,1)S(1)}, bf16[2,2,4,32,128]{4,3,2,1,0:T(8,128)(2,1)S(1)}, u32[]{:S(2)}, u32[]{:S(2)}) collective-permute-start(bf16[2,2,4,32,128]{4,3,2,1,0:T(8,128)(2,1)S(1)} %get-tuple-element.30), channel_id=1, source_target_pairs={{0,1},{1,0},{2,3},{3,2},{4,5},{5,4},{6,7},{7,6},{8,9},{9,8},{10,11... | collective-permute-start | bytes 393224 | tf_op jit(solution)/shard_map/ppermute | solution.py:302
  14.0 6.8 %collective-permute-start.5 = (bf16[2,2,4,32,128]{4,3,2,1,0:T(8,128)(2,1)S(1)}, bf16[2,2,4,32,128]{4,3,2,1,0:T(8,128)(2,1)S(1)}, u32[]{:S(2)}, u32[]{:S(2)}) collective-permute-start(bf16[2,2,4,32,128]{4,3,2,1,0:T(8,128)(2,1)S(1)} %get-tuple-element.31), channel_id=1, source_target_pairs={{0,4},{1,2},{2,1},{3,7},{4,0},{5,6},{6,5},{7,3},{8,12},{9,10},{10,... | collective-permute-start | bytes 393224 | tf_op jit(solution)/shard_map/ppermute | solution.py:302
  16.8 5.0 %collective-permute-start.8 = (bf16[2,2,4,32,128]{4,3,2,1,0:T(8,128)(2,1)S(1)}, bf16[2,2,4,32,128]{4,3,2,1,0:T(8,128)(2,1)S(1)}, u32[]{:S(2)}, u32[]{:S(2)}) collective-permute-start(bf16[2,2,4,32,128]{4,3,2,1,0:T(8,128)(2,1)S(1)} %get-tuple-element.34), channel_id=1, source_target_pairs={{0,1},{1,0},{2,3},{3,2},{4,5},{5,4},{6,7},{7,6},{8,9},{9,8},{10,11... | collective-permute-start | bytes 393224 | tf_op jit(solution)/shard_map/ppermute | solution.py:302
  16.8 7.0 %collective-permute-start.9 = (bf16[2,2,4,32,128]{4,3,2,1,0:T(8,128)(2,1)S(1)}, bf16[2,2,4,32,128]{4,3,2,1,0:T(8,128)(2,1)S(1)}, u32[]{:S(2)}, u32[]{:S(2)}) collective-permute-start(bf16[2,2,4,32,128]{4,3,2,1,0:T(8,128)(2,1)S(1)} %get-tuple-element.35), channel_id=1, source_target_pairs={{0,4},{1,2},{2,1},{3,7},{4,0},{5,6},{6,5},{7,3},{8,12},{9,10},{10,... | collective-permute-start | bytes 393224 | tf_op jit(solution)/shard_map/ppermute | solution.py:302
  19.6 5.9 %collective-permute-start.10 = (bf16[2,2,4,32,128]{4,3,2,1,0:T(8,128)(2,1)S(1)}, bf16[2,2,4,32,128]{4,3,2,1,0:T(8,128)(2,1)S(1)}, u32[]{:S(2)}, u32[]{:S(2)}) collective-permute-start(bf16[2,2,4,32,128]{4,3,2,1,0:T(8,128)(2,1)S(1)} %far_pieces.1), channel_id=1, source_target_pairs={{0,4},{1,3},{2,6},{3,1},{4,0},{5,7},{6,2},{7,5},{8,12},{9,11},{10,... | collective-permute-start | bytes 393224 | tf_op jit(solution)/shard_map/ppermute | solution.py:302

commit v6 on v5

--- a/solution.py
+++ b/solution.py
@@ -407,7 +407,7 @@
 
 
 def near_kernel(chosen, outs_count, *refs):
-    blocks, masks, outs = refs[: len(chosen)], refs[len(chosen) : -outs_count], refs[-outs_count:]
+    blocks, masks, outs = refs[: len(chosen)], refs[len(chosen) : -outs_count - 1], refs[-outs_count:]
     for mask_ref, out in zip(masks, outs, strict=True):
         views, _, channels, strip, _ = out.shape
         for v in range(views):
@@ -419,17 +419,17 @@
                         out[v, i, c, rows] = blocks[i][v, c, rows] * mask
 
 
-def near_pieces(blocks, masks, chosen, name):
+def near_pieces(blocks, masks, chosen, name, after):
     views, channels, strip, cols = blocks[0].shape
     vmem = pl.BlockSpec(memory_space=pltpu.VMEM)
     return pl.pallas_call(
         functools.partial(near_kernel, chosen, len(masks)),
-        in_specs=[vmem] * (len(blocks) + len(masks)),
+        in_specs=[vmem] * (len(blocks) + len(masks)) + [pl.BlockSpec(memory_space=pl.ANY)],
         out_specs=[vmem] * len(masks),
         out_shape=[jax.ShapeDtypeStruct((views, len(chosen), channels, strip, cols), jnp.bfloat16) for _ in masks],
         compiler_params=pltpu.CompilerParams(vmem_limit_bytes=VMEM_BYTES),
         name=name,
-    )(*blocks, *masks)
+    )(*blocks, *masks, after)
 
 
 def pack_kernel(slabs, outs_count, *refs):
@@ -600,14 +600,16 @@
     blocks = {0: strips[0]} | {k: swap_depth(strips[k], k, slabs) for k in range(1, slabs)}
     given = {("order",): masks[-1]}
     given |= {("take", step): mask for step, mask in zip(far_steps, masks[len(far) :], strict=False)}
+    after = strips[0]
     for name, chosen in (("early", tuple(range(max(1, slabs // 2)))), ("late", tuple(range(slabs - 1, max(1, slabs // 2) - 1, -1)))):
-        pieces = near_pieces([blocks[k] for k in chosen], near_masks, chosen, "near_pieces_" + name)
+        if name == "late" and far:
+            for (step, parity, lefts), piece in zip(far, packed_pieces([blocks[k] for k in range(slabs)], masks[: len(far)], "far_pieces"), strict=True):
+                given["far", step, parity] = swap_columns(piece, step, lefts, slabs, columns)
+                after = piece
+        pieces = near_pieces([blocks[k] for k in chosen], near_masks, chosen, "near_pieces_" + name, after)
         for (step, parity, lefts), piece in zip(near, pieces, strict=True):
             given["near", parity, chosen] = swap_columns(piece, step, lefts, slabs, columns)
     blocks = [blocks[k] for k in range(slabs)]
-    if far:
-        for (step, parity, lefts), piece in zip(far, packed_pieces(blocks, masks[: len(far)], "far_pieces"), strict=True):
-            given["far", step, parity] = swap_columns(piece, step, lefts, slabs, columns)
     (given["own",],) = packed_pieces(blocks, masks[-2:-1], "kept_pieces")
     nears = {key: value for key, value in given.items() if key[0] in ("order", "near", "own")}
     fars = {key: value for key, value in given.items() if key not in nears}

time: 26.4 us -> 26.4 us (level)
  no operation moved by 1% of the time
where the time goes in v6:
time: 26.4 us; the launch traced here: 26.2 us
  starting transfers between devices  13 us (49%)
  Pallas kernels  6.66 us (25%)
  waiting for transfers between devices  6.41 us (24%)
    ppermute x6, starting transfers between devices, swap_depth(): lax.ppermute(value, 'depth', [(i, int(partner(i, k, count)) if count & co...  7.11 us
    ppermute x5, starting transfers between devices, swap_columns(): return lax.ppermute(value, ('depth', 'row', 'col'), pairs)  5.94 us
    ppermute x5, waiting for transfers between devices, swap_columns(): return lax.ppermute(value, ('depth', 'row', 'col'), pairs)  5.33 us
    pallas_call x1, Pallas kernels, image_sums(): pl.pallas_call(functools.partial(sums_kernel, 16, min(rows, 128)), in_spe...  2.64 us
    pallas_call x1, Pallas kernels, slab_code(): pl.pallas_call(functools.partial(plane_kernel, parts), in_specs=[pl.Block...  1.27 us
    ppermute x6, waiting for transfers between devices, swap_depth(): lax.ppermute(value, 'depth', [(i, int(partner(i, k, count)) if count & co...  1.08 us
    pallas_call x2, Pallas kernels, lit_strips(): pl.pallas_call(functools.partial(lit_kernel, slabs, depth_cells, chosen),...  1.07 us
    pallas_call x1, Pallas kernels, composed_frame(): pl.pallas_call(functools.partial(frame_kernel, list(given)), in_specs=[vm...  0.78 us
  transfers between devices with their start and end apart: 11, of which 8 were waited for; matrix products, arithmetic and copies ran while one was open for 0% of the time, Pallas kernels for 15%

profile of v6, /device:TPU:8, one launch (start us, length us, event | category | flops | bytes accessed | tf_op | source)
XLA Modules:
  0.0 26.2 jit_solution(6167079052255357492)
XLA Ops:
  0.0 0.0 copy-start
  0.0 1.3 %slab_code.1 = (bf16[128,128]{1,0:T(8,128)(2,1)S(1)}, f32[16,128,128]{2,1,0:T(8,128)S(1)}) custom-call(f32[16,128,128]{2,1,0:T(8,128)} %density_hbm.1), custom_call_target="tpu_custom_call" | custom-call | tf_op jit(solution)/shard_map/slab_code/pallas_call | solution.py:68
  1.3 2.5 %collective-permute-start = (bf16[128,128]{1,0:T(8,128)(2,1)S(1)}, bf16[128,128]{1,0:T(8,128)(2,1)S(1)}, u32[]{:S(2)}, u32[]{:S(2)}) collective-permute-start(bf16[128,128]{1,0:T(8,128)(2,1)S(1)} %get-tuple-element.25.refs_0_), channel_id=1, source_target_pairs={{0,24},{8,16},{16,8},{24,0},{1,25},{9,17},{17,9},{25,1},{2,26},{10... | collective-permute-start | bytes 98312 | tf_op jit(solution)/shard_map/ppermute | solution.py:215
  3.8 0.5 %collective-permute-start.1 = (bf16[128,128]{1,0:T(8,128)(2,1)S(1)}, bf16[128,128]{1,0:T(8,128)(2,1)S(1)}, u32[]{:S(2)}, u32[]{:S(2)}) collective-permute-start(bf16[128,128]{1,0:T(8,128)(2,1)S(1)} %get-tuple-element.25.refs_0_), channel_id=1, source_target_pairs={{0,16},{8,24},{16,0},{24,8},{1,17},{9,25},{17,1},{25,9},{2,18},{10... | collective-permute-start | bytes 98312 | tf_op jit(solution)/shard_map/ppermute | solution.py:215
  4.3 0.5 %collective-permute-start.2 = (bf16[128,128]{1,0:T(8,128)(2,1)S(1)}, bf16[128,128]{1,0:T(8,128)(2,1)S(1)}, u32[]{:S(2)}, u32[]{:S(2)}) collective-permute-start(bf16[128,128]{1,0:T(8,128)(2,1)S(1)} %get-tuple-element.25.refs_0_), channel_id=1, source_target_pairs={{0,8},{8,0},{16,24},{24,16},{1,9},{9,1},{17,25},{25,17},{2,10},{10... | collective-permute-start | bytes 98312 | tf_op jit(solution)/shard_map/ppermute | solution.py:215
  4.8 0.0 copy-start.1
  4.8 0.0 copy-start.2
  4.8 2.6 %image_sums.1 = (f32[42,128,128]{2,1,0:T(8,128)S(1)}, bf16[2,128,128]{2,1,0:T(8,128)(2,1)S(1)}) custom-call(f32[16,128,128]{2,1,0:T(8,128)S(1)} %get-tuple-element.22.density_ref, bf16[3,16,128,128]{3,2,1,0:T(8,128)(2,1)} %albedo_hbm.1), custom_call_target="tpu_custom_call" | custom-call | flops 15728640 | bytes 5373952 | tf_op jit(solution)/shard_map/image_sums/pallas_call | solution.py:185
  7.5 0.0 collective-permute-done.refs_1_
  7.5 0.2 collective-permute-done.1.refs_2_
  7.7 0.5 %collective-permute-done.2.refs_3_ = bf16[128,128]{1,0:T(8,128)(2,1)S(1)} collective-permute-done((bf16[128,128]{1,0:T(8,128)(2,1)S(1)}, bf16[128,128]{1,0:T(8,128)(2,1)S(1)}, u32[]{:S(2)}, u32[]{:S(2)}) %collective-permute-start.2) | collective-permute-done | bytes 32800 | tf_op jit(solution)/shard_map/ppermute | solution.py:215
  8.2 0.0 copy-done
  8.2 0.7 %lit_strips_123.1 = (bf16[2,4,32,128]{3,2,1,0:T(8,128)(2,1)S(1)}, bf16[2,4,32,128]{3,2,1,0:T(8,128)(2,1)S(1)}, bf16[2,4,32,128]{3,2,1,0:T(8,128)(2,1)S(1)}) custom-call(s32[2,4]{1,0:T(2,128)S(1)} %bitcast.1, s32[2,4]{1,0:T(2,128)S(1)} %bitcast.2, bf16[128,128]{1,0:T(8,128)(2,1)S(1)} %get-tuple-element.25.refs_0_, ...), custom_call_target="tpu_custom_call" | custom-call | tf_op jit(solution)/shard_map/lit_strips_123/pallas_call | solution.py:265
  8.9 0.9 %collective-permute-start.3 = (bf16[2,4,32,128]{3,2,1,0:T(8,128)(2,1)S(1)}, bf16[2,4,32,128]{3,2,1,0:T(8,128)(2,1)S(1)}, u32[]{:S(2)}, u32[]{:S(2)}) collective-permute-start(bf16[2,4,32,128]{3,2,1,0:T(8,128)(2,1)S(1)} %get-tuple-element.27), channel_id=1, source_target_pairs={{0,8},{8,0},{16,24},{24,16},{1,9},{9,1},{17,25},{25,17},{2,10},{10... | collective-permute-start | bytes 196616 | tf_op jit(solution)/shard_map/ppermute | solution.py:215
  9.8 2.2 %collective-permute-start.6 = (bf16[2,4,32,128]{3,2,1,0:T(8,128)(2,1)S(1)}, bf16[2,4,32,128]{3,2,1,0:T(8,128)(2,1)S(1)}, u32[]{:S(2)}, u32[]{:S(2)}) collective-permute-start(bf16[2,4,32,128]{3,2,1,0:T(8,128)(2,1)S(1)} %get-tuple-element.32), channel_id=1, source_target_pairs={{0,24},{8,16},{16,8},{24,0},{1,25},{9,17},{17,9},{25,1},{2,26},{10... | collective-permute-start | bytes 196616 | tf_op jit(solution)/shard_map/ppermute | solution.py:215
  12.0 0.5 %collective-permute-start.7 = (bf16[2,4,32,128]{3,2,1,0:T(8,128)(2,1)S(1)}, bf16[2,4,32,128]{3,2,1,0:T(8,128)(2,1)S(1)}, u32[]{:S(2)}, u32[]{:S(2)}) collective-permute-start(bf16[2,4,32,128]{3,2,1,0:T(8,128)(2,1)S(1)} %get-tuple-element.33), channel_id=1, source_target_pairs={{0,16},{8,24},{16,0},{24,8},{1,17},{9,25},{17,1},{25,9},{2,18},{10... | collective-permute-start | bytes 196616 | tf_op jit(solution)/shard_map/ppermute | solution.py:215
  12.5 0.0 copy-done.1
  12.5 0.0 copy-done.2
  12.5 0.2 piece_plans.1
  12.7 0.4 %lit_strips_0.1.refs_0_.refs_4_ = bf16[2,4,32,128]{3,2,1,0:T(8,128)(2,1)S(1)} custom-call(s32[2,4]{1,0:T(2,128)S(1)} %bitcast.4, s32[2,4]{1,0:T(2,128)S(1)} %bitcast.5, bf16[128,128]{1,0:T(8,128)(2,1)S(1)} %get-tuple-element.25.refs_0_, bf16[128,128]{1,0:T(8,128)(2,1)S(1)} %collective-permute-done.refs_1_, ...), custom_call_target="tpu_custom_call" | custom-call | tf_op jit(solution)/shard_map/lit_strips_0/pallas_call | solution.py:265
  13.1 0.4 %collective-permute-done.3.refs_1_ = bf16[2,4,32,128]{3,2,1,0:T(8,128)(2,1)S(1)} collective-permute-done((bf16[2,4,32,128]{3,2,1,0:T(8,128)(2,1)S(1)}, bf16[2,4,32,128]{3,2,1,0:T(8,128)(2,1)S(1)}, u32[]{:S(2)}, u32[]{:S(2)}) %collective-permute-start.3) | collective-permute-done | bytes 65568 | tf_op jit(solution)/shard_map/ppermute | solution.py:215
  13.5 0.5 %collective-permute-start.4 = (bf16[2,2,4,32,128]{4,3,2,1,0:T(8,128)(2,1)S(1)}, bf16[2,2,4,32,128]{4,3,2,1,0:T(8,128)(2,1)S(1)}, u32[]{:S(2)}, u32[]{:S(2)}) collective-permute-start(bf16[2,2,4,32,128]{4,3,2,1,0:T(8,128)(2,1)S(1)} %get-tuple-element.30), channel_id=1, source_target_pairs={{0,1},{1,0},{2,3},{3,2},{4,5},{5,4},{6,7},{7,6},{8,9},{9,8},{10,11... | collective-permute-start | bytes 393224 | tf_op jit(solution)/shard_map/ppermute | solution.py:302
  14.0 2.7 %collective-permute-start.5 = (bf16[2,2,4,32,128]{4,3,2,1,0:T(8,128)(2,1)S(1)}, bf16[2,2,4,32,128]{4,3,2,1,0:T(8,128)(2,1)S(1)}, u32[]{:S(2)}, u32[]{:S(2)}) collective-permute-start(bf16[2,2,4,32,128]{4,3,2,1,0:T(8,128)(2,1)S(1)} %get-tuple-element.31), channel_id=1, source_target_pairs={{0,4},{1,2},{2,1},{3,7},{4,0},{5,6},{6,5},{7,3},{8,12},{9,10},{10,... | collective-permute-start | bytes 393224 | tf_op jit(solution)/shard_map/ppermute | solution.py:302
  16.7 0.0 collective-permute-done.6.refs_3_.refs_0_
  16.7 0.0 collective-permute-done.7.refs_2_.refs_1_
  16.7 0.1 far_pieces.1.refs_4_
  16.8 0.1 collective-permute-start.8
  16.9 2.6 %collective-permute-start.9 = (bf16[2,2,4,32,128]{4,3,2,1,0:T(8,128)(2,1)S(1)}, bf16[2,2,4,32,128]{4,3,2,1,0:T(8,128)(2,1)S(1)}, u32[]{:S(2)}, u32[]{:S(2)}) collective-permute-start(bf16[2,2,4,32,128]{4,3,2,1,0:T(8,128)(2,1)S(1)} %get-tuple-element.36), channel_id=1, source_target_pairs={{0,4},{1,2},{2,1},{3,7},{4,0},{5,6},{6,5},{7,3},{8,12},{9,10},{10,... | collective-permute-start | bytes 393224 | tf_op jit(solution)/shard_map/ppermute | solution.py:302
  19.6 0.0 collective-permute-start.10
  19.6 0.2 kept_pieces.1.refs_5_
  19.7 0.2 collective-permute-done.4.refs_1_
  19.9 0.9 %collective-permute-done.5.refs_2_ = bf16[2,2,4,32,128]{4,3,2,1,0:T(8,128)(2,1)S(1)} collective-permute-done((bf16[2,2,4,32,128]{4,3,2,1,0:T(8,128)(2,1)S(1)}, bf16[2,2,4,32,128]{4,3,2,1,0:T(8,128)(2,1)S(1)}, u32[]{:S(2)}, u32[]{:S(2)}) %collective-permute-start.5) | collective-permute-done | bytes 131104 | tf_op jit(solution)/shard_map/ppermute | solution.py:302
  20.8 1.1 %collective-permute-done.8.refs_3_ = bf16[2,2,4,32,128]{4,3,2,1,0:T(8,128)(2,1)S(1)} collective-permute-done((bf16[2,2,4,32,128]{4,3,2,1,0:T(8,128)(2,1)S(1)}, bf16[2,2,4,32,128]{4,3,2,1,0:T(8,128)(2,1)S(1)}, u32[]{:S(2)}, u32[]{:S(2)}) %collective-permute-start.8) | collective-permute-done | bytes 131104 | tf_op jit(solution)/shard_map/ppermute | solution.py:302
  21.9 2.0 %collective-permute-done.9.refs_4_ = bf16[2,2,4,32,128]{4,3,2,1,0:T(8,128)(2,1)S(1)} collective-permute-done((bf16[2,2,4,32,128]{4,3,2,1,0:T(8,128)(2,1)S(1)}, bf16[2,2,4,32,128]{4,3,2,1,0:T(8,128)(2,1)S(1)}, u32[]{:S(2)}, u32[]{:S(2)}) %collective-permute-start.9) | collective-permute-done | bytes 131104 | tf_op jit(solution)/shard_map/ppermute | solution.py:302
  23.9 0.4 %blend_pieces.1.refs_0_ = f32[2,4,4,32,128]{4,3,2,1,0:T(8,128)S(1)} custom-call(bf16[2,4,4,16,128]{4,3,2,1,0:T(8,128)(2,1)S(1)} %get-tuple-element.24.refs_0_, bf16[2,2,4,32,128]{4,3,2,1,0:T(8,128)(2,1)S(1)} %collective-permute-done.4.refs_1_, bf16[2,2,4,32,128]{4,3,2,1,0:T(8,128)(2,1)S(1)} %collective-permute-done.5.refs_2_, ...), custom_call_target="tpu_custom_call" | custom-call | tf_op jit(solution)/shard_map/blend_pieces/pallas_call | solution.py:514
  24.2 1.2 %collective-permute-done.10.refs_2_ = bf16[2,2,4,32,128]{4,3,2,1,0:T(8,128)(2,1)S(1)} collective-permute-done((bf16[2,2,4,32,128]{4,3,2,1,0:T(8,128)(2,1)S(1)}, bf16[2,2,4,32,128]{4,3,2,1,0:T(8,128)(2,1)S(1)}, u32[]{:S(2)}, u32[]{:S(2)}) %collective-permute-start.10) | collective-permute-done | bytes 131104 | tf_op jit(solution)/shard_map/ppermute | solution.py:302
  25.4 0.8 %compose_frame.1 = f32[2,4,1,32,128]{4,3,2,1,0:T(8,128)} custom-call(f32[2,4,4,32,128]{4,3,2,1,0:T(8,128)S(1)} %blend_pieces.1.refs_0_, bf16[2,4,2,16,128]{4,3,2,1,0:T(8,128)(2,1)S(1)} %get-tuple-element.38.refs_1_, bf16[2,2,4,32,128]{4,3,2,1,0:T(8,128)(2,1)S(1)} %collective-permute-done.10.refs_2_), custom_call_target="tpu_custom_call" | custom-call | tf_op jit(solution)/shard_map/compose_frame/pallas_call | solution.py:570
  (2 shorter events, 0.1 us)
Async XLA Ops:
  0.0 8.2 %copy-start = (s32[2,4,1,1]{1,3,2,0:T(1,128)S(1)}, s32[2,4,1,1]{1,3,2,0:T(1,128)}, u32[]{:S(2)}) copy-start(s32[2,4,1,1]{1,3,2,0:T(1,128)} %param.8) | copy-start | bytes 100
  1.3 6.2 %collective-permute-start = (bf16[128,128]{1,0:T(8,128)(2,1)S(1)}, bf16[128,128]{1,0:T(8,128)(2,1)S(1)}, u32[]{:S(2)}, u32[]{:S(2)}) collective-permute-start(bf16[128,128]{1,0:T(8,128)(2,1)S(1)} %get-tuple-element.25.refs_0_), channel_id=1, source_target_pairs={{0,24},{8,16},{16,8},{24,0},{1,25},{9,17},{17,9},{25,1},{2,26},{10... | collective-permute-start | bytes 98312 | tf_op jit(solution)/shard_map/ppermute | solution.py:215
  3.8 3.9 %collective-permute-start.1 = (bf16[128,128]{1,0:T(8,128)(2,1)S(1)}, bf16[128,128]{1,0:T(8,128)(2,1)S(1)}, u32[]{:S(2)}, u32[]{:S(2)}) collective-permute-start(bf16[128,128]{1,0:T(8,128)(2,1)S(1)} %get-tuple-element.25.refs_0_), channel_id=1, source_target_pairs={{0,16},{8,24},{16,0},{24,8},{1,17},{9,25},{17,1},{25,9},{2,18},{10... | collective-permute-start | bytes 98312 | tf_op jit(solution)/shard_map/ppermute | solution.py:215
  4.3 3.9 %collective-permute-start.2 = (bf16[128,128]{1,0:T(8,128)(2,1)S(1)}, bf16[128,128]{1,0:T(8,128)(2,1)S(1)}, u32[]{:S(2)}, u32[]{:S(2)}) collective-permute-start(bf16[128,128]{1,0:T(8,128)(2,1)S(1)} %get-tuple-element.25.refs_0_), channel_id=1, source_target_pairs={{0,8},{8,0},{16,24},{24,16},{1,9},{9,1},{17,25},{25,17},{2,10},{10... | collective-permute-start | bytes 98312 | tf_op jit(solution)/shard_map/ppermute | solution.py:215
  4.8 7.6 %copy-start.1 = (s32[2,4,1,4]{3,2,1,0:T(1,128)S(1)}, s32[2,4,1,4]{3,2,1,0:T(1,128)}, u32[]{:S(2)}) copy-start(s32[2,4,1,4]{3,2,1,0:T(1,128)} %targets_ref.1) | copy-start | bytes 388
  4.8 7.6 %copy-start.2 = (s32[2,4]{1,0:T(2,128)S(1)}, s32[2,4]{1,0:T(2,128)}, u32[]{:S(2)}) copy-start(s32[2,4]{1,0:T(2,128)} %order_ref.1) | copy-start | bytes 100
  8.9 4.5 %collective-permute-start.3 = (bf16[2,4,32,128]{3,2,1,0:T(8,128)(2,1)S(1)}, bf16[2,4,32,128]{3,2,1,0:T(8,128)(2,1)S(1)}, u32[]{:S(2)}, u32[]{:S(2)}) collective-permute-start(bf16[2,4,32,128]{3,2,1,0:T(8,128)(2,1)S(1)} %get-tuple-element.27), channel_id=1, source_target_pairs={{0,8},{8,0},{16,24},{24,16},{1,9},{9,1},{17,25},{25,17},{2,10},{10... | collective-permute-start | bytes 196616 | tf_op jit(solution)/shard_map/ppermute | solution.py:215
  9.8 6.9 %collective-permute-start.6 = (bf16[2,4,32,128]{3,2,1,0:T(8,128)(2,1)S(1)}, bf16[2,4,32,128]{3,2,1,0:T(8,128)(2,1)S(1)}, u32[]{:S(2)}, u32[]{:S(2)}) collective-permute-start(bf16[2,4,32,128]{3,2,1,0:T(8,128)(2,1)S(1)} %get-tuple-element.32), channel_id=1, source_target_pairs={{0,24},{8,16},{16,8},{24,0},{1,25},{9,17},{17,9},{25,1},{2,26},{10... | collective-permute-start | bytes 196616 | tf_op jit(solution)/shard_map/ppermute | solution.py:215
  12.0 4.8 %collective-permute-start.7 = (bf16[2,4,32,128]{3,2,1,0:T(8,128)(2,1)S(1)}, bf16[2,4,32,128]{3,2,1,0:T(8,128)(2,1)S(1)}, u32[]{:S(2)}, u32[]{:S(2)}) collective-permute-start(bf16[2,4,32,128]{3,2,1,0:T(8,128)(2,1)S(1)} %get-tuple-element.33), channel_id=1, source_target_pairs={{0,16},{8,24},{16,0},{24,8},{1,17},{9,25},{17,1},{25,9},{2,18},{10... | collective-permute-start | bytes 196616 | tf_op jit(solution)/shard_map/ppermute | solution.py:215
  13.5 6.4 %collective-permute-start.4 = (bf16[2,2,4,32,128]{4,3,2,1,0:T(8,128)(2,1)S(1)}, bf16[2,2,4,32,128]{4,3,2,1,0:T(8,128)(2,1)S(1)}, u32[]{:S(2)}, u32[]{:S(2)}) collective-permute-start(bf16[2,2,4,32,128]{4,3,2,1,0:T(8,128)(2,1)S(1)} %get-tuple-element.30), channel_id=1, source_target_pairs={{0,1},{1,0},{2,3},{3,2},{4,5},{5,4},{6,7},{7,6},{8,9},{9,8},{10,11... | collective-permute-start | bytes 393224 | tf_op jit(solution)/shard_map/ppermute | solution.py:302
  14.0 6.8 %collective-permute-start.5 = (bf16[2,2,4,32,128]{4,3,2,1,0:T(8,128)(2,1)S(1)}, bf16[2,2,4,32,128]{4,3,2,1,0:T(8,128)(2,1)S(1)}, u32[]{:S(2)}, u32[]{:S(2)}) collective-permute-start(bf16[2,2,4,32,128]{4,3,2,1,0:T(8,128)(2,1)S(1)} %get-tuple-element.31), channel_id=1, source_target_pairs={{0,4},{1,2},{2,1},{3,7},{4,0},{5,6},{6,5},{7,3},{8,12},{9,10},{10,... | collective-permute-start | bytes 393224 | tf_op jit(solution)/shard_map/ppermute | solution.py:302
  16.8 5.0 %collective-permute-start.8 = (bf16[2,2,4,32,128]{4,3,2,1,0:T(8,128)(2,1)S(1)}, bf16[2,2,4,32,128]{4,3,2,1,0:T(8,128)(2,1)S(1)}, u32[]{:S(2)}, u32[]{:S(2)}) collective-permute-start(bf16[2,2,4,32,128]{4,3,2,1,0:T(8,128)(2,1)S(1)} %get-tuple-element.35), channel_id=1, source_target_pairs={{0,1},{1,0},{2,3},{3,2},{4,5},{5,4},{6,7},{7,6},{8,9},{9,8},{10,11... | collective-permute-start | bytes 393224 | tf_op jit(solution)/shard_map/ppermute | solution.py:302
  16.9 6.9 %collective-permute-start.9 = (bf16[2,2,4,32,128]{4,3,2,1,0:T(8,128)(2,1)S(1)}, bf16[2,2,4,32,128]{4,3,2,1,0:T(8,128)(2,1)S(1)}, u32[]{:S(2)}, u32[]{:S(2)}) collective-permute-start(bf16[2,2,4,32,128]{4,3,2,1,0:T(8,128)(2,1)S(1)} %get-tuple-element.36), channel_id=1, source_target_pairs={{0,4},{1,2},{2,1},{3,7},{4,0},{5,6},{6,5},{7,3},{8,12},{9,10},{10,... | collective-permute-start | bytes 393224 | tf_op jit(solution)/shard_map/ppermute | solution.py:302
  19.6 5.9 %collective-permute-start.10 = (bf16[2,2,4,32,128]{4,3,2,1,0:T(8,128)(2,1)S(1)}, bf16[2,2,4,32,128]{4,3,2,1,0:T(8,128)(2,1)S(1)}, u32[]{:S(2)}, u32[]{:S(2)}) collective-permute-start(bf16[2,2,4,32,128]{4,3,2,1,0:T(8,128)(2,1)S(1)} %far_pieces.1.refs_4_), channel_id=1, source_target_pairs={{0,4},{1,3},{2,6},{3,1},{4,0},{5,7},{6,2},{7,5},{8,12},{9,11},{10,... | collective-permute-start | bytes 393224 | tf_op jit(solution)/shard_map/ppermute | solution.py:302

commit v7 on v5

--- a/solution.py
+++ b/solution.py
@@ -477,6 +477,8 @@
     def by_strip(groups, v, p, c, rows):
         total = None
         for chosen, ref in groups:
+            if not chosen:
+                total = ref[v, p, c, rows] if total is None else total + ref[v, p, c, rows]
             for i, k in enumerate(chosen):
                 term = ref[v, i, c, rows] * order_ref[v, p, k]
                 total = term if total is None else total + term
@@ -506,6 +508,32 @@
 
     for phase in range(2):
         pl.when(lax.rem(tile, 2) == phase)(functools.partial(blend, near[(phase - 1) % 2], near[phase]))
+
+
+def ordered_kernel(chosen, order_ref, piece_ref, out):
+    views, slabs, channels, strip, _ = out.shape
+    for v in range(views):
+        for p in range(slabs):
+            for c in range(channels):
+                for row in range(0, strip, 16):
+                    rows = pl.ds(row, 16)
+                    total = piece_ref[v, 0, c, rows] * order_ref[v, p, chosen[0]]
+                    for i, k in list(enumerate(chosen))[1:]:
+                        total = total + piece_ref[v, i, c, rows] * order_ref[v, p, k]
+                    out[v, p, c, rows] = total
+
+
+def ordered_pieces(order, piece, chosen):
+    views, _, channels, strip, cols = piece.shape
+    vmem = pl.BlockSpec(memory_space=pltpu.VMEM)
+    return pl.pallas_call(
+        functools.partial(ordered_kernel, chosen),
+        in_specs=[vmem, vmem],
+        out_specs=vmem,
+        out_shape=pltpu.VMEM((views, order.shape[1], channels, strip, cols), jnp.bfloat16),
+        compiler_params=pltpu.CompilerParams(vmem_limit_bytes=VMEM_BYTES),
+        name="ordered_pieces",
+    )(order, piece)
 
 
 def blended_pieces(given, slabs):
@@ -611,6 +639,13 @@
     (given["own",],) = packed_pieces(blocks, masks[-2:-1], "kept_pieces")
     nears = {key: value for key, value in given.items() if key[0] in ("order", "near", "own")}
     fars = {key: value for key, value in given.items() if key not in nears}
+    early = tuple(range(max(1, slabs // 2)))
+    nears = {
+        (("near", key[1], ()) if key[0] == "near" and key[2] == early else key): (
+            ordered_pieces(given["order",], value, early) if key[0] == "near" and key[2] == early else value
+        )
+        for key, value in nears.items()
+    }
     return composed_frame(blended_pieces(nears, slabs), fars)
 
 

time: 26.4 us -> 26.4 us (level)
  no operation moved by 1% of the time
where the time goes in v7:
time: 26.4 us; the launch traced here: 26.3 us
  starting transfers between devices  13.1 us (50%)
  Pallas kernels  6.66 us (25%)
  waiting for transfers between devices  6.39 us (24%)
    ppermute x6, starting transfers between devices, swap_depth(): lax.ppermute(value, 'depth', [(i, int(partner(i, k, count)) if count & co...  7.11 us
    ppermute x5, starting transfers between devices, swap_columns(): return lax.ppermute(value, ('depth', 'row', 'col'), pairs)  6 us
    ppermute x5, waiting for transfers between devices, swap_columns(): return lax.ppermute(value, ('depth', 'row', 'col'), pairs)  5.3 us
    pallas_call x1, Pallas kernels, image_sums(): pl.pallas_call(functools.partial(sums_kernel, 16, min(rows, 128)), in_spe...  2.64 us
    pallas_call x1, Pallas kernels, slab_code(): pl.pallas_call(functools.partial(plane_kernel, parts), in_specs=[pl.Block...  1.27 us
    ppermute x6, waiting for transfers between devices, swap_depth(): lax.ppermute(value, 'depth', [(i, int(partner(i, k, count)) if count & co...  1.08 us
    pallas_call x2, Pallas kernels, lit_strips(): pl.pallas_call(functools.partial(lit_kernel, slabs, depth_cells, chosen),...  1.07 us
    pallas_call x1, Pallas kernels, composed_frame(): pl.pallas_call(functools.partial(frame_kernel, list(given)), in_specs=[vm...  0.78 us
  transfers between devices with their start and end apart: 11, of which 8 were waited for; matrix products, arithmetic and copies ran while one was open for 0% of the time, Pallas kernels for 15%

profile of v7, /device:TPU:8, one launch (start us, length us, event | category | flops | bytes accessed | tf_op | source)
XLA Modules:
  0.0 26.3 jit_solution(9982248035875223940)
XLA Ops:
  0.0 0.0 copy-start
  0.0 1.3 %slab_code.1 = (bf16[128,128]{1,0:T(8,128)(2,1)S(1)}, f32[16,128,128]{2,1,0:T(8,128)S(1)}) custom-call(f32[16,128,128]{2,1,0:T(8,128)} %density_hbm.1), custom_call_target="tpu_custom_call" | custom-call | tf_op jit(solution)/shard_map/slab_code/pallas_call | solution.py:68
  1.3 2.5 %collective-permute-start = (bf16[128,128]{1,0:T(8,128)(2,1)S(1)}, bf16[128,128]{1,0:T(8,128)(2,1)S(1)}, u32[]{:S(2)}, u32[]{:S(2)}) collective-permute-start(bf16[128,128]{1,0:T(8,128)(2,1)S(1)} %get-tuple-element.25.refs_0_), channel_id=1, source_target_pairs={{0,24},{8,16},{16,8},{24,0},{1,25},{9,17},{17,9},{25,1},{2,26},{10... | collective-permute-start | bytes 98312 | tf_op jit(solution)/shard_map/ppermute | solution.py:215
  3.8 0.5 %collective-permute-start.1 = (bf16[128,128]{1,0:T(8,128)(2,1)S(1)}, bf16[128,128]{1,0:T(8,128)(2,1)S(1)}, u32[]{:S(2)}, u32[]{:S(2)}) collective-permute-start(bf16[128,128]{1,0:T(8,128)(2,1)S(1)} %get-tuple-element.25.refs_0_), channel_id=1, source_target_pairs={{0,16},{8,24},{16,0},{24,8},{1,17},{9,25},{17,1},{25,9},{2,18},{10... | collective-permute-start | bytes 98312 | tf_op jit(solution)/shard_map/ppermute | solution.py:215
  4.3 0.5 %collective-permute-start.2 = (bf16[128,128]{1,0:T(8,128)(2,1)S(1)}, bf16[128,128]{1,0:T(8,128)(2,1)S(1)}, u32[]{:S(2)}, u32[]{:S(2)}) collective-permute-start(bf16[128,128]{1,0:T(8,128)(2,1)S(1)} %get-tuple-element.25.refs_0_), channel_id=1, source_target_pairs={{0,8},{8,0},{16,24},{24,16},{1,9},{9,1},{17,25},{25,17},{2,10},{10... | collective-permute-start | bytes 98312 | tf_op jit(solution)/shard_map/ppermute | solution.py:215
  4.8 0.0 copy-start.1
  4.8 0.0 copy-start.2
  4.8 2.6 %image_sums.1 = (f32[42,128,128]{2,1,0:T(8,128)S(1)}, bf16[2,128,128]{2,1,0:T(8,128)(2,1)S(1)}) custom-call(f32[16,128,128]{2,1,0:T(8,128)S(1)} %get-tuple-element.22.density_ref, bf16[3,16,128,128]{3,2,1,0:T(8,128)(2,1)} %albedo_hbm.1), custom_call_target="tpu_custom_call" | custom-call | flops 15728640 | bytes 5373952 | tf_op jit(solution)/shard_map/image_sums/pallas_call | solution.py:185
  7.5 0.0 collective-permute-done.refs_1_
  7.5 0.2 collective-permute-done.1.refs_2_
  7.7 0.5 %collective-permute-done.2.refs_3_ = bf16[128,128]{1,0:T(8,128)(2,1)S(1)} collective-permute-done((bf16[128,128]{1,0:T(8,128)(2,1)S(1)}, bf16[128,128]{1,0:T(8,128)(2,1)S(1)}, u32[]{:S(2)}, u32[]{:S(2)}) %collective-permute-start.2) | collective-permute-done | bytes 32800 | tf_op jit(solution)/shard_map/ppermute | solution.py:215
  8.2 0.0 copy-done
  8.2 0.7 %lit_strips_123.1 = (bf16[2,4,32,128]{3,2,1,0:T(8,128)(2,1)S(1)}, bf16[2,4,32,128]{3,2,1,0:T(8,128)(2,1)S(1)}, bf16[2,4,32,128]{3,2,1,0:T(8,128)(2,1)S(1)}) custom-call(s32[2,4]{1,0:T(2,128)S(1)} %bitcast.1, s32[2,4]{1,0:T(2,128)S(1)} %bitcast.2, bf16[128,128]{1,0:T(8,128)(2,1)S(1)} %get-tuple-element.25.refs_0_, ...), custom_call_target="tpu_custom_call" | custom-call | tf_op jit(solution)/shard_map/lit_strips_123/pallas_call | solution.py:265
  8.9 0.9 %collective-permute-start.3 = (bf16[2,4,32,128]{3,2,1,0:T(8,128)(2,1)S(1)}, bf16[2,4,32,128]{3,2,1,0:T(8,128)(2,1)S(1)}, u32[]{:S(2)}, u32[]{:S(2)}) collective-permute-start(bf16[2,4,32,128]{3,2,1,0:T(8,128)(2,1)S(1)} %get-tuple-element.27), channel_id=1, source_target_pairs={{0,8},{8,0},{16,24},{24,16},{1,9},{9,1},{17,25},{25,17},{2,10},{10... | collective-permute-start | bytes 196616 | tf_op jit(solution)/shard_map/ppermute | solution.py:215
  9.8 2.2 %collective-permute-start.6 = (bf16[2,4,32,128]{3,2,1,0:T(8,128)(2,1)S(1)}, bf16[2,4,32,128]{3,2,1,0:T(8,128)(2,1)S(1)}, u32[]{:S(2)}, u32[]{:S(2)}) collective-permute-start(bf16[2,4,32,128]{3,2,1,0:T(8,128)(2,1)S(1)} %get-tuple-element.32), channel_id=1, source_target_pairs={{0,24},{8,16},{16,8},{24,0},{1,25},{9,17},{17,9},{25,1},{2,26},{10... | collective-permute-start | bytes 196616 | tf_op jit(solution)/shard_map/ppermute | solution.py:215
  12.0 0.5 %collective-permute-start.7 = (bf16[2,4,32,128]{3,2,1,0:T(8,128)(2,1)S(1)}, bf16[2,4,32,128]{3,2,1,0:T(8,128)(2,1)S(1)}, u32[]{:S(2)}, u32[]{:S(2)}) collective-permute-start(bf16[2,4,32,128]{3,2,1,0:T(8,128)(2,1)S(1)} %get-tuple-element.33), channel_id=1, source_target_pairs={{0,16},{8,24},{16,0},{24,8},{1,17},{9,25},{17,1},{25,9},{2,18},{10... | collective-permute-start | bytes 196616 | tf_op jit(solution)/shard_map/ppermute | solution.py:215
  12.5 0.0 copy-done.1
  12.5 0.0 copy-done.2
  12.5 0.2 piece_plans.1
  12.7 0.4 %lit_strips_0.1.refs_0_ = bf16[2,4,32,128]{3,2,1,0:T(8,128)(2,1)S(1)} custom-call(s32[2,4]{1,0:T(2,128)S(1)} %bitcast.4, s32[2,4]{1,0:T(2,128)S(1)} %bitcast.5, bf16[128,128]{1,0:T(8,128)(2,1)S(1)} %get-tuple-element.25.refs_0_, bf16[128,128]{1,0:T(8,128)(2,1)S(1)} %collective-permute-done.refs_1_, bf16[128,128]{1,0:T(8,128)(2,1)S(1)} %collective-permute-done.1.refs_2_, ...), custom_call_target="tpu_custom_call" | custom-call | tf_op jit(solution)/shard_map/lit_strips_0/pallas_call | solution.py:265
  13.1 0.4 %collective-permute-done.3.refs_1_ = bf16[2,4,32,128]{3,2,1,0:T(8,128)(2,1)S(1)} collective-permute-done((bf16[2,4,32,128]{3,2,1,0:T(8,128)(2,1)S(1)}, bf16[2,4,32,128]{3,2,1,0:T(8,128)(2,1)S(1)}, u32[]{:S(2)}, u32[]{:S(2)}) %collective-permute-start.3) | collective-permute-done | bytes 65568 | tf_op jit(solution)/shard_map/ppermute | solution.py:215
  13.5 0.5 %collective-permute-start.4 = (bf16[2,2,4,32,128]{4,3,2,1,0:T(8,128)(2,1)S(1)}, bf16[2,2,4,32,128]{4,3,2,1,0:T(8,128)(2,1)S(1)}, u32[]{:S(2)}, u32[]{:S(2)}) collective-permute-start(bf16[2,2,4,32,128]{4,3,2,1,0:T(8,128)(2,1)S(1)} %get-tuple-element.30), channel_id=1, source_target_pairs={{0,1},{1,0},{2,3},{3,2},{4,5},{5,4},{6,7},{7,6},{8,9},{9,8},{10,11... | collective-permute-start | bytes 393224 | tf_op jit(solution)/shard_map/ppermute | solution.py:302
  14.0 2.7 %collective-permute-start.5 = (bf16[2,2,4,32,128]{4,3,2,1,0:T(8,128)(2,1)S(1)}, bf16[2,2,4,32,128]{4,3,2,1,0:T(8,128)(2,1)S(1)}, u32[]{:S(2)}, u32[]{:S(2)}) collective-permute-start(bf16[2,2,4,32,128]{4,3,2,1,0:T(8,128)(2,1)S(1)} %get-tuple-element.31), channel_id=1, source_target_pairs={{0,4},{1,2},{2,1},{3,7},{4,0},{5,6},{6,5},{7,3},{8,12},{9,10},{10,... | collective-permute-start | bytes 393224 | tf_op jit(solution)/shard_map/ppermute | solution.py:302
  16.7 0.0 collective-permute-done.6.refs_0_.refs_3_
  16.7 0.0 collective-permute-done.7.refs_1_.refs_2_
  16.8 0.1 collective-permute-start.8
  16.8 2.6 %collective-permute-start.9 = (bf16[2,2,4,32,128]{4,3,2,1,0:T(8,128)(2,1)S(1)}, bf16[2,2,4,32,128]{4,3,2,1,0:T(8,128)(2,1)S(1)}, u32[]{:S(2)}, u32[]{:S(2)}) collective-permute-start(bf16[2,2,4,32,128]{4,3,2,1,0:T(8,128)(2,1)S(1)} %get-tuple-element.35), channel_id=1, source_target_pairs={{0,4},{1,2},{2,1},{3,7},{4,0},{5,6},{6,5},{7,3},{8,12},{9,10},{10,... | collective-permute-start | bytes 393224 | tf_op jit(solution)/shard_map/ppermute | solution.py:302
  19.5 0.1 far_pieces.1
  19.6 0.1 collective-permute-start.10
  19.6 0.1 kept_pieces.1.refs_5_
  19.8 0.1 collective-permute-done.4.piece_ref
  19.9 0.1 ordered_pieces.2.refs_1_
  19.9 0.8 %collective-permute-done.5.piece_ref = bf16[2,2,4,32,128]{4,3,2,1,0:T(8,128)(2,1)S(1)} collective-permute-done((bf16[2,2,4,32,128]{4,3,2,1,0:T(8,128)(2,1)S(1)}, bf16[2,2,4,32,128]{4,3,2,1,0:T(8,128)(2,1)S(1)}, u32[]{:S(2)}, u32[]{:S(2)}) %collective-permute-start.5) | collective-permute-done | bytes 131104 | tf_op jit(solution)/shard_map/ppermute | solution.py:302
  20.8 0.1 ordered_pieces.3.refs_2_
  20.9 0.9 %collective-permute-done.8.refs_3_ = bf16[2,2,4,32,128]{4,3,2,1,0:T(8,128)(2,1)S(1)} collective-permute-done((bf16[2,2,4,32,128]{4,3,2,1,0:T(8,128)(2,1)S(1)}, bf16[2,2,4,32,128]{4,3,2,1,0:T(8,128)(2,1)S(1)}, u32[]{:S(2)}, u32[]{:S(2)}) %collective-permute-start.8) | collective-permute-done | bytes 131104 | tf_op jit(solution)/shard_map/ppermute | solution.py:302
  21.8 2.1 %collective-permute-done.9.refs_4_ = bf16[2,2,4,32,128]{4,3,2,1,0:T(8,128)(2,1)S(1)} collective-permute-done((bf16[2,2,4,32,128]{4,3,2,1,0:T(8,128)(2,1)S(1)}, bf16[2,2,4,32,128]{4,3,2,1,0:T(8,128)(2,1)S(1)}, u32[]{:S(2)}, u32[]{:S(2)}) %collective-permute-start.9) | collective-permute-done | bytes 131104 | tf_op jit(solution)/shard_map/ppermute | solution.py:302
  23.9 0.3 %blend_pieces.1.refs_0_ = f32[2,4,4,32,128]{4,3,2,1,0:T(8,128)S(1)} custom-call(bf16[2,4,4,16,128]{4,3,2,1,0:T(8,128)(2,1)S(1)} %get-tuple-element.24.order_ref.refs_0_, bf16[2,4,4,32,128]{4,3,2,1,0:T(8,128)(2,1)S(1)} %ordered_pieces.2.refs_1_, bf16[2,4,4,32,128]{4,3,2,1,0:T(8,128)(2,1)S(1)} %ordered_pieces.3.refs_2_, ...), custom_call_target="tpu_custom_call" | custom-call | tf_op jit(solution)/shard_map/blend_pieces/pallas_call | solution.py:542
  24.1 1.4 %collective-permute-done.10.refs_2_ = bf16[2,2,4,32,128]{4,3,2,1,0:T(8,128)(2,1)S(1)} collective-permute-done((bf16[2,2,4,32,128]{4,3,2,1,0:T(8,128)(2,1)S(1)}, bf16[2,2,4,32,128]{4,3,2,1,0:T(8,128)(2,1)S(1)}, u32[]{:S(2)}, u32[]{:S(2)}) %collective-permute-start.10) | collective-permute-done | bytes 131104 | tf_op jit(solution)/shard_map/ppermute | solution.py:302
  25.5 0.8 %compose_frame.1 = f32[2,4,1,32,128]{4,3,2,1,0:T(8,128)} custom-call(f32[2,4,4,32,128]{4,3,2,1,0:T(8,128)S(1)} %blend_pieces.1.refs_0_, bf16[2,4,2,16,128]{4,3,2,1,0:T(8,128)(2,1)S(1)} %get-tuple-element.37.refs_1_, bf16[2,2,4,32,128]{4,3,2,1,0:T(8,128)(2,1)S(1)} %collective-permute-done.10.refs_2_), custom_call_target="tpu_custom_call" | custom-call | tf_op jit(solution)/shard_map/compose_frame/pallas_call | solution.py:598
  (2 shorter events, 0.1 us)
Async XLA Ops:
  0.0 8.2 %copy-start = (s32[2,4,1,1]{1,3,2,0:T(1,128)S(1)}, s32[2,4,1,1]{1,3,2,0:T(1,128)}, u32[]{:S(2)}) copy-start(s32[2,4,1,1]{1,3,2,0:T(1,128)} %param.8) | copy-start | bytes 100
  1.3 6.2 %collective-permute-start = (bf16[128,128]{1,0:T(8,128)(2,1)S(1)}, bf16[128,128]{1,0:T(8,128)(2,1)S(1)}, u32[]{:S(2)}, u32[]{:S(2)}) collective-permute-start(bf16[128,128]{1,0:T(8,128)(2,1)S(1)} %get-tuple-element.25.refs_0_), channel_id=1, source_target_pairs={{0,24},{8,16},{16,8},{24,0},{1,25},{9,17},{17,9},{25,1},{2,26},{10... | collective-permute-start | bytes 98312 | tf_op jit(solution)/shard_map/ppermute | solution.py:215
  3.8 3.9 %collective-permute-start.1 = (bf16[128,128]{1,0:T(8,128)(2,1)S(1)}, bf16[128,128]{1,0:T(8,128)(2,1)S(1)}, u32[]{:S(2)}, u32[]{:S(2)}) collective-permute-start(bf16[128,128]{1,0:T(8,128)(2,1)S(1)} %get-tuple-element.25.refs_0_), channel_id=1, source_target_pairs={{0,16},{8,24},{16,0},{24,8},{1,17},{9,25},{17,1},{25,9},{2,18},{10... | collective-permute-start | bytes 98312 | tf_op jit(solution)/shard_map/ppermute | solution.py:215
  4.3 3.9 %collective-permute-start.2 = (bf16[128,128]{1,0:T(8,128)(2,1)S(1)}, bf16[128,128]{1,0:T(8,128)(2,1)S(1)}, u32[]{:S(2)}, u32[]{:S(2)}) collective-permute-start(bf16[128,128]{1,0:T(8,128)(2,1)S(1)} %get-tuple-element.25.refs_0_), channel_id=1, source_target_pairs={{0,8},{8,0},{16,24},{24,16},{1,9},{9,1},{17,25},{25,17},{2,10},{10... | collective-permute-start | bytes 98312 | tf_op jit(solution)/shard_map/ppermute | solution.py:215
  4.8 7.6 %copy-start.1 = (s32[2,4,1,4]{3,2,1,0:T(1,128)S(1)}, s32[2,4,1,4]{3,2,1,0:T(1,128)}, u32[]{:S(2)}) copy-start(s32[2,4,1,4]{3,2,1,0:T(1,128)} %targets_ref.1) | copy-start | bytes 388
  4.8 7.6 %copy-start.2 = (s32[2,4]{1,0:T(2,128)S(1)}, s32[2,4]{1,0:T(2,128)}, u32[]{:S(2)}) copy-start(s32[2,4]{1,0:T(2,128)} %order_ref.1) | copy-start | bytes 100
  8.9 4.5 %collective-permute-start.3 = (bf16[2,4,32,128]{3,2,1,0:T(8,128)(2,1)S(1)}, bf16[2,4,32,128]{3,2,1,0:T(8,128)(2,1)S(1)}, u32[]{:S(2)}, u32[]{:S(2)}) collective-permute-start(bf16[2,4,32,128]{3,2,1,0:T(8,128)(2,1)S(1)} %get-tuple-element.27), channel_id=1, source_target_pairs={{0,8},{8,0},{16,24},{24,16},{1,9},{9,1},{17,25},{25,17},{2,10},{10... | collective-permute-start | bytes 196616 | tf_op jit(solution)/shard_map/ppermute | solution.py:215
  9.8 6.9 %collective-permute-start.6 = (bf16[2,4,32,128]{3,2,1,0:T(8,128)(2,1)S(1)}, bf16[2,4,32,128]{3,2,1,0:T(8,128)(2,1)S(1)}, u32[]{:S(2)}, u32[]{:S(2)}) collective-permute-start(bf16[2,4,32,128]{3,2,1,0:T(8,128)(2,1)S(1)} %get-tuple-element.32), channel_id=1, source_target_pairs={{0,24},{8,16},{16,8},{24,0},{1,25},{9,17},{17,9},{25,1},{2,26},{10... | collective-permute-start | bytes 196616 | tf_op jit(solution)/shard_map/ppermute | solution.py:215
  12.0 4.8 %collective-permute-start.7 = (bf16[2,4,32,128]{3,2,1,0:T(8,128)(2,1)S(1)}, bf16[2,4,32,128]{3,2,1,0:T(8,128)(2,1)S(1)}, u32[]{:S(2)}, u32[]{:S(2)}) collective-permute-start(bf16[2,4,32,128]{3,2,1,0:T(8,128)(2,1)S(1)} %get-tuple-element.33), channel_id=1, source_target_pairs={{0,16},{8,24},{16,0},{24,8},{1,17},{9,25},{17,1},{25,9},{2,18},{10... | collective-permute-start | bytes 196616 | tf_op jit(solution)/shard_map/ppermute | solution.py:215
  13.5 6.4 %collective-permute-start.4 = (bf16[2,2,4,32,128]{4,3,2,1,0:T(8,128)(2,1)S(1)}, bf16[2,2,4,32,128]{4,3,2,1,0:T(8,128)(2,1)S(1)}, u32[]{:S(2)}, u32[]{:S(2)}) collective-permute-start(bf16[2,2,4,32,128]{4,3,2,1,0:T(8,128)(2,1)S(1)} %get-tuple-element.30), channel_id=1, source_target_pairs={{0,1},{1,0},{2,3},{3,2},{4,5},{5,4},{6,7},{7,6},{8,9},{9,8},{10,11... | collective-permute-start | bytes 393224 | tf_op jit(solution)/shard_map/ppermute | solution.py:302
  14.0 6.8 %collective-permute-start.5 = (bf16[2,2,4,32,128]{4,3,2,1,0:T(8,128)(2,1)S(1)}, bf16[2,2,4,32,128]{4,3,2,1,0:T(8,128)(2,1)S(1)}, u32[]{:S(2)}, u32[]{:S(2)}) collective-permute-start(bf16[2,2,4,32,128]{4,3,2,1,0:T(8,128)(2,1)S(1)} %get-tuple-element.31), channel_id=1, source_target_pairs={{0,4},{1,2},{2,1},{3,7},{4,0},{5,6},{6,5},{7,3},{8,12},{9,10},{10,... | collective-permute-start | bytes 393224 | tf_op jit(solution)/shard_map/ppermute | solution.py:302
  16.8 5.0 %collective-permute-start.8 = (bf16[2,2,4,32,128]{4,3,2,1,0:T(8,128)(2,1)S(1)}, bf16[2,2,4,32,128]{4,3,2,1,0:T(8,128)(2,1)S(1)}, u32[]{:S(2)}, u32[]{:S(2)}) collective-permute-start(bf16[2,2,4,32,128]{4,3,2,1,0:T(8,128)(2,1)S(1)} %get-tuple-element.34), channel_id=1, source_target_pairs={{0,1},{1,0},{2,3},{3,2},{4,5},{5,4},{6,7},{7,6},{8,9},{9,8},{10,11... | collective-permute-start | bytes 393224 | tf_op jit(solution)/shard_map/ppermute | solution.py:302
  16.8 7.0 %collective-permute-start.9 = (bf16[2,2,4,32,128]{4,3,2,1,0:T(8,128)(2,1)S(1)}, bf16[2,2,4,32,128]{4,3,2,1,0:T(8,128)(2,1)S(1)}, u32[]{:S(2)}, u32[]{:S(2)}) collective-permute-start(bf16[2,2,4,32,128]{4,3,2,1,0:T(8,128)(2,1)S(1)} %get-tuple-element.35), channel_id=1, source_target_pairs={{0,4},{1,2},{2,1},{3,7},{4,0},{5,6},{6,5},{7,3},{8,12},{9,10},{10,... | collective-permute-start | bytes 393224 | tf_op jit(solution)/shard_map/ppermute | solution.py:302
  19.6 5.9 %collective-permute-start.10 = (bf16[2,2,4,32,128]{4,3,2,1,0:T(8,128)(2,1)S(1)}, bf16[2,2,4,32,128]{4,3,2,1,0:T(8,128)(2,1)S(1)}, u32[]{:S(2)}, u32[]{:S(2)}) collective-permute-start(bf16[2,2,4,32,128]{4,3,2,1,0:T(8,128)(2,1)S(1)} %far_pieces.1), channel_id=1, source_target_pairs={{0,4},{1,3},{2,6},{3,1},{4,0},{5,7},{6,2},{7,5},{8,12},{9,11},{10,... | collective-permute-start | bytes 393224 | tf_op jit(solution)/shard_map/ppermute | solution.py:302
